TPU v7x, 32 devices: a whole 2x2x4 slice. The times are simulated.
32 devices in a mesh: row: 2 (over core), col: 16 (over z, y, x).
Axes of the slice: x: 2, y: 2, z: 4, core: 2. Of those that a mesh axis runs over, the one named last changes fastest.
Arguments:
- tokens: bfloat16 [512, 12288], P('col', 'row'), may hold values from -6 to 6
- up_weight: bfloat16 [12288, 24576], P('row', 'col'), may hold values from -0.109375 to 0.109375
- down_weight: bfloat16 [24576, 12288], P('col', 'row'), may hold values from -0.078125 to 0.078125
- cotangent: bfloat16 [512, 12288], P('col', 'row'), may hold values from -6 to 6
- up_pattern: int32 [96, 192], P('row', 'col'), may hold values 0 or 1
- down_pattern: int32 [192, 96], P('col', 'row'), may hold values 0 or 1
Outputs:
- input_grad: bfloat16 [512, 12288], P('col', 'row')
- up_grad: bfloat16 [12288, 24576], P('row', 'col')
- down_grad: bfloat16 [24576, 12288], P('col', 'row')
All inputs are finite; a program needn't handle non-finite values. No bound on the sum of `up_pattern` or of `down_pattern` on one device may be relied on, other than what follows from the above.
Results may differ from a plain program's by a relative error of at most 0.015.
Values may be sent and summed in bfloat16 or wider, within the bound.
No kernel may reach another device: no remote copies, remote signals or barrier semaphores. Data moves between devices by JAX's collectives and lax.ppermute only.
A program may use at most 192 MiB of HBM per device.

v0:
```python
import jax
import jax.numpy as jnp
from jax import lax
from jax.sharding import PartitionSpec as P

half_root = 0.7071067811865476
inv_root_tau = 0.3989422804014327


def widen(pattern, height, breadth):
    blocks_down, blocks_across = pattern.shape
    spread = pattern.astype(jnp.bfloat16)[:, None, :, None]
    spread = jnp.broadcast_to(
        spread, (blocks_down, height // blocks_down, blocks_across, breadth // blocks_across)
    )
    return spread.reshape(height, breadth)


def activate(pre, dact):
    cdf = 0.5 * (1.0 + jax.scipy.special.erf(pre * half_root))
    dens = jnp.exp(-0.5 * pre * pre) * inv_root_tau
    active = (pre * cdf).astype(jnp.bfloat16)
    dhid = (dact * (cdf + pre * dens)).astype(jnp.bfloat16)
    return (active, dhid)


def on_device(tokens, up_weight, down_weight, cotangent, up_pattern, down_pattern):
    full_tokens, full_cotangent = (
        lax.all_gather(tokens, "col", axis=0, tiled=True),
        lax.all_gather(cotangent, "col", axis=0, tiled=True),
    )
    up_mask = widen(up_pattern, up_weight.shape[0], up_weight.shape[1])
    down_mask = widen(down_pattern, down_weight.shape[0], down_weight.shape[1])
    up_eff = up_weight * up_mask
    down_eff = down_weight * down_mask
    pre_part = jnp.dot(full_tokens, up_eff, preferred_element_type=jnp.float32)
    dact_part = lax.dot_general(
        full_cotangent, down_eff, (((1,), (1,)), ((), ())), preferred_element_type=jnp.float32
    )
    pre, dact = (
        lax.psum_scatter(pre_part, "row", scatter_dimension=0, tiled=True),
        lax.psum_scatter(dact_part, "row", scatter_dimension=0, tiled=True),
    )
    active_share, dhid_share = activate(pre, dact)
    active, dhid = (
        lax.all_gather(active_share, "row", axis=0, tiled=True),
        lax.all_gather(dhid_share, "row", axis=0, tiled=True),
    )
    input_grad = lax.psum_scatter(
        lax.dot_general(
            dhid, up_eff, (((1,), (1,)), ((), ())), preferred_element_type=jnp.float32
        ).astype(jnp.bfloat16),
        "col",
        scatter_dimension=0,
        tiled=True,
    )
    factor = 1.0 / jnp.sqrt(jnp.float32(full_tokens.shape[0]))
    up_grad = lax.dot_general(
        full_tokens, dhid, (((0,), (0,)), ((), ())), preferred_element_type=jnp.float32
    )
    up_grad = (up_grad * up_mask.astype(jnp.float32) * factor).astype(jnp.bfloat16)
    down_grad = lax.dot_general(
        active, full_cotangent, (((0,), (0,)), ((), ())), preferred_element_type=jnp.float32
    )
    down_grad = (down_grad * down_mask.astype(jnp.float32) * factor).astype(jnp.bfloat16)
    return (input_grad, up_grad, down_grad)


def solution(mesh):
    return jax.shard_map(
        on_device,
        mesh=mesh,
        in_specs=(
            P("col", "row"),
            P("row", "col"),
            P("col", "row"),
            P("col", "row"),
            P("row", "col"),
            P("col", "row"),
        ),
        out_specs=(P("col", "row"), P("row", "col"), P("col", "row")),
        check_vma=False,
    )
```

profile of v0, /device:TPU:0, one launch (start us, length us, event | category | flops | bytes accessed | tf_op | source)
XLA Modules:
  0.0 429.3 jit_solution(5608237277476569969)
XLA Ops:
  7.2 0.0 all-gather.7.cloned.1.call-start
  7.2 0.7 all-gather.7.cloned.1.call-update
  7.9 0.0 all-gather.5.cloned.1.call-start
  7.9 0.7 all-gather.5.cloned.1.call-update
  8.6 0.0 copy-start
  8.7 0.0 reduce-scatter.6.cloned.1.call-start
  8.7 24.6 %copy.9 = bf16[6144,1536]{0,1:T(8,128)(2,1)} copy(bf16[6144,1536]{1,0:T(8,128)(2,1)} %param.7) | data formatting | bytes 37748736 | tf_op args[1]
  33.3 0.0 copy-done
  33.4 74.3 %all-gather.7.cloned.1.call-done = bf16[512,6144]{1,0:T(8,128)(2,1)} async-done(((bf16[32,6144]{1,0:T(8,128)(2,1)}), bf16[512,6144]{1,0:T(8,128)(2,1)}) %all-gather.7.cloned.1.call-update) | async-done | bytes 6291472 | tf_op jit(solution)/shard_map/all_gather | solution.py:29
  107.6 6.8 %broadcast_in_dim.5 = bf16[48,128,12,128]{1,0,3,2:T(8,128)(2,1)} broadcast(bf16[48,12]{0,1:T(8,128)(2,1)S(1)} %convert_element_type.28), dimensions={0,2} | broadcast | bytes 18875520 | tf_op jit(solution)/shard_map/broadcast_in_dim | solution.py:13
  114.5 0.0 copy-start.1
  114.5 20.1 %fusion.5 = f32[512,1536]{0,1:T(8,128)} fusion(bf16[512,6144]{1,0:T(8,128)(2,1)} %all-gather.7.cloned.1.call-done, bf16[6144,1536]{0,1:T(8,128)(2,1)} %copy.9, bf16[192,8,48,128]{3,2,1,0:T(8,128)(2,1)} %bitcast.36), kind=kOutput, calls=%fused_computation.10 | convolution fusion | flops 9673113600 | bytes 47185920 | tf_op jit(solution)/shard_map/dot_general | solution.py:36
  134.6 0.0 reduce-scatter.6.cloned.1.call-update
  134.6 0.0 reduce-scatter.4.cloned.1.call-start
  134.7 0.0 copy-done.1
  134.7 68.2 %all-gather.5.cloned.1.call-done = bf16[512,6144]{1,0:T(8,128)(2,1)} async-done(((bf16[32,6144]{1,0:T(8,128)(2,1)}), bf16[512,6144]{1,0:T(8,128)(2,1)}) %all-gather.5.cloned.1.call-update) | async-done | bytes 6291472 | tf_op jit(solution)/shard_map/all_gather | solution.py:30
  202.9 6.9 %broadcast_in_dim.4 = bf16[12,128,48,128]{3,2,1,0:T(8,128)(2,1)} broadcast(bf16[12,48]{1,0:T(8,128)(2,1)S(1)} %convert_element_type.27), dimensions={0,2} | broadcast | bytes 18875520 | tf_op jit(solution)/shard_map/broadcast_in_dim | solution.py:13
  209.8 20.5 %fusion.6 = f32[512,1536]{0,1:T(8,128)} fusion(bf16[512,6144]{1,0:T(8,128)(2,1)} %all-gather.5.cloned.1.call-done, bf16[1536,6144]{1,0:T(8,128)(2,1)} %param.8, bf16[192,8,48,128]{3,2,1,0:T(8,128)(2,1)} %bitcast.39), kind=kOutput, calls=%fused_computation.11 | convolution fusion | flops 9673113600 | bytes 47185920 | tf_op jit(solution)/shard_map/dot_general | solution.py:37
  230.3 0.0 reduce-scatter.4.cloned.1.call-update
  230.3 0.0 all-gather.9.cloned.1.call-start
  230.4 0.0 reduce-scatter.6.cloned.1.call-done
  230.4 10.0 %reduce-scatter.4.cloned.1.call-done = f32[256,1536]{0,1:T(8,128)} async-done(((f32[512,1536]{0,1:T(8,128)}), f32[256,1536]{0,1:T(8,128)}) %reduce-scatter.4.cloned.1.call-update) | async-done | bytes 1572880 | tf_op jit(solution)/shard_map/reduce_scatter | solution.py:42
  240.4 3.7 multiply_convert_fusion.1
  244.1 0.0 all-gather.9.cloned.1.call-update
  244.1 0.0 all-gather.11.cloned.1.call-start
  244.2 0.5 all-gather.11.cloned.1.call-update
  244.7 0.2 reduce-scatter.8.cloned.1.call-start
  244.9 10.1 %all-gather.9.cloned.1.call-done = bf16[512,1536]{0,1:T(8,128)(2,1)} async-done(((bf16[256,1536]{0,1:T(8,128)(2,1)}), bf16[512,1536]{0,1:T(8,128)(2,1)}) %all-gather.9.cloned.1.call-update) | async-done | bytes 1572880 | tf_op jit(solution)/shard_map/all_gather | solution.py:47
  255.1 20.3 %convolution_convert_fusion = bf16[512,6144]{1,0:T(8,128)(2,1)} fusion(bf16[512,1536]{0,1:T(8,128)(2,1)} %all-gather.9.cloned.1.call-done, bf16[6144,1536]{0,1:T(8,128)(2,1)} %copy.9, bf16[192,8,48,128]{3,2,1,0:T(8,128)(2,1)} %bitcast.37), kind=kOutput, calls=%fused_computation.8 | convolution fusion | flops 9676259328 | bytes 45613056 | tf_op jit(solution)/shard_map/dot_general | solution.py:50
  275.3 0.0 copy-start.2
  275.3 0.0 reduce-scatter.8.cloned.1.call-update
  275.4 1.4 copy-done.2
  276.8 20.6 %fusion.1 = bf16[6144,1536]{0,1:T(8,128)(2,1)} fusion(bf16[512,1536]{0,1:T(8,128)(2,1)S(1)} %copy-done.2, bf16[512,6144]{1,0:T(8,128)(2,1)} %all-gather.7.cloned.1.call-done, bf16[192,8,48,128]{3,2,1,0:T(8,128)(2,1)} %bitcast.38), kind=kOutput, calls=%fused_computation.2 | convolution fusion | flops 9701425152 | bytes 45613056 | tf_op jit(solution)/shard_map/dot_general | solution.py:58
  297.4 24.7 %copy.10 = bf16[6144,1536]{1,0:T(8,128)(2,1)} copy(bf16[6144,1536]{0,1:T(8,128)(2,1)} %fusion.1) | data formatting | bytes 37748736
  322.1 0.0 all-gather.11.cloned.1.call-done
  322.1 22.6 %multiply_convert_fusion = bf16[1536,6144]{1,0:T(8,128)(2,1)} fusion(bf16[512,1536]{0,1:T(8,128)(2,1)} %all-gather.11.cloned.1.call-done, bf16[512,6144]{1,0:T(8,128)(2,1)} %all-gather.5.cloned.1.call-done, bf16[192,8,48,128]{3,2,1,0:T(8,128)(2,1)} %bitcast.40), kind=kOutput, calls=%fused_computation.3 | convolution fusion | flops 9701425152 | bytes 45613056 | tf_op jit(solution)/shard_map/dot_general | solution.py:62
  344.7 77.7 %reduce-scatter.8.cloned.1.call-done = bf16[32,6144]{1,0:T(8,128)(2,1)} async-done(((bf16[512,6144]{1,0:T(8,128)(2,1)}), bf16[32,6144]{1,0:T(8,128)(2,1)}) %reduce-scatter.8.cloned.1.call-update) | async-done | bytes 393232 | tf_op jit(solution)/shard_map/reduce_scatter | solution.py:49
  (2 shorter events, 0.0 us)
Async XLA Ops:
  7.2 100.5 %all-gather.7.cloned.1.call-start = ((), (), s32[]{:S(2)}) async-start(), calls=%async_computation.5 | async-start | bytes 6684672 | tf_op jit(solution)/shard_map/all_gather | solution.py:29
  7.9 195.0 %all-gather.5.cloned.1.call-start = ((), (), s32[]{:S(2)}) async-start(), calls=%async_computation.3 | async-start | bytes 6684672 | tf_op jit(solution)/shard_map/all_gather | solution.py:30
  8.6 24.7 %copy-start = (s32[48,12]{0,1:T(8,128)S(1)}, s32[48,12]{0,1:T(8,128)}, u32[]{:S(2)}) copy-start(s32[48,12]{0,1:T(8,128)} %param.10) | copy-start | bytes 6916
  8.7 221.7 %reduce-scatter.6.cloned.1.call-start = ((), (), s32[]{:S(2)}) async-start(), calls=%async_computation.6 | async-start | bytes 4718592 | tf_op jit(solution)/shard_map/reduce_scatter | solution.py:41
  114.5 20.2 %copy-start.1 = (s32[12,48]{1,0:T(8,128)S(1)}, s32[12,48]{1,0:T(8,128)}, u32[]{:S(2)}) copy-start(s32[12,48]{1,0:T(8,128)} %param.11) | copy-start | bytes 6916
  134.6 105.7 %reduce-scatter.4.cloned.1.call-start = ((), (), s32[]{:S(2)}) async-start(), calls=%async_computation.4 | async-start | bytes 4718592 | tf_op jit(solution)/shard_map/reduce_scatter | solution.py:42
  230.3 24.8 %all-gather.9.cloned.1.call-start = ((), (), s32[]{:S(2)}) async-start(), calls=%async_computation.7 | async-start | bytes 2359296 | tf_op jit(solution)/shard_map/all_gather | solution.py:47
  244.1 78.0 %all-gather.11.cloned.1.call-start = ((), (), s32[]{:S(2)}) async-start(), calls=%async_computation.9 | async-start | bytes 2359296 | tf_op jit(solution)/shard_map/all_gather | solution.py:46
  244.7 177.7 %reduce-scatter.8.cloned.1.call-start = ((), (), s32[]{:S(2)}) async-start(), calls=%async_computation.8 | async-start | bytes 6684672 | tf_op jit(solution)/shard_map/reduce_scatter | solution.py:49
  275.3 1.4 copy-start.2
Sparse Core Ops, SparseCore 0:
  10.8 96.8 all-gather.6
  110.4 92.3 all-gather.4
  205.1 9.1 reduce-scatter.5
  230.4 9.8 reduce-scatter.3
  244.3 10.7 all-gather.8
  256.5 10.8 all-gather.10
  275.5 146.8 reduce-scatter.7
where the time goes:
time: 431 us; the launch traced here: 429 us
  waiting for transfers between devices  242 us (56%)
  matrix products  104 us (24%)
  local copies, waits for them, and re-layouts  64.5 us (15%)
  between operations  14.2 us (3%)
    reduce_scatter x1, waiting for transfers between devices, on_device(): lax.psum_scatter(lax.dot_general(dhid, up_eff, (((1,), (1,)), ((), ())),...  77.7 us
    all_gather x1, waiting for transfers between devices, on_device(): lax.all_gather(tokens, 'col', axis=0, tiled=True)  74.3 us
    all_gather x1, waiting for transfers between devices, on_device(): lax.all_gather(cotangent, 'col', axis=0, tiled=True)  68.2 us
    unnamed x8, local copies, waits for them, and re-layouts  50.7 us
    dot_general x1, matrix products, on_device(): lax.dot_general(active, full_cotangent, (((0,), (0,)), ((), ())), preferr...  22.6 us
    dot_general x1, matrix products, on_device(): lax.dot_general(full_tokens, dhid, (((0,), (0,)), ((), ())), preferred_el...  20.6 us
    dot_general x1, matrix products, on_device(): lax.dot_general(full_cotangent, down_eff, (((1,), (1,)), ((), ())), prefe...  20.5 us
    dot_general x1, matrix products, on_device(): lax.dot_general(dhid, up_eff, (((1,), (1,)), ((), ())), preferred_element...  20.3 us
  transfers between devices with their start and end apart: 7, of which 5 were waited for; matrix products, arithmetic and copies ran while one was open for 39% of the time, Pallas kernels for 0%

commit v1 on v0

v1 whole, which is shorter than its diff:
```python
import functools

import jax
import jax.numpy as jnp
from jax import lax
from jax.experimental import pallas as pl
from jax.experimental.pallas import tpu as pltpu
from jax.sharding import PartitionSpec as P

half_root = 0.7071067811865476
inv_root_tau = 0.3989422804014327
GROUPS = 2
SPLIT = (18, 20)
OUT_OF = 48


def activate(pre, dact):
    cdf = 0.5 * (1.0 + jax.scipy.special.erf(pre * half_root))
    dens = jnp.exp(-0.5 * pre * pre) * inv_root_tau
    active = (pre * cdf).astype(jnp.bfloat16)
    dhid = (dact * (cdf + pre * dens)).astype(jnp.bfloat16)
    return (active, dhid)


def divisor(count, most):
    return max(k for k in range(1, most + 1) if count % k == 0)


def kept(flag, block):
    return jnp.where(flag != 0, block, jnp.zeros_like(block))


def runs(order, height, half):
    found = []
    for m in range(1 << len(order)):
        common = sum(((m >> k) & 1) << bit for k, bit in enumerate(order)) * height
        side, row = divmod(m * height, half)
        last = found[-1] if found else None
        if last and last[0] == side and last[2] + last[3] == common:
            last[3] += height
        else:
            found.append([side, row, common, height])
    return found


def forward_kernel(moves, block, up_on, down_on, *refs):
    arrays = 1 + max(move[0] for move in moves)
    held = refs[:arrays]
    up_hbm, down_hbm = refs[arrays : arrays + 2]
    full_hbm, *sum_hbm = refs[-11:-8]
    full, sums, up_buf, down_buf = refs[-8:-4]
    in_sems, out_sems, weight_sems, full_sem = refs[-4:]
    rows, width = full.shape[1:]
    columns, down = sums.shape[2] // block, width // block
    slots, each = up_buf.shape[0], up_buf.shape[2] // block
    turns = columns // each

    def here(turn):
        return pl.ds(pl.multiple_of(turn * each * block, each * block), each * block)

    def fetch(turn):
        slot = lax.rem(turn, slots)
        return (
            pltpu.make_async_copy(up_hbm.at[:, here(turn)], up_buf.at[slot], weight_sems.at[0, slot]),
            pltpu.make_async_copy(down_hbm.at[here(turn), :], down_buf.at[slot], weight_sems.at[1, slot]),
        )

    copies = [
        pltpu.make_async_copy(
            held[array].at[:, pl.ds(source, tall), :],
            full.at[:, pl.ds(target, tall), pl.ds(lane, breadth)],
            in_sems.at[at],
        )
        for at, (array, source, target, tall, lane, breadth) in enumerate(moves)
    ]
    for copy in copies:
        copy.start()
    for turn in range(min(slots, turns)):
        for copy in fetch(turn):
            copy.start()
    for copy in copies:
        copy.wait()
    whole = pltpu.make_async_copy(full, full_hbm, full_sem)
    whole.start()

    def leave(turn):
        return [
            pltpu.make_async_copy(
                sums.at[w, :, here(turn)], sum_hbm[w].at[:, here(turn)], out_sems.at[w, turn]
            )
            for w in range(2)
        ]

    def step(turn, carry):
        lanes = here(turn)
        slot = lax.rem(turn, slots)
        for copy in fetch(turn):
            copy.wait()
        right = jnp.concatenate(
            [
                jnp.concatenate(
                    [
                        kept(
                            up_on[i, turn * each + c],
                            up_buf[slot, i * block : (i + 1) * block, c * block : (c + 1) * block],
                        )
                        for c in range(each)
                    ],
                    1,
                )
                for i in range(down)
            ],
            0,
        )
        pre = jnp.dot(full[0], right, preferred_element_type=jnp.float32)
        sums[0, :, lanes] = pre.astype(jnp.bfloat16)
        right = jnp.concatenate(
            [
                jnp.concatenate(
                    [
                        kept(
                            down_on[turn * each + c, i],
                            down_buf[
                                slot, c * block : (c + 1) * block, i * block : (i + 1) * block
                            ],
                        )
                        for i in range(down)
                    ],
                    1,
                )
                for c in range(each)
            ],
            0,
        )
        dact = lax.dot_general(
            full[1], right, (((1,), (1,)), ((), ())), preferred_element_type=jnp.float32
        )
        sums[1, :, lanes] = dact.astype(jnp.bfloat16)

        @pl.when(turn + slots < turns)
        def _():
            for copy in fetch(turn + slots):
                copy.start()

        for copy in leave(turn):
            copy.start()
        return carry

    lax.fori_loop(0, turns, step, 0)
    for turn in range(turns):
        for copy in leave(turn):
            copy.wait()
    whole.wait()


def forward(held, orders, height, up_weight, down_weight, up_on, down_on, after):
    width, hidden = up_weight.shape
    block = width // up_on.shape[0]
    rows = 2 * held[0][0].shape[1]
    moves, arrays, lane = [], [], 0
    for (low, high), order in zip(held, orders):
        for side, source, target, tall in runs(order, height, rows // 2):
            moves.append((len(arrays) + side, source, target, tall, lane, low.shape[2]))
        arrays += [low, high]
        lane += low.shape[2]
    any_space = pl.BlockSpec(memory_space=pl.ANY)
    smem = pl.BlockSpec(memory_space=pltpu.SMEM)
    each = divisor(hidden // block, 2)
    slots = 3
    shapes = [
        ((2, rows, width), jnp.bfloat16),
        ((2, rows, hidden), jnp.bfloat16),
    ]
    return pl.pallas_call(
        functools.partial(forward_kernel, moves, block),
        in_specs=[smem] * 2 + [any_space] * (len(arrays) + 2 + len(after)),
        out_specs=[any_space] * 3,
        scratch_shapes=[pltpu.VMEM(*shape) for shape in shapes]
        + [
            pltpu.VMEM((slots, width, each * block), jnp.bfloat16),
            pltpu.VMEM((slots, each * block, width), jnp.bfloat16),
            pltpu.SemaphoreType.DMA((len(moves),)),
            pltpu.SemaphoreType.DMA((2, hidden // block // each)),
            pltpu.SemaphoreType.DMA((2, slots)),
            pltpu.SemaphoreType.DMA,
        ],
        out_shape=[jax.ShapeDtypeStruct(*shape) for shape in shapes[:1]]
        + [jax.ShapeDtypeStruct((rows, hidden), jnp.bfloat16)] * 2,
        compiler_params=pltpu.CompilerParams(vmem_limit_bytes=48 * 1024 * 1024),
        cost_estimate=pl.CostEstimate(
            flops=rows * width, bytes_accessed=rows * width, transcendentals=0
        ),
        name="forward",
    )(up_on, down_on, *arrays, up_weight, down_weight, *after)


def backward_kernel(parts, block, up_on, dhid_ref, up_hbm, *refs):
    outs, (buf, sems) = refs[-2 - 2 * len(parts) : -2], refs[-2:]
    across = up_hbm.shape[1] // block
    tiles, at = [], 0
    for part, (moves, count) in enumerate(parts):
        each = divisor(count, 6)
        tiles += [(part, moves, at + r, r, each) for r in range(0, count, each)]
        at += count
    copies = []
    for k, (part, moves, row, lane, each) in enumerate(tiles):
        rows = pl.ds(row * block, each * block)
        copies.append(pltpu.make_async_copy(up_hbm.at[rows, :], buf.at[rows, :], sems.at[k]))
    for copy in copies:
        copy.start()
    for copy, (part, moves, row, lane, each) in zip(copies, tiles):
        copy.wait()
        right = jnp.concatenate(
            [
                jnp.concatenate(
                    [
                        kept(
                            up_on[row + r, c],
                            buf[(row + r) * block : (row + r + 1) * block, c * block : (c + 1) * block],
                        )
                        for c in range(across)
                    ],
                    1,
                )
                for r in range(each)
            ],
            0,
        )
        acc = lax.dot_general(
            dhid_ref[...], right, (((1,), (1,)), ((), ())), preferred_element_type=jnp.float32
        ).astype(jnp.bfloat16)
        for side, target, source, tall in moves:
            outs[2 * part + side][
                target : target + tall, lane * block : (lane + each) * block
            ] = acc[source : source + tall]


def backward(dhid, up_weight, up_on, orders, height, bounds, after):
    width, hidden = up_weight.shape
    block = width // up_on.shape[0]
    rows = dhid.shape[0]
    parts = [
        (runs(order, height, rows // 2), (stop - start) // block)
        for order, (start, stop) in zip(orders, bounds)
    ]
    tiles = sum(count // divisor(count, 6) for moves, count in parts)
    vmem = pl.BlockSpec(memory_space=pltpu.VMEM)
    smem = pl.BlockSpec(memory_space=pltpu.SMEM)
    any_space = pl.BlockSpec(memory_space=pl.ANY)
    outs = pl.pallas_call(
        functools.partial(backward_kernel, parts, block),
        in_specs=[smem, vmem] + [any_space] * (1 + len(after)),
        out_specs=[vmem] * (2 * len(parts)),
        scratch_shapes=[pltpu.VMEM((width, hidden), jnp.bfloat16), pltpu.SemaphoreType.DMA((tiles,))],
        out_shape=[
            jax.ShapeDtypeStruct((rows // 2, count * block), jnp.bfloat16)
            for moves, count in parts
            for side in range(2)
        ],
        compiler_params=pltpu.CompilerParams(vmem_limit_bytes=48 * 1024 * 1024),
        cost_estimate=pl.CostEstimate(
            flops=rows * width, bytes_accessed=rows * width, transcendentals=0
        ),
        name="backward",
    )(up_on, dhid, up_weight, *after)
    return [(outs[2 * part], outs[2 * part + 1]) for part in range(len(parts))]


def grad_kernel(block, factor, first, groups, pattern, *refs):
    lefts, rights, out_ref = refs[:groups], refs[groups : 2 * groups], refs[-1]
    down, across = out_ref.shape[0] // block, out_ref.shape[1] // block
    row = first[0] + pl.program_id(0) * down
    column = first[1] + pl.program_id(1) * across
    chunk = 2 if across % 2 == 0 else 1
    left = jnp.concatenate([ref[...] for ref in lefts], axis=0)
    for c in range(0, across, chunk):
        lanes = slice(c * block, (c + chunk) * block)
        acc = lax.dot_general(
            left,
            jnp.concatenate([ref[:, lanes] for ref in rights], axis=0),
            (((0,), (0,)), ((), ())),
            preferred_element_type=jnp.float32,
        )
        for r in range(down):
            for q in range(chunk):
                scale = jnp.where(pattern[row + r, column + c + q] != 0, factor, 0.0)
                out_ref[r * block : (r + 1) * block, (c + q) * block : (c + q + 1) * block] = (
                    acc[r * block : (r + 1) * block, q * block : (q + 1) * block] * scale
                ).astype(jnp.bfloat16)


def grad(lefts, rights, pattern, block, most, left_which, right_which, shares, by_column):
    groups = len(lefts)
    tall, broad = lefts[0].shape[-1], rights[0].shape[-1]
    tile = (
        divisor(tall // block // (1 if by_column else shares), most[0]) * block,
        divisor(broad // block // (shares if by_column else 1), most[1]) * block,
    )
    rows = lefts[0].shape[-2]
    tokens = groups * rows
    factor = float(1.0 / tokens**0.5)
    steps = [tall // tile[0], broad // tile[1]]
    steps[int(by_column)] //= shares

    def spec(which, breadth, index):
        if which is None:
            return pl.BlockSpec((rows, breadth), lambda i, c, *_: (0, index(i, c)))
        return pl.BlockSpec((None, rows, breadth), lambda i, c, *_: (which, 0, index(i, c)))

    def make(share):
        off = (0, share * steps[1]) if by_column else (share * steps[0], 0)

        def call(out, after):
            in_specs = [spec(left_which, tile[0], lambda i, c: off[0] + i)] * groups
            in_specs += [spec(right_which, tile[1], lambda i, c: off[1] + c)] * groups
            args = [*lefts, *rights, *after]
            in_specs += [pl.BlockSpec(memory_space=pl.ANY)] * len(after)
            aliases = {}
            if out is not None:
                in_specs.append(pl.BlockSpec(memory_space=pl.ANY))
                args.append(out)
                aliases = {len(args): 0}
            return pl.pallas_call(
                functools.partial(
                    grad_kernel,
                    block,
                    factor,
                    (off[0] * tile[0] // block, off[1] * tile[1] // block),
                    groups,
                ),
                grid_spec=pltpu.PrefetchScalarGridSpec(
                    num_scalar_prefetch=1,
                    grid=tuple(steps),
                    in_specs=in_specs,
                    out_specs=pl.BlockSpec(tile, lambda i, c, *_: (off[0] + i, off[1] + c)),
                ),
                out_shape=jax.ShapeDtypeStruct((tall, broad), jnp.bfloat16),
                input_output_aliases=aliases,
                compiler_params=pltpu.CompilerParams(vmem_limit_bytes=32 * 1024 * 1024),
                cost_estimate=pl.CostEstimate(
                    flops=2 * tokens * tall * broad // shares,
                    bytes_accessed=2 * tall * broad // shares,
                    transcendentals=0,
                ),
                name="grad",
            )(pattern, *args)

        return call

    return [make(share) for share in range(shares)]


def add(left, right):
    return (left.astype(jnp.float32) + right.astype(jnp.float32)).astype(jnp.bfloat16)


def halves(value):
    half = value.shape[0] // 2
    return (value[:half], value[half:])


def on_device(sizes, tokens, up_weight, down_weight, cotangent, up_pattern, down_pattern):
    n, across = sizes["col"], sizes["row"]
    bits = n.bit_length() - 1
    far = list(range(bits - 1, 1, -1))
    outer, near = far[:-1], far[-1:]
    orders = [[*outer, 1, *near, 0], [*outer, *near, 0, 1], [*outer, 0, 1, *near]]
    width, hidden = up_weight.shape
    down = up_pattern.shape[0]
    block = width // down
    height = tokens.shape[0] // GROUPS
    bounds = [0, SPLIT[0] * down // OUT_OF, sum(SPLIT) * down // OUT_OF, down]
    bounds = [(at * block, to * block) for at, to in zip(bounds, bounds[1:])]

    def swap(value, bit):
        return lax.ppermute(value, "col", [(i, i ^ (1 << bit)) for i in range(n)])

    def later(value, *marks):
        return lax.optimization_barrier((value, *marks))[0]

    def beside(sums, marks):
        for bit in range(across.bit_length() - 1):
            pairs = [(i, i ^ (1 << bit)) for i in range(across)]
            others = [later(lax.ppermute(part.astype(jnp.bfloat16), "row", pairs), *marks) for part in sums]
            sums = [
                part.astype(jnp.float32) + other.astype(jnp.float32) for part, other in zip(sums, others)
            ]
        return sums

    helds = []
    for g in range(GROUPS):
        rows = slice(g * height, (g + 1) * height)
        own = jnp.stack([tokens[rows], cotangent[rows]])
        if g > 0:
            own = later(own, *ahead)
        for bit in outer:
            own = jnp.concatenate([own, swap(own, bit)], axis=1)
        if g > 0:
            own = later(own, *helds[-1])
        held, ahead = [], []
        for part, (start, stop) in enumerate(bounds):
            low = own[:, :, start:stop]
            rest = orders[part][len(outer) :]
            for bit in rest[:-1]:
                low = jnp.concatenate([low, swap(low, bit)], axis=1)
                if bit == rest[0]:
                    ahead.append(low)
            held.append(low)
        helds.append(held)
    for g, held in enumerate(helds):
        marks = helds[g + 1] if g + 1 < GROUPS else []
        helds[g] = [(low, swap(later(low, *marks), order[-1])) for low, order in zip(held, orders)]

    def stage(held, at, mark, marked):
        summed = []
        for part, (low, high) in enumerate(held):
            other = swap(high, orders[part][-1 - at])
            summed.append(add(low, other if mark is None or part >= marked else later(other, mark)))
        return summed

    def finish(summed, mark):
        total = jnp.concatenate(summed, axis=1)
        for bit in reversed(outer):
            low, high = halves(total)
            other = swap(high, bit)
            total = add(low, other if mark is None else later(other, mark))
        return total

    stages = len(orders[0]) - len(outer)
    last = GROUPS - 1
    fulls, actives, dhids, totals = [], [], [], []
    for g in range(GROUPS):
        after = [low for low, high in helds[g + 1]] if g + 1 < GROUPS else []
        after = after + ([half for pair in totals[-1] for half in pair] if g > 0 else [])
        full, *sums = forward(
            helds[g], orders, height, up_weight, down_weight, up_pattern, down_pattern, after
        )
        marks = [high for low, high in helds[g + 1][:2]] if g + 1 < GROUPS else []
        active, dhid = activate(*beside(sums, marks))
        fulls.append(full)
        actives.append(active)
        dhids.append(dhid)
        early, after = totals, []
        if g == last:
            for at, mark in zip(range(stages - 1), (sums[1], dhid)):
                early = [stage(held, at, mark, len(orders)) for held in early]
                after = [total for summed in early for total in summed]
                early = [[halves(total) for total in summed] for summed in early]
        totals.append(
            backward(dhid, up_weight, up_pattern, orders, height, bounds, after)
        )

    grads = [
        grad(fulls, dhids, up_pattern, block, (8, 12), 0, None, 2, False),
        grad(actives, fulls, down_pattern, block, (12, 8), None, 1, 2, True),
    ]
    work = [(which, call) for pair in zip(*grads) for which, call in enumerate(pair)]
    outs = [None, None]

    def advance(count, after):
        for which, call in work[:count]:
            outs[which] = call(outs[which], after)
        del work[:count]

    held = totals[last]
    late = [stage(pairs, stages - 1, held[0][0], len(orders)) for pairs in early]
    advance(2, [half for pair in held for half in pair] + [total for summed in late for total in summed])
    shares = [finish(summed, outs[1]) for summed in late]
    for at in range(stages):
        summed = stage(held, at, outs[1 - at] if at < 2 else None, 2)
        if at == 0:
            advance(1, summed)
        if at < stages - 1:
            summed = lax.optimization_barrier(summed)
        held = [halves(total) for total in summed]
    advance(len(work), summed)
    shares.append(finish(summed, None))
    input_grad = jnp.concatenate(shares, axis=0)
    return (input_grad, outs[0], outs[1])


def solution(mesh):
    return jax.shard_map(
        functools.partial(on_device, dict(mesh.shape)),
        mesh=mesh,
        in_specs=(
            P("col", "row"),
            P("row", "col"),
            P("col", "row"),
            P("col", "row"),
            P("row", "col"),
            P("col", "row"),
        ),
        out_specs=(P("col", "row"), P("row", "col"), P("col", "row")),
        check_vma=False,
    )
```

time: 431 us -> 270 us (0.63)
  waiting for transfers between devices: 242 us -> 108 us
  matrix products: 104 us -> 0 us
  Pallas kernels: 0 us -> 96.5 us
  local copies, waits for them, and re-layouts: 64.5 us -> 4.47 us
  starting transfers between devices: 0.46 us -> 50.9 us
  between operations: 14.2 us -> 1.12 us
  other arithmetic: 3.74 us -> 8.37 us
    all_gather x4 -> x0, waiting for transfers between devices: 153 us -> none  [the longest x1 74.3 us: on_device(): lax.all_gather(tokens, 'col', axis=0, tiled=True)]
    ppermute x0 -> x44, waiting for transfers between devices: none -> 108 us  [the longest x40 107 us: swap(): return lax.ppermute(value, 'col', [(i, i ^ 1 << bit) for i in range(n)])]
    dot_general x5 -> x0, matrix products: 104 us -> none  [the longest x1 22.6 us: on_device(): lax.dot_general(active, full_cotangent, (((0,), (0,)), ((), ())), preferr...]
    pallas_call x0 -> x8, Pallas kernels: none -> 96.5 us  [the longest x2 39.3 us: forward(): pl.pallas_call(functools.partial(forward_kernel, moves, block), in_specs=...]
    reduce_scatter x3 -> x0, waiting for transfers between devices: 87.7 us -> none  [the longest x1 77.7 us: on_device(): lax.psum_scatter(lax.dot_general(dhid, up_eff, (((1,), (1,)), ((), ())),...]
    ppermute x0 -> x44, starting transfers between devices: none -> 50.9 us  [the longest x40 49.7 us: swap(): return lax.ppermute(value, 'col', [(i, i ^ 1 << bit) for i in range(n)])]
    unnamed x8 -> x11, local copies, waits for them, and re-layouts: 50.7 us -> 2.89 us
    broadcast_in_dim x2 -> x0, local copies, waits for them, and re-layouts: 13.7 us -> none  [widen(): jnp.broadcast_to(spread, (blocks_down, height // blocks_down, blocks_acro...]
  transfers between devices with their start and end apart: 7 -> 44, of which waited for: 5 -> 23; matrix products, arithmetic and copies ran while one was open for 39% -> 2% of each run, Pallas kernels for 0% -> 36%
where the time goes in v1:
time: 270 us
  waiting for transfers between devices  108 us (40%)
  Pallas kernels  96.5 us (36%)
  starting transfers between devices  50.9 us (19%)
  other arithmetic  8.37 us (3%)
  local copies, waits for them, and re-layouts  4.47 us (2%)
    ppermute x40, waiting for transfers between devices, swap(): return lax.ppermute(value, 'col', [(i, i ^ 1 << bit) for i in range(n)])  107 us
    ppermute x40, starting transfers between devices, swap(): return lax.ppermute(value, 'col', [(i, i ^ 1 << bit) for i in range(n)])  49.7 us
    pallas_call x2, Pallas kernels, forward(): pl.pallas_call(functools.partial(forward_kernel, moves, block), in_specs=...  39.3 us
    pallas_call x4, Pallas kernels, call(): pl.pallas_call(functools.partial(grad_kernel, block, factor, (off[0] * ti...  33.3 us
    pallas_call x2, Pallas kernels, backward(): pl.pallas_call(functools.partial(backward_kernel, parts, block), in_specs...  23.9 us
  transfers between devices with their start and end apart: 44, of which 23 were waited for; matrix products, arithmetic and copies ran while one was open for 2% of the time, Pallas kernels for 36%

profile of v1, /device:TPU:0, one launch (start us, length us, event | category | flops | bytes accessed | tf_op | source)
XLA Modules:
  0.0 269.7 jit_solution(6145139397458604646)
XLA Ops:
  2.0 4.1 %collective-permute-start = (bf16[2,16,6144]{2,1,0:T(8,128)(2,1)S(1)}, bf16[2,16,6144]{2,1,0:T(8,128)(2,1)S(1)}, u32[]{:S(2)}, u32[]{:S(2)}) collective-permute-start(bf16[2,16,6144]{2,1,0:T(8,128)(2,1)S(1)} %pad_maximum_fusion.12), channel_id=1, source_target_pairs={{0,8},{1,9},{2,10},{3,11},{4,12},{5,13},{6,14},{7,15},{8,0},{9,1},... | collective-permute-start | bytes 1179656 | tf_op jit(solution)/shard_map/ppermute | solution.py:376
  6.1 17.5 %collective-permute-done = bf16[2,16,6144]{2,1,0:T(8,128)(2,1)S(1)} collective-permute-done((bf16[2,16,6144]{2,1,0:T(8,128)(2,1)S(1)}, bf16[2,16,6144]{2,1,0:T(8,128)(2,1)S(1)}, u32[]{:S(2)}, u32[]{:S(2)}) %collective-permute-start) | collective-permute-done | bytes 393248 | tf_op jit(solution)/shard_map/ppermute | solution.py:376
  23.7 1.6 collective-permute-start.1
  25.3 1.6 collective-permute-start.4
  27.7 3.0 %collective-permute-done.4 = bf16[2,32,1280]{2,1,0:T(8,128)(2,1)S(1)} collective-permute-done((bf16[2,32,1280]{2,1,0:T(8,128)(2,1)S(1)}, bf16[2,32,1280]{2,1,0:T(8,128)(2,1)S(1)}, u32[]{:S(2)}, u32[]{:S(2)}) %collective-permute-start.4) | collective-permute-done | bytes 163872 | tf_op jit(solution)/shard_map/ppermute | solution.py:376
  31.3 1.3 collective-permute-done.1
  32.6 2.5 collective-permute-done.3
  35.1 3.4 %collective-permute-start.5 = (bf16[2,16,6144]{2,1,0:T(8,128)(2,1)S(1)}, bf16[2,16,6144]{2,1,0:T(8,128)(2,1)S(1)}, u32[]{:S(2)}, u32[]{:S(2)}) collective-permute-start(bf16[2,16,6144]{2,1,0:T(8,128)(2,1)S(1)} %pad_maximum_fusion.13), channel_id=1, source_target_pairs={{0,8},{1,9},{2,10},{3,11},{4,12},{5,13},{6,14},{7,15},{8,0},{9,1},... | collective-permute-start | bytes 1179656 | tf_op jit(solution)/shard_map/ppermute | solution.py:376
  38.5 1.7 collective-permute-start.2
  40.9 14.3 %collective-permute-done.5 = bf16[2,16,6144]{2,1,0:T(8,128)(2,1)S(1)} collective-permute-done((bf16[2,16,6144]{2,1,0:T(8,128)(2,1)S(1)}, bf16[2,16,6144]{2,1,0:T(8,128)(2,1)S(1)}, u32[]{:S(2)}, u32[]{:S(2)}) %collective-permute-start.5) | collective-permute-done | bytes 393248 | tf_op jit(solution)/shard_map/ppermute | solution.py:376
  55.2 4.5 %collective-permute-done.2 = bf16[2,64,2304]{2,1,0:T(8,128)(2,1)S(1)} collective-permute-done((bf16[2,64,2304]{2,1,0:T(8,128)(2,1)S(1)}, bf16[2,64,2304]{2,1,0:T(8,128)(2,1)S(1)}, u32[]{:S(2)}, u32[]{:S(2)}) %collective-permute-start.2) | collective-permute-done | bytes 589856 | tf_op jit(solution)/shard_map/ppermute | solution.py:376
  62.3 1.4 collective-permute-start.10
  63.6 2.8 %collective-permute-done.12 = bf16[2,32,1280]{2,1,0:T(8,128)(2,1)S(1)} collective-permute-done((bf16[2,32,1280]{2,1,0:T(8,128)(2,1)S(1)}, bf16[2,32,1280]{2,1,0:T(8,128)(2,1)S(1)}, u32[]{:S(2)}, u32[]{:S(2)}) %collective-permute-start.12) | collective-permute-done | bytes 163872 | tf_op jit(solution)/shard_map/ppermute | solution.py:376
  67.0 4.3 %collective-permute-done.8 = bf16[2,32,2304]{2,1,0:T(8,128)(2,1)S(1)} collective-permute-done((bf16[2,32,2304]{2,1,0:T(8,128)(2,1)S(1)}, bf16[2,32,2304]{2,1,0:T(8,128)(2,1)S(1)}, u32[]{:S(2)}, u32[]{:S(2)}) %collective-permute-start.8) | collective-permute-done | bytes 294944 | tf_op jit(solution)/shard_map/ppermute | solution.py:376
  72.5 2.2 collective-permute-start.11
  75.5 6.5 %collective-permute-done.9 = bf16[2,64,2304]{2,1,0:T(8,128)(2,1)S(1)} collective-permute-done((bf16[2,64,2304]{2,1,0:T(8,128)(2,1)S(1)}, bf16[2,64,2304]{2,1,0:T(8,128)(2,1)S(1)}, u32[]{:S(2)}, u32[]{:S(2)}) %collective-permute-start.9) | collective-permute-done | bytes 589856 | tf_op jit(solution)/shard_map/ppermute | solution.py:376
  84.4 1.5 collective-permute-start.15
  85.9 1.7 collective-permute-start.14
  89.8 8.9 %collective-permute-done.16.refs_5_ = bf16[2,128,1280]{2,1,0:T(8,128)(2,1)S(1)} collective-permute-done((bf16[2,128,1280]{2,1,0:T(8,128)(2,1)S(1)}, bf16[2,128,1280]{2,1,0:T(8,128)(2,1)S(1)}, u32[]{:S(2)}, u32[]{:S(2)}) %collective-permute-start.16) | collective-permute-done | bytes 655392 | tf_op jit(solution)/shard_map/ppermute | solution.py:376
  98.8 16.2 %collective-permute-done.14.refs_1_ = bf16[2,128,2304]{2,1,0:T(8,128)(2,1)} collective-permute-done((bf16[2,128,2304]{2,1,0:T(8,128)(2,1)S(1)}, bf16[2,128,2304]{2,1,0:T(8,128)(2,1)}, u32[]{:S(2)}, u32[]{:S(2)}) %collective-permute-start.14) | collective-permute-done | bytes 1179680 | tf_op jit(solution)/shard_map/ppermute | solution.py:376
  114.9 1.5 collective-permute-done.15.refs_3_
  116.5 19.7 %forward.2 = (bf16[2,256,6144]{2,1,0:T(8,128)(2,1)}, bf16[256,1536]{1,0:T(8,128)(2,1)S(1)}, bf16[256,1536]{1,0:T(8,128)(2,1)S(1)}) custom-call(s32[48,12]{1,0:T(8,128)S(1)} %copy.12.up_on.pattern, s32[12,48]{1,0:T(8,128)S(1)} %copy-done.1, bf16[2,128,2304]{2,1,0:T(8,128)(2,1)S(1)} %pad_maximum_fusion.2.refs_0_, ...), custom_call_target="tpu_custom_call" | custom-call | flops 1572864 | bytes 1572864 | tf_op jit(solution)/shard_map/forward/pallas_call | solution.py:174
  140.7 11.7 %backward.2 = (bf16[128,2304]{1,0:T(8,128)(2,1)S(1)}, bf16[128,2304]{1,0:T(8,128)(2,1)S(1)}, bf16[128,2560]{1,0:T(8,128)(2,1)S(1)}, bf16[128,2560]{1,0:T(8,128)(...) custom-call(s32[48,12]{1,0:T(8,128)S(1)} %copy.12.up_on.pattern, ...), custom_call_target="tpu_custom_call" | custom-call | flops 1572864 | bytes 1572864 | tf_op jit(solution)/shard_map/backward/pallas_call | solution.py:250
  152.4 1.3 collective-permute-start.29
  153.8 1.5 collective-permute-start.21
  155.2 1.6 collective-permute-start.27
  156.8 19.5 %forward.3 = (bf16[2,256,6144]{2,1,0:T(8,128)(2,1)}, bf16[256,1536]{1,0:T(8,128)(2,1)S(1)}, bf16[256,1536]{1,0:T(8,128)(2,1)S(1)}) custom-call(s32[48,12]{1,0:T(8,128)S(1)} %copy.12.up_on.pattern, s32[12,48]{1,0:T(8,128)S(1)} %copy-done.1, bf16[2,128,2304]{2,1,0:T(8,128)(2,1)} %pad_maximum_fusion.3.refs_8_.refs_0_, ...), custom_call_target="tpu_custom_call" | custom-call | flops 1572864 | bytes 1572864 | tf_op jit(solution)/shard_map/forward/pallas_call | solution.py:174
  177.7 1.6 collective-permute-start.23
  180.9 2.4 collective-permute-done.30
  183.9 2.6 collective-permute-done.23
  186.6 1.6 collective-permute-start.26
  188.3 1.4 collective-permute-done.28
  189.8 12.2 %backward.3 = (bf16[128,2304]{1,0:T(8,128)(2,1)S(1)}, bf16[128,2304]{1,0:T(8,128)(2,1)S(1)}, bf16[128,2560]{1,0:T(8,128)(2,1)S(1)}, bf16[128,2560]{1,0:T(8,128)(...) custom-call(s32[48,12]{1,0:T(8,128)S(1)} %copy.12.up_on.pattern, ...), custom_call_target="tpu_custom_call" | custom-call | flops 1572864 | bytes 1572864 | tf_op jit(solution)/shard_map/backward/pallas_call | solution.py:250
  203.1 1.6 collective-permute-start.35
  205.4 6.1 %collective-permute-done.31 = bf16[32,2560]{1,0:T(8,128)(2,1)S(1)} collective-permute-done((bf16[32,2560]{1,0:T(8,128)(2,1)S(1)}, bf16[32,2560]{1,0:T(8,128)(2,1)S(1)}, u32[]{:S(2)}, u32[]{:S(2)}) %collective-permute-start.31) | collective-permute-done | bytes 163872 | tf_op jit(solution)/shard_map/ppermute | solution.py:376
  211.8 2.8 %copy-done = bf16[2,256,6144]{2,1,0:T(8,128)(2,1)S(1)} copy-done((bf16[2,256,6144]{2,1,0:T(8,128)(2,1)S(1)}, bf16[2,256,6144]{2,1,0:T(8,128)(2,1)}, u32[]{:S(2)}) %copy-start) | copy-done | bytes 6291480
  214.5 8.7 %grad.5.refs_7_ = bf16[6144,1536]{1,0:T(8,128)(2,1)} custom-call(s32[48,12]{1,0:T(8,128)S(1)} %copy.12.up_on.pattern, bf16[2,256,6144]{2,1,0:T(8,128)(2,1)S(1)} %bitcast.9, bf16[2,256,6144]{2,1,0:T(8,128)(2,1)S(1)} %copy-done, bf16[256,1536]{1,0:T(8,128)(2,1)S(1)} %get-tuple-element.96.dhid_ref.refs_2_, ...), custom_call_target="tpu_custom_call" | custom-call | flops 4831838208 | bytes 9437184 | tf_op jit(solution)/shard_map/grad/pallas_call | solution.py:323
  223.2 8.1 %grad.4.refs_7_ = bf16[1536,6144]{1,0:T(8,128)(2,1)} custom-call(s32[12,48]{1,0:T(8,128)S(1)} %copy-done.1, bf16[256,1536]{1,0:T(8,128)(2,1)S(1)} %get-tuple-element.95.refs_0_, bf16[256,1536]{1,0:T(8,128)(2,1)S(1)} %get-tuple-element.93.refs_1_, bf16[2,256,6144]{2,1,0:T(8,128)(2,1)S(1)} %bitcast.9, bf16[2,256,6144]{2,1,0:T(8,128)(2,1)S(1)} %copy-done, ...), custom_call_target="tpu_custom_call" | custom-call | flops 4831838208 | bytes 9437184 | tf_op jit(solution)/shard_map/grad/pallas_call | solution.py:323
  231.8 2.3 collective-permute-start.37
  234.1 1.5 collective-permute-start.39
  235.6 8.4 %grad.6 = bf16[6144,1536]{1,0:T(8,128)(2,1)} custom-call(s32[48,12]{1,0:T(8,128)S(1)} %copy.12.up_on.pattern, bf16[2,256,6144]{2,1,0:T(8,128)(2,1)S(1)} %bitcast.9, bf16[2,256,6144]{2,1,0:T(8,128)(2,1)S(1)} %copy-done, bf16[256,1536]{1,0:T(8,128)(2,1)S(1)} %get-tuple-element.96.dhid_ref.refs_2_, ...), custom_call_target="tpu_custom_call", output_to_operand_aliasing={{}: (8, {})} | custom-call | flops 4831838208 | bytes 9437184 | tf_op jit(solution)/shard_map/grad/pallas_call | solution.py:323
  244.0 1.7 collective-permute-start.38
  245.8 5.3 %collective-permute-done.38 = bf16[64,2560]{1,0:T(8,128)(2,1)S(1)} collective-permute-done((bf16[64,2560]{1,0:T(8,128)(2,1)S(1)}, bf16[64,2560]{1,0:T(8,128)(2,1)S(1)}, u32[]{:S(2)}, u32[]{:S(2)}) %collective-permute-start.38) | collective-permute-done | bytes 327712 | tf_op jit(solution)/shard_map/ppermute | solution.py:376
  251.3 1.7 collective-permute-start.42
  253.9 1.8 collective-permute-done.42
  255.8 2.5 collective-permute-done.40
  258.5 2.2 collective-permute-start.43
  260.7 8.1 %grad.7 = bf16[1536,6144]{1,0:T(8,128)(2,1)} custom-call(s32[12,48]{1,0:T(8,128)S(1)} %copy-done.1, bf16[256,1536]{1,0:T(8,128)(2,1)S(1)} %get-tuple-element.95.refs_0_, bf16[256,1536]{1,0:T(8,128)(2,1)S(1)} %get-tuple-element.93.refs_1_, bf16[2,256,6144]{2,1,0:T(8,128)(2,1)S(1)} %bitcast.9, ...), custom_call_target="tpu_custom_call", output_to_operand_aliasing={{}: (8, {})} | custom-call | flops 4831838208 | bytes 9437184 | tf_op jit(solution)/shard_map/grad/pallas_call | solution.py:323
  (122 shorter events, 25.9 us)
Async XLA Ops:
  2.0 21.6 %collective-permute-start = (bf16[2,16,6144]{2,1,0:T(8,128)(2,1)S(1)}, bf16[2,16,6144]{2,1,0:T(8,128)(2,1)S(1)}, u32[]{:S(2)}, u32[]{:S(2)}) collective-permute-start(bf16[2,16,6144]{2,1,0:T(8,128)(2,1)S(1)} %pad_maximum_fusion.12), channel_id=1, source_target_pairs={{0,8},{1,9},{2,10},{3,11},{4,12},{5,13},{6,14},{7,15},{8,0},{9,1},... | collective-permute-start | bytes 1179656 | tf_op jit(solution)/shard_map/ppermute | solution.py:376
  23.7 8.9 %collective-permute-start.1 = (bf16[2,32,2304]{2,1,0:T(8,128)(2,1)S(1)}, bf16[2,32,2304]{2,1,0:T(8,128)(2,1)S(1)}, u32[]{:S(2)}, u32[]{:S(2)}) collective-permute-start(bf16[2,32,2304]{2,1,0:T(8,128)(2,1)S(1)} %slice.152), channel_id=1, source_target_pairs={{0,2},{1,3},{2,0},{3,1},{4,6},{5,7},{6,4},{7,5},{8,10},{9,11},{10,... | collective-permute-start | bytes 884744 | tf_op jit(solution)/shard_map/ppermute | solution.py:376
  25.3 5.4 %collective-permute-start.4 = (bf16[2,32,1280]{2,1,0:T(8,128)(2,1)S(1)}, bf16[2,32,1280]{2,1,0:T(8,128)(2,1)S(1)}, u32[]{:S(2)}, u32[]{:S(2)}) collective-permute-start(bf16[2,32,1280]{2,1,0:T(8,128)(2,1)S(1)} %pad_maximum_fusion.19), channel_id=1, source_target_pairs={{0,1},{1,0},{2,3},{3,2},{4,5},{5,4},{6,7},{7,6},{8,9},{9,8},{10,11... | collective-permute-start | bytes 491528 | tf_op jit(solution)/shard_map/ppermute | solution.py:376
  27.0 8.1 %collective-permute-start.3 = (bf16[2,32,2560]{2,1,0:T(8,128)(2,1)S(1)}, bf16[2,32,2560]{2,1,0:T(8,128)(2,1)S(1)}, u32[]{:S(2)}, u32[]{:S(2)}) collective-permute-start(bf16[2,32,2560]{2,1,0:T(8,128)(2,1)S(1)} %slice.153), channel_id=1, source_target_pairs={{0,4},{1,5},{2,6},{3,7},{4,0},{5,1},{6,2},{7,3},{8,12},{9,13},{10,... | collective-permute-start | bytes 983048 | tf_op jit(solution)/shard_map/ppermute | solution.py:376
  30.7 10.1 %collective-permute-start.7 = (bf16[2,64,1280]{2,1,0:T(8,128)(2,1)S(1)}, bf16[2,64,1280]{2,1,0:T(8,128)(2,1)S(1)}, u32[]{:S(2)}, u32[]{:S(2)}) collective-permute-start(bf16[2,64,1280]{2,1,0:T(8,128)(2,1)S(1)} %pad_maximum_fusion.17), channel_id=1, source_target_pairs={{0,2},{1,3},{2,0},{3,1},{4,6},{5,7},{6,4},{7,5},{8,10},{9,11},{10,... | collective-permute-start | bytes 983048 | tf_op jit(solution)/shard_map/ppermute | solution.py:376
  35.1 20.1 %collective-permute-start.5 = (bf16[2,16,6144]{2,1,0:T(8,128)(2,1)S(1)}, bf16[2,16,6144]{2,1,0:T(8,128)(2,1)S(1)}, u32[]{:S(2)}, u32[]{:S(2)}) collective-permute-start(bf16[2,16,6144]{2,1,0:T(8,128)(2,1)S(1)} %pad_maximum_fusion.13), channel_id=1, source_target_pairs={{0,8},{1,9},{2,10},{3,11},{4,12},{5,13},{6,14},{7,15},{8,0},{9,1},... | collective-permute-start | bytes 1179656 | tf_op jit(solution)/shard_map/ppermute | solution.py:376
  38.5 21.3 %collective-permute-start.2 = (bf16[2,64,2304]{2,1,0:T(8,128)(2,1)S(1)}, bf16[2,64,2304]{2,1,0:T(8,128)(2,1)S(1)}, u32[]{:S(2)}, u32[]{:S(2)}) collective-permute-start(bf16[2,64,2304]{2,1,0:T(8,128)(2,1)S(1)} %pad_maximum_fusion.10), channel_id=1, source_target_pairs={{0,4},{1,5},{2,6},{3,7},{4,0},{5,1},{6,2},{7,3},{8,12},{9,13},{10,... | collective-permute-start | bytes 1769480 | tf_op jit(solution)/shard_map/ppermute | solution.py:376
  40.3 19.6 %collective-permute-start.6 = (bf16[2,64,2560]{2,1,0:T(8,128)(2,1)S(1)}, bf16[2,64,2560]{2,1,0:T(8,128)(2,1)S(1)}, u32[]{:S(2)}, u32[]{:S(2)}) collective-permute-start(bf16[2,64,2560]{2,1,0:T(8,128)(2,1)S(1)} %pad_maximum_fusion.6), channel_id=1, source_target_pairs={{0,1},{1,0},{2,3},{3,2},{4,5},{5,4},{6,7},{7,6},{8,9},{9,8},{10,11... | collective-permute-start | bytes 1966088 | tf_op jit(solution)/shard_map/ppermute | solution.py:376
  61.0 5.4 %collective-permute-start.12 = (bf16[2,32,1280]{2,1,0:T(8,128)(2,1)S(1)}, bf16[2,32,1280]{2,1,0:T(8,128)(2,1)S(1)}, u32[]{:S(2)}, u32[]{:S(2)}) collective-permute-start(bf16[2,32,1280]{2,1,0:T(8,128)(2,1)S(1)} %slice.123), channel_id=1, source_target_pairs={{0,1},{1,0},{2,3},{3,2},{4,5},{5,4},{6,7},{7,6},{8,9},{9,8},{10,11... | collective-permute-start | bytes 491528 | tf_op jit(solution)/shard_map/ppermute | solution.py:376
  61.7 9.6 %collective-permute-start.8 = (bf16[2,32,2304]{2,1,0:T(8,128)(2,1)S(1)}, bf16[2,32,2304]{2,1,0:T(8,128)(2,1)S(1)}, u32[]{:S(2)}, u32[]{:S(2)}) collective-permute-start(bf16[2,32,2304]{2,1,0:T(8,128)(2,1)S(1)} %slice.121), channel_id=1, source_target_pairs={{0,2},{1,3},{2,0},{3,1},{4,6},{5,7},{6,4},{7,5},{8,10},{9,11},{10,... | collective-permute-start | bytes 884744 | tf_op jit(solution)/shard_map/ppermute | solution.py:376
  62.3 10.2 %collective-permute-start.10 = (bf16[2,32,2560]{2,1,0:T(8,128)(2,1)S(1)}, bf16[2,32,2560]{2,1,0:T(8,128)(2,1)S(1)}, u32[]{:S(2)}, u32[]{:S(2)}) collective-permute-start(bf16[2,32,2560]{2,1,0:T(8,128)(2,1)S(1)} %slice.122), channel_id=1, source_target_pairs={{0,4},{1,5},{2,6},{3,7},{4,0},{5,1},{6,2},{7,3},{8,12},{9,13},{10,... | collective-permute-start | bytes 983048 | tf_op jit(solution)/shard_map/ppermute | solution.py:376
  66.5 9.0 %collective-permute-start.13 = (bf16[2,64,1280]{2,1,0:T(8,128)(2,1)S(1)}, bf16[2,64,1280]{2,1,0:T(8,128)(2,1)S(1)}, u32[]{:S(2)}, u32[]{:S(2)}) collective-permute-start(bf16[2,64,1280]{2,1,0:T(8,128)(2,1)S(1)} %pad_maximum_fusion.18), channel_id=1, source_target_pairs={{0,2},{1,3},{2,0},{3,1},{4,6},{5,7},{6,4},{7,5},{8,10},{9,11},{10,... | collective-permute-start | bytes 983048 | tf_op jit(solution)/shard_map/ppermute | solution.py:376
  71.3 10.7 %collective-permute-start.9 = (bf16[2,64,2304]{2,1,0:T(8,128)(2,1)S(1)}, bf16[2,64,2304]{2,1,0:T(8,128)(2,1)S(1)}, u32[]{:S(2)}, u32[]{:S(2)}) collective-permute-start(bf16[2,64,2304]{2,1,0:T(8,128)(2,1)S(1)} %pad_maximum_fusion.11), channel_id=1, source_target_pairs={{0,4},{1,5},{2,6},{3,7},{4,0},{5,1},{6,2},{7,3},{8,12},{9,13},{10,... | collective-permute-start | bytes 1769480 | tf_op jit(solution)/shard_map/ppermute | solution.py:376
  72.5 10.8 %collective-permute-start.11 = (bf16[2,64,2560]{2,1,0:T(8,128)(2,1)S(1)}, bf16[2,64,2560]{2,1,0:T(8,128)(2,1)S(1)}, u32[]{:S(2)}, u32[]{:S(2)}) collective-permute-start(bf16[2,64,2560]{2,1,0:T(8,128)(2,1)S(1)} %pad_maximum_fusion.8), channel_id=1, source_target_pairs={{0,1},{1,0},{2,3},{3,2},{4,5},{5,4},{6,7},{7,6},{8,9},{9,8},{10,11... | collective-permute-start | bytes 1966088 | tf_op jit(solution)/shard_map/ppermute | solution.py:376
  83.2 6.5 %copy-start.2 = (s32[48,12]{0,1:T(8,128)S(1)}, s32[48,12]{0,1:T(8,128)}, u32[]{:S(2)}) copy-start(s32[48,12]{0,1:T(8,128)} %param.10) | copy-start | bytes 6916
  83.2 33.3 %copy-start.1 = (s32[12,48]{1,0:T(8,128)S(1)}, s32[12,48]{1,0:T(8,128)}, u32[]{:S(2)}) copy-start(s32[12,48]{1,0:T(8,128)} %pattern.5) | copy-start | bytes 6916
  84.4 32.0 %collective-permute-start.15 = (bf16[2,128,2560]{2,1,0:T(8,128)(2,1)}, bf16[2,128,2560]{2,1,0:T(8,128)(2,1)}, u32[]{:S(2)}, u32[]{:S(2)}) collective-permute-start(bf16[2,128,2560]{2,1,0:T(8,128)(2,1)} %pad_maximum_fusion.refs_2_), channel_id=1, source_target_pairs={{0,2},{1,3},{2,0},{3,1},{4,6},{5,7},{6,4},{7,5},{8,10},{9,11},{10,... | collective-permute-start | bytes 3932168 | tf_op jit(solution)/shard_map/ppermute | solution.py:376
  85.9 29.0 %collective-permute-start.14 = (bf16[2,128,2304]{2,1,0:T(8,128)(2,1)S(1)}, bf16[2,128,2304]{2,1,0:T(8,128)(2,1)}, u32[]{:S(2)}, u32[]{:S(2)}) collective-permute-start(bf16[2,128,2304]{2,1,0:T(8,128)(2,1)S(1)} %pad_maximum_fusion.2.refs_0_), channel_id=1, source_target_pairs={{0,1},{1,0},{2,3},{3,2},{4,5},{5,4},{6,7},{7,6},{8,9},{9,8},{10,11... | collective-permute-start | bytes 3538952 | tf_op jit(solution)/shard_map/ppermute | solution.py:376
  87.6 11.1 %collective-permute-start.16 = (bf16[2,128,1280]{2,1,0:T(8,128)(2,1)S(1)}, bf16[2,128,1280]{2,1,0:T(8,128)(2,1)S(1)}, u32[]{:S(2)}, u32[]{:S(2)}) collective-permute-start(bf16[2,128,1280]{2,1,0:T(8,128)(2,1)S(1)} %pad_maximum_fusion.7.refs_4_), channel_id=1, source_target_pairs={{0,4},{1,5},{2,6},{3,7},{4,0},{5,1},{6,2},{7,3},{8,12},{9,13},{10,... | collective-permute-start | bytes 1966088 | tf_op jit(solution)/shard_map/ppermute | solution.py:376
  88.7 50.0 %collective-permute-start.19 = (bf16[2,128,2560]{2,1,0:T(8,128)(2,1)}, bf16[2,128,2560]{2,1,0:T(8,128)(2,1)}, u32[]{:S(2)}, u32[]{:S(2)}) collective-permute-start(bf16[2,128,2560]{2,1,0:T(8,128)(2,1)} %pad_maximum_fusion.1.refs_9_.refs_2_), channel_id=1, source_target_pairs={{0,2},{1,3},{2,0},{3,1},{4,6},{5,7},{6,4},{7,5},{8,10},{9,11},{10,... | collective-permute-start | bytes 3932168 | tf_op jit(solution)/shard_map/ppermute | solution.py:376
  89.2 48.8 %collective-permute-start.18 = (bf16[2,128,2304]{2,1,0:T(8,128)(2,1)}, bf16[2,128,2304]{2,1,0:T(8,128)(2,1)}, u32[]{:S(2)}, u32[]{:S(2)}) collective-permute-start(bf16[2,128,2304]{2,1,0:T(8,128)(2,1)} %pad_maximum_fusion.3.refs_8_.refs_0_), channel_id=1, source_target_pairs={{0,1},{1,0},{2,3},{3,2},{4,5},{5,4},{6,7},{7,6},{8,9},{9,8},{10,11... | collective-permute-start | bytes 3538952 | tf_op jit(solution)/shard_map/ppermute | solution.py:376
  136.2 2.5 collective-permute-start.20
  136.3 3.4 %collective-permute-start.17 = (bf16[256,1536]{1,0:T(8,128)(2,1)S(1)}, bf16[256,1536]{1,0:T(8,128)(2,1)S(1)}, u32[]{:S(2)}, u32[]{:S(2)}) collective-permute-start(bf16[256,1536]{1,0:T(8,128)(2,1)S(1)} %get-tuple-element.53), channel_id=1, source_target_pairs={{0,16},{16,0},{1,17},{17,1},{2,18},{18,2},{3,19},{19,3},{4,20},{20... | collective-permute-start | bytes 2359304 | tf_op jit(solution)/shard_map/ppermute | solution.py:384
  136.8 20.0 %collective-permute-start.22 = (bf16[2,128,1280]{2,1,0:T(8,128)(2,1)S(1)}, bf16[2,128,1280]{2,1,0:T(8,128)(2,1)S(1)}, u32[]{:S(2)}, u32[]{:S(2)}) collective-permute-start(bf16[2,128,1280]{2,1,0:T(8,128)(2,1)S(1)} %pad_maximum_fusion.9.refs_10_.refs_4_), channel_id=1, source_target_pairs={{0,4},{1,5},{2,6},{3,7},{4,0},{5,1},{6,2},{7,3},{8,12},{9,13},{10,... | collective-permute-start | bytes 1966088 | tf_op jit(solution)/shard_map/ppermute | solution.py:376
  152.4 24.5 %collective-permute-start.29 = (bf16[128,1280]{1,0:T(8,128)(2,1)S(1)}, bf16[128,1280]{1,0:T(8,128)(2,1)S(1)}, u32[]{:S(2)}, u32[]{:S(2)}) collective-permute-start(bf16[128,1280]{1,0:T(8,128)(2,1)S(1)} %get-tuple-element.62.refs_13_), channel_id=1, source_target_pairs={{0,4},{1,5},{2,6},{3,7},{4,0},{5,1},{6,2},{7,3},{8,12},{9,13},{10,... | collective-permute-start | bytes 983048 | tf_op jit(solution)/shard_map/ppermute | solution.py:376
  153.8 23.8 %collective-permute-start.21 = (bf16[128,2304]{1,0:T(8,128)(2,1)S(1)}, bf16[128,2304]{1,0:T(8,128)(2,1)S(1)}, u32[]{:S(2)}, u32[]{:S(2)}) collective-permute-start(bf16[128,2304]{1,0:T(8,128)(2,1)S(1)} %get-tuple-element.58.refs_9_), channel_id=1, source_target_pairs={{0,1},{1,0},{2,3},{3,2},{4,5},{5,4},{6,7},{7,6},{8,9},{9,8},{10,11... | collective-permute-start | bytes 1769480 | tf_op jit(solution)/shard_map/ppermute | solution.py:376
  155.2 24.1 %collective-permute-start.27 = (bf16[128,2560]{1,0:T(8,128)(2,1)S(1)}, bf16[128,2560]{1,0:T(8,128)(2,1)S(1)}, u32[]{:S(2)}, u32[]{:S(2)}) collective-permute-start(bf16[128,2560]{1,0:T(8,128)(2,1)S(1)} %get-tuple-element.60.refs_11_), channel_id=1, source_target_pairs={{0,2},{1,3},{2,0},{3,1},{4,6},{5,7},{6,4},{7,5},{8,10},{9,11},{10,... | collective-permute-start | bytes 1966088 | tf_op jit(solution)/shard_map/ppermute | solution.py:376
  176.4 3.2 %collective-permute-start.25 = (bf16[256,1536]{1,0:T(8,128)(2,1)S(1)}, bf16[256,1536]{1,0:T(8,128)(2,1)S(1)}, u32[]{:S(2)}, u32[]{:S(2)}) collective-permute-start(bf16[256,1536]{1,0:T(8,128)(2,1)S(1)} %get-tuple-element.65), channel_id=1, source_target_pairs={{0,16},{16,0},{1,17},{17,1},{2,18},{18,2},{3,19},{19,3},{4,20},{20... | collective-permute-start | bytes 2359304 | tf_op jit(solution)/shard_map/ppermute | solution.py:384
  176.5 3.4 %collective-permute-start.24 = (bf16[256,1536]{1,0:T(8,128)(2,1)S(1)}, bf16[256,1536]{1,0:T(8,128)(2,1)S(1)}, u32[]{:S(2)}, u32[]{:S(2)}) collective-permute-start(bf16[256,1536]{1,0:T(8,128)(2,1)S(1)} %get-tuple-element.63), channel_id=1, source_target_pairs={{0,16},{16,0},{1,17},{17,1},{2,18},{18,2},{3,19},{19,3},{4,20},{20... | collective-permute-start | bytes 2359304 | tf_op jit(solution)/shard_map/ppermute | solution.py:384
  177.1 6.2 %collective-permute-start.30 = (bf16[64,1280]{1,0:T(8,128)(2,1)S(1)}, bf16[64,1280]{1,0:T(8,128)(2,1)S(1)}, u32[]{:S(2)}, u32[]{:S(2)}) collective-permute-start(bf16[64,1280]{1,0:T(8,128)(2,1)S(1)} %slice.161), channel_id=1, source_target_pairs={{0,2},{1,3},{2,0},{3,1},{4,6},{5,7},{6,4},{7,5},{8,10},{9,11},{10,... | collective-permute-start | bytes 491528 | tf_op jit(solution)/shard_map/ppermute | solution.py:376
  177.7 8.8 %collective-permute-start.23 = (bf16[64,2304]{1,0:T(8,128)(2,1)S(1)}, bf16[64,2304]{1,0:T(8,128)(2,1)S(1)}, u32[]{:S(2)}, u32[]{:S(2)}) collective-permute-start(bf16[64,2304]{1,0:T(8,128)(2,1)S(1)} %slice.155), channel_id=1, source_target_pairs={{0,4},{1,5},{2,6},{3,7},{4,0},{5,1},{6,2},{7,3},{8,12},{9,13},{10,... | collective-permute-start | bytes 884744 | tf_op jit(solution)/shard_map/ppermute | solution.py:376
  179.5 10.1 %collective-permute-start.28 = (bf16[64,2560]{1,0:T(8,128)(2,1)S(1)}, bf16[64,2560]{1,0:T(8,128)(2,1)S(1)}, u32[]{:S(2)}, u32[]{:S(2)}) collective-permute-start(bf16[64,2560]{1,0:T(8,128)(2,1)S(1)} %slice.159), channel_id=1, source_target_pairs={{0,1},{1,0},{2,3},{3,2},{4,5},{5,4},{6,7},{7,6},{8,9},{9,8},{10,11... | collective-permute-start | bytes 983048 | tf_op jit(solution)/shard_map/ppermute | solution.py:376
  183.4 19.7 %collective-permute-start.32 = (bf16[32,1280]{1,0:T(8,128)(2,1)S(1)}, bf16[32,1280]{1,0:T(8,128)(2,1)S(1)}, u32[]{:S(2)}, u32[]{:S(2)}) collective-permute-start(bf16[32,1280]{1,0:T(8,128)(2,1)S(1)} %slice.165), channel_id=1, source_target_pairs={{0,1},{1,0},{2,3},{3,2},{4,5},{5,4},{6,7},{7,6},{8,9},{9,8},{10,11... | collective-permute-start | bytes 245768 | tf_op jit(solution)/shard_map/ppermute | solution.py:376
  186.6 18.8 %collective-permute-start.26 = (bf16[32,2304]{1,0:T(8,128)(2,1)S(1)}, bf16[32,2304]{1,0:T(8,128)(2,1)S(1)}, u32[]{:S(2)}, u32[]{:S(2)}) collective-permute-start(bf16[32,2304]{1,0:T(8,128)(2,1)S(1)} %slice.157), channel_id=1, source_target_pairs={{0,2},{1,3},{2,0},{3,1},{4,6},{5,7},{6,4},{7,5},{8,10},{9,11},{10,... | collective-permute-start | bytes 442376 | tf_op jit(solution)/shard_map/ppermute | solution.py:376
  189.7 22.0 %slice-start = ((s8[6291456]{0:T(1024)(128)(4,1)}), s8[4194304]{0:T(1024)(128)(4,1)S(1)}, s32[]{:S(2)}) async-start(s8[6291456]{0:T(1024)(128)(4,1)} %bitcast.8), calls=%async_computation | async-start | bytes 8388608
  189.7 22.0 %slice-start.1 = ((s8[6291456]{0:T(1024)(128)(4,1)}), s8[2097152]{0:T(1024)(128)(4,1)S(1)}, s32[]{:S(2)}) async-start(s8[6291456]{0:T(1024)(128)(4,1)} %bitcast.8), calls=%async_computation.1 | async-start | bytes 4194304
  202.0 29.5 %collective-permute-start.34 = (bf16[128,2304]{1,0:T(8,128)(2,1)S(1)}, bf16[128,2304]{1,0:T(8,128)(2,1)S(1)}, u32[]{:S(2)}, u32[]{:S(2)}) collective-permute-start(bf16[128,2304]{1,0:T(8,128)(2,1)S(1)} %get-tuple-element.77.refs_5_), channel_id=1, source_target_pairs={{0,1},{1,0},{2,3},{3,2},{4,5},{5,4},{6,7},{7,6},{8,9},{9,8},{10,11... | collective-permute-start | bytes 1769480 | tf_op jit(solution)/shard_map/ppermute | solution.py:376
  202.3 9.2 %collective-permute-start.31 = (bf16[32,2560]{1,0:T(8,128)(2,1)S(1)}, bf16[32,2560]{1,0:T(8,128)(2,1)S(1)}, u32[]{:S(2)}, u32[]{:S(2)}) collective-permute-start(bf16[32,2560]{1,0:T(8,128)(2,1)S(1)} %slice.163), channel_id=1, source_target_pairs={{0,4},{1,5},{2,6},{3,7},{4,0},{5,1},{6,2},{7,3},{8,12},{9,13},{10,... | collective-permute-start | bytes 491528 | tf_op jit(solution)/shard_map/ppermute | solution.py:376
  203.1 28.5 %collective-permute-start.35 = (bf16[128,2560]{1,0:T(8,128)(2,1)S(1)}, bf16[128,2560]{1,0:T(8,128)(2,1)S(1)}, u32[]{:S(2)}, u32[]{:S(2)}) collective-permute-start(bf16[128,2560]{1,0:T(8,128)(2,1)S(1)} %get-tuple-element.79.refs_7_), channel_id=1, source_target_pairs={{0,2},{1,3},{2,0},{3,1},{4,6},{5,7},{6,4},{7,5},{8,10},{9,11},{10,... | collective-permute-start | bytes 1966088 | tf_op jit(solution)/shard_map/ppermute | solution.py:376
  204.7 26.7 %collective-permute-start.36 = (bf16[128,1280]{1,0:T(8,128)(2,1)S(1)}, bf16[128,1280]{1,0:T(8,128)(2,1)S(1)}, u32[]{:S(2)}, u32[]{:S(2)}) collective-permute-start(bf16[128,1280]{1,0:T(8,128)(2,1)S(1)} %get-tuple-element.81.refs_9_), channel_id=1, source_target_pairs={{0,4},{1,5},{2,6},{3,7},{4,0},{5,1},{6,2},{7,3},{8,12},{9,13},{10,... | collective-permute-start | bytes 983048 | tf_op jit(solution)/shard_map/ppermute | solution.py:376
  211.7 19.8 %collective-permute-start.33 = (bf16[16,6144]{1,0:T(8,128)(2,1)S(1)}, bf16[16,6144]{1,0:T(8,128)(2,1)S(1)}, u32[]{:S(2)}, u32[]{:S(2)}) collective-permute-start(bf16[16,6144]{1,0:T(8,128)(2,1)S(1)} %slice.167), channel_id=1, source_target_pairs={{0,8},{1,9},{2,10},{3,11},{4,12},{5,13},{6,14},{7,15},{8,0},{9,1},... | collective-permute-start | bytes 589832 | tf_op jit(solution)/shard_map/ppermute | solution.py:376
  231.8 14.0 %collective-permute-start.37 = (bf16[64,2304]{1,0:T(8,128)(2,1)S(1)}, bf16[64,2304]{1,0:T(8,128)(2,1)S(1)}, u32[]{:S(2)}, u32[]{:S(2)}) collective-permute-start(bf16[64,2304]{1,0:T(8,128)(2,1)S(1)} %slice.139), channel_id=1, source_target_pairs={{0,4},{1,5},{2,6},{3,7},{4,0},{5,1},{6,2},{7,3},{8,12},{9,13},{10,... | collective-permute-start | bytes 884744 | tf_op jit(solution)/shard_map/ppermute | solution.py:376
  234.1 11.6 %collective-permute-start.39 = (bf16[64,1280]{1,0:T(8,128)(2,1)S(1)}, bf16[64,1280]{1,0:T(8,128)(2,1)S(1)}, u32[]{:S(2)}, u32[]{:S(2)}) collective-permute-start(bf16[64,1280]{1,0:T(8,128)(2,1)S(1)} %slice.143), channel_id=1, source_target_pairs={{0,2},{1,3},{2,0},{3,1},{4,6},{5,7},{6,4},{7,5},{8,10},{9,11},{10,... | collective-permute-start | bytes 491528 | tf_op jit(solution)/shard_map/ppermute | solution.py:376
  244.0 7.1 %collective-permute-start.38 = (bf16[64,2560]{1,0:T(8,128)(2,1)S(1)}, bf16[64,2560]{1,0:T(8,128)(2,1)S(1)}, u32[]{:S(2)}, u32[]{:S(2)}) collective-permute-start(bf16[64,2560]{1,0:T(8,128)(2,1)S(1)} %slice.141), channel_id=1, source_target_pairs={{0,1},{1,0},{2,3},{3,2},{4,5},{5,4},{6,7},{7,6},{8,9},{9,8},{10,11... | collective-permute-start | bytes 983048 | tf_op jit(solution)/shard_map/ppermute | solution.py:376
  251.3 4.5 %collective-permute-start.42 = (bf16[32,1280]{1,0:T(8,128)(2,1)S(1)}, bf16[32,1280]{1,0:T(8,128)(2,1)S(1)}, u32[]{:S(2)}, u32[]{:S(2)}) collective-permute-start(bf16[32,1280]{1,0:T(8,128)(2,1)S(1)} %slice.149), channel_id=1, source_target_pairs={{0,1},{1,0},{2,3},{3,2},{4,5},{5,4},{6,7},{7,6},{8,9},{9,8},{10,11... | collective-permute-start | bytes 245768 | tf_op jit(solution)/shard_map/ppermute | solution.py:376
  253.0 5.4 %collective-permute-start.41 = (bf16[32,2560]{1,0:T(8,128)(2,1)S(1)}, bf16[32,2560]{1,0:T(8,128)(2,1)S(1)}, u32[]{:S(2)}, u32[]{:S(2)}) collective-permute-start(bf16[32,2560]{1,0:T(8,128)(2,1)S(1)} %slice.147), channel_id=1, source_target_pairs={{0,4},{1,5},{2,6},{3,7},{4,0},{5,1},{6,2},{7,3},{8,12},{9,13},{10,... | collective-permute-start | bytes 491528 | tf_op jit(solution)/shard_map/ppermute | solution.py:376
  253.1 5.2 %collective-permute-start.40 = (bf16[32,2304]{1,0:T(8,128)(2,1)S(1)}, bf16[32,2304]{1,0:T(8,128)(2,1)S(1)}, u32[]{:S(2)}, u32[]{:S(2)}) collective-permute-start(bf16[32,2304]{1,0:T(8,128)(2,1)S(1)} %slice.145), channel_id=1, source_target_pairs={{0,2},{1,3},{2,0},{3,1},{4,6},{5,7},{6,4},{7,5},{8,10},{9,11},{10,... | collective-permute-start | bytes 442376 | tf_op jit(solution)/shard_map/ppermute | solution.py:376
  258.5 10.4 %collective-permute-start.43 = (bf16[16,6144]{1,0:T(8,128)(2,1)S(1)}, bf16[16,6144]{1,0:T(8,128)(2,1)S(1)}, u32[]{:S(2)}, u32[]{:S(2)}) collective-permute-start(bf16[16,6144]{1,0:T(8,128)(2,1)S(1)} %slice.169), channel_id=1, source_target_pairs={{0,8},{1,9},{2,10},{3,11},{4,12},{5,13},{6,14},{7,15},{8,0},{9,1},... | collective-permute-start | bytes 589832 | tf_op jit(solution)/shard_map/ppermute | solution.py:376
  (1 other events, 2.8 us)

commit v2 on v1

--- a/solution.py
+++ b/solution.py
@@ -338,8 +338,8 @@
                 input_output_aliases=aliases,
                 compiler_params=pltpu.CompilerParams(vmem_limit_bytes=32 * 1024 * 1024),
                 cost_estimate=pl.CostEstimate(
-                    flops=2 * tokens * tall * broad // shares,
-                    bytes_accessed=2 * tall * broad // shares,
+                    flops=tall * broad // shares,
+                    bytes_accessed=tokens * broad // shares,
                     transcendentals=0,
                 ),
                 name="grad",
@@ -463,8 +463,9 @@
         del work[:count]
 
     held = totals[last]
-    late = [stage(pairs, stages - 1, held[0][0], len(orders)) for pairs in early]
-    advance(2, [half for pair in held for half in pair] + [total for summed in late for total in summed])
+    advance(1, [half for pair in held for half in pair])
+    late = [stage(pairs, stages - 1, outs[0], len(orders)) for pairs in early]
+    advance(1, [total for summed in late for total in summed])
     shares = [finish(summed, outs[1]) for summed in late]
     for at in range(stages):
         summed = stage(held, at, outs[1 - at] if at < 2 else None, 2)

time: 270 us -> 262 us (0.970)
  waiting for transfers between devices: 108 us -> 100 us
    ppermute x40, waiting for transfers between devices: 107 us -> 99.3 us  [swap(): return lax.ppermute(value, 'col', [(i, i ^ 1 << bit) for i in range(n)])]
  transfers between devices with their start and end apart: 44 -> 44, of which waited for: 23 -> 22; matrix products, arithmetic and copies ran while one was open for 2% -> 2% of each run, Pallas kernels for 36% -> 37%
where the time goes in v2:
time: 262 us
  waiting for transfers between devices  100 us (38%)
  Pallas kernels  96.5 us (37%)
  starting transfers between devices  51.2 us (20%)
  other arithmetic  8.43 us (3%)
  local copies, waits for them, and re-layouts  4.47 us (2%)
    ppermute x40, waiting for transfers between devices, swap(): return lax.ppermute(value, 'col', [(i, i ^ 1 << bit) for i in range(n)])  99.3 us
    ppermute x40, starting transfers between devices, swap(): return lax.ppermute(value, 'col', [(i, i ^ 1 << bit) for i in range(n)])  50.1 us
    pallas_call x2, Pallas kernels, forward(): pl.pallas_call(functools.partial(forward_kernel, moves, block), in_specs=...  39.3 us
    pallas_call x4, Pallas kernels, call(): pl.pallas_call(functools.partial(grad_kernel, block, factor, (off[0] * ti...  33.3 us
    pallas_call x2, Pallas kernels, backward(): pl.pallas_call(functools.partial(backward_kernel, parts, block), in_specs...  23.9 us
  transfers between devices with their start and end apart: 44, of which 22 were waited for; matrix products, arithmetic and copies ran while one was open for 2% of the time, Pallas kernels for 37%

profile of v2, /device:TPU:0, one launch (start us, length us, event | category | flops | bytes accessed | tf_op | source)
XLA Modules:
  0.0 262.2 jit_solution(6532418362266393470)
XLA Ops:
  0.6 1.3 slice_bitcast_fusion.2
  2.0 4.1 %collective-permute-start = (bf16[2,16,6144]{2,1,0:T(8,128)(2,1)S(1)}, bf16[2,16,6144]{2,1,0:T(8,128)(2,1)S(1)}, u32[]{:S(2)}, u32[]{:S(2)}) collective-permute-start(bf16[2,16,6144]{2,1,0:T(8,128)(2,1)S(1)} %pad_maximum_fusion.12), channel_id=1, source_target_pairs={{0,8},{1,9},{2,10},{3,11},{4,12},{5,13},{6,14},{7,15},{8,0},{9,1},... | collective-permute-start | bytes 1179656 | tf_op jit(solution)/shard_map/ppermute | solution.py:376
  6.1 17.5 %collective-permute-done = bf16[2,16,6144]{2,1,0:T(8,128)(2,1)S(1)} collective-permute-done((bf16[2,16,6144]{2,1,0:T(8,128)(2,1)S(1)}, bf16[2,16,6144]{2,1,0:T(8,128)(2,1)S(1)}, u32[]{:S(2)}, u32[]{:S(2)}) %collective-permute-start) | collective-permute-done | bytes 393248 | tf_op jit(solution)/shard_map/ppermute | solution.py:376
  23.6 1.6 collective-permute-start.4
  25.3 1.6 collective-permute-start.1
  27.7 1.4 collective-permute-done.4
  29.1 1.6 collective-permute-start.7
  30.7 4.7 %collective-permute-done.1 = bf16[2,32,2304]{2,1,0:T(8,128)(2,1)S(1)} collective-permute-done((bf16[2,32,2304]{2,1,0:T(8,128)(2,1)S(1)}, bf16[2,32,2304]{2,1,0:T(8,128)(2,1)S(1)}, u32[]{:S(2)}, u32[]{:S(2)}) %collective-permute-start.1) | collective-permute-done | bytes 294944 | tf_op jit(solution)/shard_map/ppermute | solution.py:376
  35.4 3.1 %collective-permute-start.5 = (bf16[2,16,6144]{2,1,0:T(8,128)(2,1)S(1)}, bf16[2,16,6144]{2,1,0:T(8,128)(2,1)S(1)}, u32[]{:S(2)}, u32[]{:S(2)}) collective-permute-start(bf16[2,16,6144]{2,1,0:T(8,128)(2,1)S(1)} %pad_maximum_fusion.13), channel_id=1, source_target_pairs={{0,8},{1,9},{2,10},{3,11},{4,12},{5,13},{6,14},{7,15},{8,0},{9,1},... | collective-permute-start | bytes 1179656 | tf_op jit(solution)/shard_map/ppermute | solution.py:376
  38.5 1.7 collective-permute-start.2
  40.9 14.3 %collective-permute-done.5 = bf16[2,16,6144]{2,1,0:T(8,128)(2,1)S(1)} collective-permute-done((bf16[2,16,6144]{2,1,0:T(8,128)(2,1)S(1)}, bf16[2,16,6144]{2,1,0:T(8,128)(2,1)S(1)}, u32[]{:S(2)}, u32[]{:S(2)}) %collective-permute-start.5) | collective-permute-done | bytes 393248 | tf_op jit(solution)/shard_map/ppermute | solution.py:376
  55.2 4.5 %collective-permute-done.2 = bf16[2,64,2304]{2,1,0:T(8,128)(2,1)S(1)} collective-permute-done((bf16[2,64,2304]{2,1,0:T(8,128)(2,1)S(1)}, bf16[2,64,2304]{2,1,0:T(8,128)(2,1)S(1)}, u32[]{:S(2)}, u32[]{:S(2)}) %collective-permute-start.2) | collective-permute-done | bytes 589856 | tf_op jit(solution)/shard_map/ppermute | solution.py:376
  62.3 1.4 collective-permute-start.10
  63.6 2.8 %collective-permute-done.12 = bf16[2,32,1280]{2,1,0:T(8,128)(2,1)S(1)} collective-permute-done((bf16[2,32,1280]{2,1,0:T(8,128)(2,1)S(1)}, bf16[2,32,1280]{2,1,0:T(8,128)(2,1)S(1)}, u32[]{:S(2)}, u32[]{:S(2)}) %collective-permute-start.12) | collective-permute-done | bytes 163872 | tf_op jit(solution)/shard_map/ppermute | solution.py:376
  67.0 4.3 %collective-permute-done.8 = bf16[2,32,2304]{2,1,0:T(8,128)(2,1)S(1)} collective-permute-done((bf16[2,32,2304]{2,1,0:T(8,128)(2,1)S(1)}, bf16[2,32,2304]{2,1,0:T(8,128)(2,1)S(1)}, u32[]{:S(2)}, u32[]{:S(2)}) %collective-permute-start.8) | collective-permute-done | bytes 294944 | tf_op jit(solution)/shard_map/ppermute | solution.py:376
  72.5 2.2 collective-permute-start.11
  75.5 6.5 %collective-permute-done.9 = bf16[2,64,2304]{2,1,0:T(8,128)(2,1)S(1)} collective-permute-done((bf16[2,64,2304]{2,1,0:T(8,128)(2,1)S(1)}, bf16[2,64,2304]{2,1,0:T(8,128)(2,1)S(1)}, u32[]{:S(2)}, u32[]{:S(2)}) %collective-permute-start.9) | collective-permute-done | bytes 589856 | tf_op jit(solution)/shard_map/ppermute | solution.py:376
  84.4 1.5 collective-permute-start.15
  85.9 1.7 collective-permute-start.14
  89.8 8.9 %collective-permute-done.16.refs_5_ = bf16[2,128,1280]{2,1,0:T(8,128)(2,1)S(1)} collective-permute-done((bf16[2,128,1280]{2,1,0:T(8,128)(2,1)S(1)}, bf16[2,128,1280]{2,1,0:T(8,128)(2,1)S(1)}, u32[]{:S(2)}, u32[]{:S(2)}) %collective-permute-start.16) | collective-permute-done | bytes 655392 | tf_op jit(solution)/shard_map/ppermute | solution.py:376
  98.8 16.2 %collective-permute-done.14.refs_1_ = bf16[2,128,2304]{2,1,0:T(8,128)(2,1)} collective-permute-done((bf16[2,128,2304]{2,1,0:T(8,128)(2,1)S(1)}, bf16[2,128,2304]{2,1,0:T(8,128)(2,1)}, u32[]{:S(2)}, u32[]{:S(2)}) %collective-permute-start.14) | collective-permute-done | bytes 1179680 | tf_op jit(solution)/shard_map/ppermute | solution.py:376
  114.9 1.5 collective-permute-done.15.refs_3_
  116.5 19.7 %forward.2 = (bf16[2,256,6144]{2,1,0:T(8,128)(2,1)}, bf16[256,1536]{1,0:T(8,128)(2,1)S(1)}, bf16[256,1536]{1,0:T(8,128)(2,1)S(1)}) custom-call(s32[48,12]{1,0:T(8,128)S(1)} %copy.12.up_on.pattern, s32[12,48]{1,0:T(8,128)S(1)} %copy-done.1, bf16[2,128,2304]{2,1,0:T(8,128)(2,1)S(1)} %pad_maximum_fusion.2.refs_0_, ...), custom_call_target="tpu_custom_call" | custom-call | flops 1572864 | bytes 1572864 | tf_op jit(solution)/shard_map/forward/pallas_call | solution.py:174
  140.7 11.7 %backward.2 = (bf16[128,2304]{1,0:T(8,128)(2,1)S(1)}, bf16[128,2304]{1,0:T(8,128)(2,1)S(1)}, bf16[128,2560]{1,0:T(8,128)(2,1)S(1)}, bf16[128,2560]{1,0:T(8,128)(...) custom-call(s32[48,12]{1,0:T(8,128)S(1)} %copy.12.up_on.pattern, ...), custom_call_target="tpu_custom_call" | custom-call | flops 1572864 | bytes 1572864 | tf_op jit(solution)/shard_map/backward/pallas_call | solution.py:250
  152.4 1.3 collective-permute-start.29
  153.8 1.5 collective-permute-start.21
  155.2 1.6 collective-permute-start.27
  156.8 19.5 %forward.3 = (bf16[2,256,6144]{2,1,0:T(8,128)(2,1)}, bf16[256,1536]{1,0:T(8,128)(2,1)S(1)}, bf16[256,1536]{1,0:T(8,128)(2,1)S(1)}) custom-call(s32[48,12]{1,0:T(8,128)S(1)} %copy.12.up_on.pattern, s32[12,48]{1,0:T(8,128)S(1)} %copy-done.1, bf16[2,128,2304]{2,1,0:T(8,128)(2,1)} %pad_maximum_fusion.3.refs_8_.refs_0_, ...), custom_call_target="tpu_custom_call" | custom-call | flops 1572864 | bytes 1572864 | tf_op jit(solution)/shard_map/forward/pallas_call | solution.py:174
  177.7 1.6 collective-permute-start.23
  180.9 2.4 collective-permute-done.30
  183.9 2.6 collective-permute-done.23
  186.6 1.6 collective-permute-start.26
  188.3 1.4 collective-permute-done.28
  189.8 12.2 %backward.3 = (bf16[128,2304]{1,0:T(8,128)(2,1)S(1)}, bf16[128,2304]{1,0:T(8,128)(2,1)S(1)}, bf16[128,2560]{1,0:T(8,128)(2,1)S(1)}, bf16[128,2560]{1,0:T(8,128)(...) custom-call(s32[48,12]{1,0:T(8,128)S(1)} %copy.12.up_on.pattern, ...), custom_call_target="tpu_custom_call" | custom-call | flops 1572864 | bytes 1572864 | tf_op jit(solution)/shard_map/backward/pallas_call | solution.py:250
  203.0 1.5 collective-permute-start.35
  204.6 2.8 %copy-done = bf16[2,256,6144]{2,1,0:T(8,128)(2,1)S(1)} copy-done((bf16[2,256,6144]{2,1,0:T(8,128)(2,1)S(1)}, bf16[2,256,6144]{2,1,0:T(8,128)(2,1)}, u32[]{:S(2)}) %copy-start) | copy-done | bytes 6291480
  207.4 8.7 %grad.4.refs_7_ = bf16[6144,1536]{1,0:T(8,128)(2,1)} custom-call(s32[48,12]{1,0:T(8,128)S(1)} %copy.12.up_on.pattern, bf16[2,256,6144]{2,1,0:T(8,128)(2,1)S(1)} %bitcast.9, bf16[2,256,6144]{2,1,0:T(8,128)(2,1)S(1)} %copy-done, bf16[256,1536]{1,0:T(8,128)(2,1)S(1)} %get-tuple-element.96.dhid_ref.refs_2_, ...), custom_call_target="tpu_custom_call" | custom-call | flops 4718592 | bytes 393216 | tf_op jit(solution)/shard_map/grad/pallas_call | solution.py:323
  216.8 4.5 %collective-permute-done.31 = bf16[32,2560]{1,0:T(8,128)(2,1)S(1)} collective-permute-done((bf16[32,2560]{1,0:T(8,128)(2,1)S(1)}, bf16[32,2560]{1,0:T(8,128)(2,1)S(1)}, u32[]{:S(2)}, u32[]{:S(2)}) %collective-permute-start.31) | collective-permute-done | bytes 163872 | tf_op jit(solution)/shard_map/ppermute | solution.py:376
  221.4 8.1 %grad.5.refs_7_ = bf16[1536,6144]{1,0:T(8,128)(2,1)} custom-call(s32[12,48]{1,0:T(8,128)S(1)} %copy-done.1, bf16[256,1536]{1,0:T(8,128)(2,1)S(1)} %get-tuple-element.95.refs_0_, bf16[256,1536]{1,0:T(8,128)(2,1)S(1)} %get-tuple-element.93.refs_1_, bf16[2,256,6144]{2,1,0:T(8,128)(2,1)S(1)} %bitcast.9, bf16[2,256,6144]{2,1,0:T(8,128)(2,1)S(1)} %copy-done, ...), custom_call_target="tpu_custom_call" | custom-call | flops 4718592 | bytes 1572864 | tf_op jit(solution)/shard_map/grad/pallas_call | solution.py:323
  230.6 1.7 collective-permute-start.33
  232.4 1.6 collective-permute-start.37
  234.0 1.8 collective-permute-start.38
  235.8 8.4 %grad.6 = bf16[6144,1536]{1,0:T(8,128)(2,1)} custom-call(s32[48,12]{1,0:T(8,128)S(1)} %copy.12.up_on.pattern, bf16[2,256,6144]{2,1,0:T(8,128)(2,1)S(1)} %bitcast.9, bf16[2,256,6144]{2,1,0:T(8,128)(2,1)S(1)} %copy-done, bf16[256,1536]{1,0:T(8,128)(2,1)S(1)} %get-tuple-element.96.dhid_ref.refs_2_, ...), custom_call_target="tpu_custom_call", output_to_operand_aliasing={{}: (8, {})} | custom-call | flops 4718592 | bytes 393216 | tf_op jit(solution)/shard_map/grad/pallas_call | solution.py:323
  245.4 1.8 collective-permute-start.41
  247.2 1.8 collective-permute-done.42
  250.1 1.3 collective-permute-done.41
  251.5 1.7 collective-permute-start.43
  253.2 8.1 %grad.7 = bf16[1536,6144]{1,0:T(8,128)(2,1)} custom-call(s32[12,48]{1,0:T(8,128)S(1)} %copy-done.1, bf16[256,1536]{1,0:T(8,128)(2,1)S(1)} %get-tuple-element.95.refs_0_, bf16[256,1536]{1,0:T(8,128)(2,1)S(1)} %get-tuple-element.93.refs_1_, bf16[2,256,6144]{2,1,0:T(8,128)(2,1)S(1)} %bitcast.9, ...), custom_call_target="tpu_custom_call", output_to_operand_aliasing={{}: (8, {})} | custom-call | flops 4718592 | bytes 1572864 | tf_op jit(solution)/shard_map/grad/pallas_call | solution.py:323
  (122 shorter events, 25.8 us)
Async XLA Ops:
  2.0 21.6 %collective-permute-start = (bf16[2,16,6144]{2,1,0:T(8,128)(2,1)S(1)}, bf16[2,16,6144]{2,1,0:T(8,128)(2,1)S(1)}, u32[]{:S(2)}, u32[]{:S(2)}) collective-permute-start(bf16[2,16,6144]{2,1,0:T(8,128)(2,1)S(1)} %pad_maximum_fusion.12), channel_id=1, source_target_pairs={{0,8},{1,9},{2,10},{3,11},{4,12},{5,13},{6,14},{7,15},{8,0},{9,1},... | collective-permute-start | bytes 1179656 | tf_op jit(solution)/shard_map/ppermute | solution.py:376
  23.6 5.5 %collective-permute-start.4 = (bf16[2,32,1280]{2,1,0:T(8,128)(2,1)S(1)}, bf16[2,32,1280]{2,1,0:T(8,128)(2,1)S(1)}, u32[]{:S(2)}, u32[]{:S(2)}) collective-permute-start(bf16[2,32,1280]{2,1,0:T(8,128)(2,1)S(1)} %pad_maximum_fusion.19), channel_id=1, source_target_pairs={{0,1},{1,0},{2,3},{3,2},{4,5},{5,4},{6,7},{7,6},{8,9},{9,8},{10,11... | collective-permute-start | bytes 491528 | tf_op jit(solution)/shard_map/ppermute | solution.py:376
  25.3 10.0 %collective-permute-start.1 = (bf16[2,32,2304]{2,1,0:T(8,128)(2,1)S(1)}, bf16[2,32,2304]{2,1,0:T(8,128)(2,1)S(1)}, u32[]{:S(2)}, u32[]{:S(2)}) collective-permute-start(bf16[2,32,2304]{2,1,0:T(8,128)(2,1)S(1)} %slice.152), channel_id=1, source_target_pairs={{0,2},{1,3},{2,0},{3,1},{4,6},{5,7},{6,4},{7,5},{8,10},{9,11},{10,... | collective-permute-start | bytes 884744 | tf_op jit(solution)/shard_map/ppermute | solution.py:376
  27.0 8.4 %collective-permute-start.3 = (bf16[2,32,2560]{2,1,0:T(8,128)(2,1)S(1)}, bf16[2,32,2560]{2,1,0:T(8,128)(2,1)S(1)}, u32[]{:S(2)}, u32[]{:S(2)}) collective-permute-start(bf16[2,32,2560]{2,1,0:T(8,128)(2,1)S(1)} %slice.153), channel_id=1, source_target_pairs={{0,4},{1,5},{2,6},{3,7},{4,0},{5,1},{6,2},{7,3},{8,12},{9,13},{10,... | collective-permute-start | bytes 983048 | tf_op jit(solution)/shard_map/ppermute | solution.py:376
  29.1 11.7 %collective-permute-start.7 = (bf16[2,64,1280]{2,1,0:T(8,128)(2,1)S(1)}, bf16[2,64,1280]{2,1,0:T(8,128)(2,1)S(1)}, u32[]{:S(2)}, u32[]{:S(2)}) collective-permute-start(bf16[2,64,1280]{2,1,0:T(8,128)(2,1)S(1)} %pad_maximum_fusion.17), channel_id=1, source_target_pairs={{0,2},{1,3},{2,0},{3,1},{4,6},{5,7},{6,4},{7,5},{8,10},{9,11},{10,... | collective-permute-start | bytes 983048 | tf_op jit(solution)/shard_map/ppermute | solution.py:376
  35.4 19.8 %collective-permute-start.5 = (bf16[2,16,6144]{2,1,0:T(8,128)(2,1)S(1)}, bf16[2,16,6144]{2,1,0:T(8,128)(2,1)S(1)}, u32[]{:S(2)}, u32[]{:S(2)}) collective-permute-start(bf16[2,16,6144]{2,1,0:T(8,128)(2,1)S(1)} %pad_maximum_fusion.13), channel_id=1, source_target_pairs={{0,8},{1,9},{2,10},{3,11},{4,12},{5,13},{6,14},{7,15},{8,0},{9,1},... | collective-permute-start | bytes 1179656 | tf_op jit(solution)/shard_map/ppermute | solution.py:376
  38.5 21.3 %collective-permute-start.2 = (bf16[2,64,2304]{2,1,0:T(8,128)(2,1)S(1)}, bf16[2,64,2304]{2,1,0:T(8,128)(2,1)S(1)}, u32[]{:S(2)}, u32[]{:S(2)}) collective-permute-start(bf16[2,64,2304]{2,1,0:T(8,128)(2,1)S(1)} %pad_maximum_fusion.10), channel_id=1, source_target_pairs={{0,4},{1,5},{2,6},{3,7},{4,0},{5,1},{6,2},{7,3},{8,12},{9,13},{10,... | collective-permute-start | bytes 1769480 | tf_op jit(solution)/shard_map/ppermute | solution.py:376
  40.3 19.6 %collective-permute-start.6 = (bf16[2,64,2560]{2,1,0:T(8,128)(2,1)S(1)}, bf16[2,64,2560]{2,1,0:T(8,128)(2,1)S(1)}, u32[]{:S(2)}, u32[]{:S(2)}) collective-permute-start(bf16[2,64,2560]{2,1,0:T(8,128)(2,1)S(1)} %pad_maximum_fusion.6), channel_id=1, source_target_pairs={{0,1},{1,0},{2,3},{3,2},{4,5},{5,4},{6,7},{7,6},{8,9},{9,8},{10,11... | collective-permute-start | bytes 1966088 | tf_op jit(solution)/shard_map/ppermute | solution.py:376
  61.0 5.4 %collective-permute-start.12 = (bf16[2,32,1280]{2,1,0:T(8,128)(2,1)S(1)}, bf16[2,32,1280]{2,1,0:T(8,128)(2,1)S(1)}, u32[]{:S(2)}, u32[]{:S(2)}) collective-permute-start(bf16[2,32,1280]{2,1,0:T(8,128)(2,1)S(1)} %slice.123), channel_id=1, source_target_pairs={{0,1},{1,0},{2,3},{3,2},{4,5},{5,4},{6,7},{7,6},{8,9},{9,8},{10,11... | collective-permute-start | bytes 491528 | tf_op jit(solution)/shard_map/ppermute | solution.py:376
  61.7 9.6 %collective-permute-start.8 = (bf16[2,32,2304]{2,1,0:T(8,128)(2,1)S(1)}, bf16[2,32,2304]{2,1,0:T(8,128)(2,1)S(1)}, u32[]{:S(2)}, u32[]{:S(2)}) collective-permute-start(bf16[2,32,2304]{2,1,0:T(8,128)(2,1)S(1)} %slice.121), channel_id=1, source_target_pairs={{0,2},{1,3},{2,0},{3,1},{4,6},{5,7},{6,4},{7,5},{8,10},{9,11},{10,... | collective-permute-start | bytes 884744 | tf_op jit(solution)/shard_map/ppermute | solution.py:376
  62.3 10.2 %collective-permute-start.10 = (bf16[2,32,2560]{2,1,0:T(8,128)(2,1)S(1)}, bf16[2,32,2560]{2,1,0:T(8,128)(2,1)S(1)}, u32[]{:S(2)}, u32[]{:S(2)}) collective-permute-start(bf16[2,32,2560]{2,1,0:T(8,128)(2,1)S(1)} %slice.122), channel_id=1, source_target_pairs={{0,4},{1,5},{2,6},{3,7},{4,0},{5,1},{6,2},{7,3},{8,12},{9,13},{10,... | collective-permute-start | bytes 983048 | tf_op jit(solution)/shard_map/ppermute | solution.py:376
  66.5 9.0 %collective-permute-start.13 = (bf16[2,64,1280]{2,1,0:T(8,128)(2,1)S(1)}, bf16[2,64,1280]{2,1,0:T(8,128)(2,1)S(1)}, u32[]{:S(2)}, u32[]{:S(2)}) collective-permute-start(bf16[2,64,1280]{2,1,0:T(8,128)(2,1)S(1)} %pad_maximum_fusion.18), channel_id=1, source_target_pairs={{0,2},{1,3},{2,0},{3,1},{4,6},{5,7},{6,4},{7,5},{8,10},{9,11},{10,... | collective-permute-start | bytes 983048 | tf_op jit(solution)/shard_map/ppermute | solution.py:376
  71.3 10.7 %collective-permute-start.9 = (bf16[2,64,2304]{2,1,0:T(8,128)(2,1)S(1)}, bf16[2,64,2304]{2,1,0:T(8,128)(2,1)S(1)}, u32[]{:S(2)}, u32[]{:S(2)}) collective-permute-start(bf16[2,64,2304]{2,1,0:T(8,128)(2,1)S(1)} %pad_maximum_fusion.11), channel_id=1, source_target_pairs={{0,4},{1,5},{2,6},{3,7},{4,0},{5,1},{6,2},{7,3},{8,12},{9,13},{10,... | collective-permute-start | bytes 1769480 | tf_op jit(solution)/shard_map/ppermute | solution.py:376
  72.5 10.8 %collective-permute-start.11 = (bf16[2,64,2560]{2,1,0:T(8,128)(2,1)S(1)}, bf16[2,64,2560]{2,1,0:T(8,128)(2,1)S(1)}, u32[]{:S(2)}, u32[]{:S(2)}) collective-permute-start(bf16[2,64,2560]{2,1,0:T(8,128)(2,1)S(1)} %pad_maximum_fusion.8), channel_id=1, source_target_pairs={{0,1},{1,0},{2,3},{3,2},{4,5},{5,4},{6,7},{7,6},{8,9},{9,8},{10,11... | collective-permute-start | bytes 1966088 | tf_op jit(solution)/shard_map/ppermute | solution.py:376
  83.2 6.5 %copy-start.2 = (s32[48,12]{0,1:T(8,128)S(1)}, s32[48,12]{0,1:T(8,128)}, u32[]{:S(2)}) copy-start(s32[48,12]{0,1:T(8,128)} %param.10) | copy-start | bytes 6916
  83.2 33.3 %copy-start.1 = (s32[12,48]{1,0:T(8,128)S(1)}, s32[12,48]{1,0:T(8,128)}, u32[]{:S(2)}) copy-start(s32[12,48]{1,0:T(8,128)} %pattern.5) | copy-start | bytes 6916
  84.4 32.0 %collective-permute-start.15 = (bf16[2,128,2560]{2,1,0:T(8,128)(2,1)}, bf16[2,128,2560]{2,1,0:T(8,128)(2,1)}, u32[]{:S(2)}, u32[]{:S(2)}) collective-permute-start(bf16[2,128,2560]{2,1,0:T(8,128)(2,1)} %pad_maximum_fusion.refs_2_), channel_id=1, source_target_pairs={{0,2},{1,3},{2,0},{3,1},{4,6},{5,7},{6,4},{7,5},{8,10},{9,11},{10,... | collective-permute-start | bytes 3932168 | tf_op jit(solution)/shard_map/ppermute | solution.py:376
  85.9 29.0 %collective-permute-start.14 = (bf16[2,128,2304]{2,1,0:T(8,128)(2,1)S(1)}, bf16[2,128,2304]{2,1,0:T(8,128)(2,1)}, u32[]{:S(2)}, u32[]{:S(2)}) collective-permute-start(bf16[2,128,2304]{2,1,0:T(8,128)(2,1)S(1)} %pad_maximum_fusion.2.refs_0_), channel_id=1, source_target_pairs={{0,1},{1,0},{2,3},{3,2},{4,5},{5,4},{6,7},{7,6},{8,9},{9,8},{10,11... | collective-permute-start | bytes 3538952 | tf_op jit(solution)/shard_map/ppermute | solution.py:376
  87.6 11.1 %collective-permute-start.16 = (bf16[2,128,1280]{2,1,0:T(8,128)(2,1)S(1)}, bf16[2,128,1280]{2,1,0:T(8,128)(2,1)S(1)}, u32[]{:S(2)}, u32[]{:S(2)}) collective-permute-start(bf16[2,128,1280]{2,1,0:T(8,128)(2,1)S(1)} %pad_maximum_fusion.7.refs_4_), channel_id=1, source_target_pairs={{0,4},{1,5},{2,6},{3,7},{4,0},{5,1},{6,2},{7,3},{8,12},{9,13},{10,... | collective-permute-start | bytes 1966088 | tf_op jit(solution)/shard_map/ppermute | solution.py:376
  88.7 50.0 %collective-permute-start.19 = (bf16[2,128,2560]{2,1,0:T(8,128)(2,1)}, bf16[2,128,2560]{2,1,0:T(8,128)(2,1)}, u32[]{:S(2)}, u32[]{:S(2)}) collective-permute-start(bf16[2,128,2560]{2,1,0:T(8,128)(2,1)} %pad_maximum_fusion.1.refs_9_.refs_2_), channel_id=1, source_target_pairs={{0,2},{1,3},{2,0},{3,1},{4,6},{5,7},{6,4},{7,5},{8,10},{9,11},{10,... | collective-permute-start | bytes 3932168 | tf_op jit(solution)/shard_map/ppermute | solution.py:376
  89.2 48.8 %collective-permute-start.18 = (bf16[2,128,2304]{2,1,0:T(8,128)(2,1)}, bf16[2,128,2304]{2,1,0:T(8,128)(2,1)}, u32[]{:S(2)}, u32[]{:S(2)}) collective-permute-start(bf16[2,128,2304]{2,1,0:T(8,128)(2,1)} %pad_maximum_fusion.3.refs_8_.refs_0_), channel_id=1, source_target_pairs={{0,1},{1,0},{2,3},{3,2},{4,5},{5,4},{6,7},{7,6},{8,9},{9,8},{10,11... | collective-permute-start | bytes 3538952 | tf_op jit(solution)/shard_map/ppermute | solution.py:376
  136.2 2.5 collective-permute-start.17
  136.3 3.4 %collective-permute-start.20 = (bf16[256,1536]{1,0:T(8,128)(2,1)S(1)}, bf16[256,1536]{1,0:T(8,128)(2,1)S(1)}, u32[]{:S(2)}, u32[]{:S(2)}) collective-permute-start(bf16[256,1536]{1,0:T(8,128)(2,1)S(1)} %get-tuple-element.55), channel_id=1, source_target_pairs={{0,16},{16,0},{1,17},{17,1},{2,18},{18,2},{3,19},{19,3},{4,20},{20... | collective-permute-start | bytes 2359304 | tf_op jit(solution)/shard_map/ppermute | solution.py:384
  136.8 20.0 %collective-permute-start.22 = (bf16[2,128,1280]{2,1,0:T(8,128)(2,1)S(1)}, bf16[2,128,1280]{2,1,0:T(8,128)(2,1)S(1)}, u32[]{:S(2)}, u32[]{:S(2)}) collective-permute-start(bf16[2,128,1280]{2,1,0:T(8,128)(2,1)S(1)} %pad_maximum_fusion.9.refs_10_.refs_4_), channel_id=1, source_target_pairs={{0,4},{1,5},{2,6},{3,7},{4,0},{5,1},{6,2},{7,3},{8,12},{9,13},{10,... | collective-permute-start | bytes 1966088 | tf_op jit(solution)/shard_map/ppermute | solution.py:376
  152.4 24.5 %collective-permute-start.29 = (bf16[128,1280]{1,0:T(8,128)(2,1)S(1)}, bf16[128,1280]{1,0:T(8,128)(2,1)S(1)}, u32[]{:S(2)}, u32[]{:S(2)}) collective-permute-start(bf16[128,1280]{1,0:T(8,128)(2,1)S(1)} %get-tuple-element.62.refs_13_), channel_id=1, source_target_pairs={{0,4},{1,5},{2,6},{3,7},{4,0},{5,1},{6,2},{7,3},{8,12},{9,13},{10,... | collective-permute-start | bytes 983048 | tf_op jit(solution)/shard_map/ppermute | solution.py:376
  153.8 23.8 %collective-permute-start.21 = (bf16[128,2304]{1,0:T(8,128)(2,1)S(1)}, bf16[128,2304]{1,0:T(8,128)(2,1)S(1)}, u32[]{:S(2)}, u32[]{:S(2)}) collective-permute-start(bf16[128,2304]{1,0:T(8,128)(2,1)S(1)} %get-tuple-element.58.refs_9_), channel_id=1, source_target_pairs={{0,1},{1,0},{2,3},{3,2},{4,5},{5,4},{6,7},{7,6},{8,9},{9,8},{10,11... | collective-permute-start | bytes 1769480 | tf_op jit(solution)/shard_map/ppermute | solution.py:376
  155.2 24.1 %collective-permute-start.27 = (bf16[128,2560]{1,0:T(8,128)(2,1)S(1)}, bf16[128,2560]{1,0:T(8,128)(2,1)S(1)}, u32[]{:S(2)}, u32[]{:S(2)}) collective-permute-start(bf16[128,2560]{1,0:T(8,128)(2,1)S(1)} %get-tuple-element.60.refs_11_), channel_id=1, source_target_pairs={{0,2},{1,3},{2,0},{3,1},{4,6},{5,7},{6,4},{7,5},{8,10},{9,11},{10,... | collective-permute-start | bytes 1966088 | tf_op jit(solution)/shard_map/ppermute | solution.py:376
  176.4 3.2 %collective-permute-start.25 = (bf16[256,1536]{1,0:T(8,128)(2,1)S(1)}, bf16[256,1536]{1,0:T(8,128)(2,1)S(1)}, u32[]{:S(2)}, u32[]{:S(2)}) collective-permute-start(bf16[256,1536]{1,0:T(8,128)(2,1)S(1)} %get-tuple-element.65), channel_id=1, source_target_pairs={{0,16},{16,0},{1,17},{17,1},{2,18},{18,2},{3,19},{19,3},{4,20},{20... | collective-permute-start | bytes 2359304 | tf_op jit(solution)/shard_map/ppermute | solution.py:384
  176.5 3.4 %collective-permute-start.24 = (bf16[256,1536]{1,0:T(8,128)(2,1)S(1)}, bf16[256,1536]{1,0:T(8,128)(2,1)S(1)}, u32[]{:S(2)}, u32[]{:S(2)}) collective-permute-start(bf16[256,1536]{1,0:T(8,128)(2,1)S(1)} %get-tuple-element.63), channel_id=1, source_target_pairs={{0,16},{16,0},{1,17},{17,1},{2,18},{18,2},{3,19},{19,3},{4,20},{20... | collective-permute-start | bytes 2359304 | tf_op jit(solution)/shard_map/ppermute | solution.py:384
  177.1 6.2 %collective-permute-start.30 = (bf16[64,1280]{1,0:T(8,128)(2,1)S(1)}, bf16[64,1280]{1,0:T(8,128)(2,1)S(1)}, u32[]{:S(2)}, u32[]{:S(2)}) collective-permute-start(bf16[64,1280]{1,0:T(8,128)(2,1)S(1)} %slice.161), channel_id=1, source_target_pairs={{0,2},{1,3},{2,0},{3,1},{4,6},{5,7},{6,4},{7,5},{8,10},{9,11},{10,... | collective-permute-start | bytes 491528 | tf_op jit(solution)/shard_map/ppermute | solution.py:376
  177.7 8.8 %collective-permute-start.23 = (bf16[64,2304]{1,0:T(8,128)(2,1)S(1)}, bf16[64,2304]{1,0:T(8,128)(2,1)S(1)}, u32[]{:S(2)}, u32[]{:S(2)}) collective-permute-start(bf16[64,2304]{1,0:T(8,128)(2,1)S(1)} %slice.155), channel_id=1, source_target_pairs={{0,4},{1,5},{2,6},{3,7},{4,0},{5,1},{6,2},{7,3},{8,12},{9,13},{10,... | collective-permute-start | bytes 884744 | tf_op jit(solution)/shard_map/ppermute | solution.py:376
  179.5 10.1 %collective-permute-start.28 = (bf16[64,2560]{1,0:T(8,128)(2,1)S(1)}, bf16[64,2560]{1,0:T(8,128)(2,1)S(1)}, u32[]{:S(2)}, u32[]{:S(2)}) collective-permute-start(bf16[64,2560]{1,0:T(8,128)(2,1)S(1)} %slice.159), channel_id=1, source_target_pairs={{0,1},{1,0},{2,3},{3,2},{4,5},{5,4},{6,7},{7,6},{8,9},{9,8},{10,11... | collective-permute-start | bytes 983048 | tf_op jit(solution)/shard_map/ppermute | solution.py:376
  183.4 32.6 %collective-permute-start.32 = (bf16[32,1280]{1,0:T(8,128)(2,1)S(1)}, bf16[32,1280]{1,0:T(8,128)(2,1)S(1)}, u32[]{:S(2)}, u32[]{:S(2)}) collective-permute-start(bf16[32,1280]{1,0:T(8,128)(2,1)S(1)} %slice.165), channel_id=1, source_target_pairs={{0,1},{1,0},{2,3},{3,2},{4,5},{5,4},{6,7},{7,6},{8,9},{9,8},{10,11... | collective-permute-start | bytes 245768 | tf_op jit(solution)/shard_map/ppermute | solution.py:376
  186.6 30.2 %collective-permute-start.26 = (bf16[32,2304]{1,0:T(8,128)(2,1)S(1)}, bf16[32,2304]{1,0:T(8,128)(2,1)S(1)}, u32[]{:S(2)}, u32[]{:S(2)}) collective-permute-start(bf16[32,2304]{1,0:T(8,128)(2,1)S(1)} %slice.157), channel_id=1, source_target_pairs={{0,2},{1,3},{2,0},{3,1},{4,6},{5,7},{6,4},{7,5},{8,10},{9,11},{10,... | collective-permute-start | bytes 442376 | tf_op jit(solution)/shard_map/ppermute | solution.py:376
  189.7 14.9 %slice-start = ((s8[6291456]{0:T(1024)(128)(4,1)}), s8[4194304]{0:T(1024)(128)(4,1)S(1)}, s32[]{:S(2)}) async-start(s8[6291456]{0:T(1024)(128)(4,1)} %bitcast.8), calls=%async_computation | async-start | bytes 8388608
  189.7 14.8 %slice-start.1 = ((s8[6291456]{0:T(1024)(128)(4,1)}), s8[2097152]{0:T(1024)(128)(4,1)S(1)}, s32[]{:S(2)}) async-start(s8[6291456]{0:T(1024)(128)(4,1)} %bitcast.8), calls=%async_computation.1 | async-start | bytes 4194304
  202.0 27.6 %collective-permute-start.36 = (bf16[128,1280]{1,0:T(8,128)(2,1)S(1)}, bf16[128,1280]{1,0:T(8,128)(2,1)S(1)}, u32[]{:S(2)}, u32[]{:S(2)}) collective-permute-start(bf16[128,1280]{1,0:T(8,128)(2,1)S(1)} %get-tuple-element.78.refs_9_), channel_id=1, source_target_pairs={{0,4},{1,5},{2,6},{3,7},{4,0},{5,1},{6,2},{7,3},{8,12},{9,13},{10,... | collective-permute-start | bytes 983048 | tf_op jit(solution)/shard_map/ppermute | solution.py:376
  202.5 27.1 %collective-permute-start.34 = (bf16[128,2304]{1,0:T(8,128)(2,1)S(1)}, bf16[128,2304]{1,0:T(8,128)(2,1)S(1)}, u32[]{:S(2)}, u32[]{:S(2)}) collective-permute-start(bf16[128,2304]{1,0:T(8,128)(2,1)S(1)} %get-tuple-element.74.refs_5_), channel_id=1, source_target_pairs={{0,1},{1,0},{2,3},{3,2},{4,5},{5,4},{6,7},{7,6},{8,9},{9,8},{10,11... | collective-permute-start | bytes 1769480 | tf_op jit(solution)/shard_map/ppermute | solution.py:376
  203.0 26.7 %collective-permute-start.35 = (bf16[128,2560]{1,0:T(8,128)(2,1)S(1)}, bf16[128,2560]{1,0:T(8,128)(2,1)S(1)}, u32[]{:S(2)}, u32[]{:S(2)}) collective-permute-start(bf16[128,2560]{1,0:T(8,128)(2,1)S(1)} %get-tuple-element.76.refs_7_), channel_id=1, source_target_pairs={{0,2},{1,3},{2,0},{3,1},{4,6},{5,7},{6,4},{7,5},{8,10},{9,11},{10,... | collective-permute-start | bytes 1966088 | tf_op jit(solution)/shard_map/ppermute | solution.py:376
  216.0 5.3 %collective-permute-start.31 = (bf16[32,2560]{1,0:T(8,128)(2,1)S(1)}, bf16[32,2560]{1,0:T(8,128)(2,1)S(1)}, u32[]{:S(2)}, u32[]{:S(2)}) collective-permute-start(bf16[32,2560]{1,0:T(8,128)(2,1)S(1)} %slice.163), channel_id=1, source_target_pairs={{0,4},{1,5},{2,6},{3,7},{4,0},{5,1},{6,2},{7,3},{8,12},{9,13},{10,... | collective-permute-start | bytes 491528 | tf_op jit(solution)/shard_map/ppermute | solution.py:376
  230.0 14.2 %collective-permute-start.39 = (bf16[64,1280]{1,0:T(8,128)(2,1)S(1)}, bf16[64,1280]{1,0:T(8,128)(2,1)S(1)}, u32[]{:S(2)}, u32[]{:S(2)}) collective-permute-start(bf16[64,1280]{1,0:T(8,128)(2,1)S(1)} %slice.143), channel_id=1, source_target_pairs={{0,2},{1,3},{2,0},{3,1},{4,6},{5,7},{6,4},{7,5},{8,10},{9,11},{10,... | collective-permute-start | bytes 491528 | tf_op jit(solution)/shard_map/ppermute | solution.py:376
  230.6 14.2 %collective-permute-start.33 = (bf16[16,6144]{1,0:T(8,128)(2,1)S(1)}, bf16[16,6144]{1,0:T(8,128)(2,1)S(1)}, u32[]{:S(2)}, u32[]{:S(2)}) collective-permute-start(bf16[16,6144]{1,0:T(8,128)(2,1)S(1)} %slice.167), channel_id=1, source_target_pairs={{0,8},{1,9},{2,10},{3,11},{4,12},{5,13},{6,14},{7,15},{8,0},{9,1},... | collective-permute-start | bytes 589832 | tf_op jit(solution)/shard_map/ppermute | solution.py:376
  232.4 11.8 %collective-permute-start.37 = (bf16[64,2304]{1,0:T(8,128)(2,1)S(1)}, bf16[64,2304]{1,0:T(8,128)(2,1)S(1)}, u32[]{:S(2)}, u32[]{:S(2)}) collective-permute-start(bf16[64,2304]{1,0:T(8,128)(2,1)S(1)} %slice.139), channel_id=1, source_target_pairs={{0,4},{1,5},{2,6},{3,7},{4,0},{5,1},{6,2},{7,3},{8,12},{9,13},{10,... | collective-permute-start | bytes 884744 | tf_op jit(solution)/shard_map/ppermute | solution.py:376
  234.0 10.3 %collective-permute-start.38 = (bf16[64,2560]{1,0:T(8,128)(2,1)S(1)}, bf16[64,2560]{1,0:T(8,128)(2,1)S(1)}, u32[]{:S(2)}, u32[]{:S(2)}) collective-permute-start(bf16[64,2560]{1,0:T(8,128)(2,1)S(1)} %slice.141), channel_id=1, source_target_pairs={{0,1},{1,0},{2,3},{3,2},{4,5},{5,4},{6,7},{7,6},{8,9},{9,8},{10,11... | collective-permute-start | bytes 983048 | tf_op jit(solution)/shard_map/ppermute | solution.py:376
  244.4 4.5 %collective-permute-start.42 = (bf16[32,1280]{1,0:T(8,128)(2,1)S(1)}, bf16[32,1280]{1,0:T(8,128)(2,1)S(1)}, u32[]{:S(2)}, u32[]{:S(2)}) collective-permute-start(bf16[32,1280]{1,0:T(8,128)(2,1)S(1)} %slice.149), channel_id=1, source_target_pairs={{0,1},{1,0},{2,3},{3,2},{4,5},{5,4},{6,7},{7,6},{8,9},{9,8},{10,11... | collective-permute-start | bytes 245768 | tf_op jit(solution)/shard_map/ppermute | solution.py:376
  244.8 5.2 %collective-permute-start.40 = (bf16[32,2304]{1,0:T(8,128)(2,1)S(1)}, bf16[32,2304]{1,0:T(8,128)(2,1)S(1)}, u32[]{:S(2)}, u32[]{:S(2)}) collective-permute-start(bf16[32,2304]{1,0:T(8,128)(2,1)S(1)} %slice.145), channel_id=1, source_target_pairs={{0,2},{1,3},{2,0},{3,1},{4,6},{5,7},{6,4},{7,5},{8,10},{9,11},{10,... | collective-permute-start | bytes 442376 | tf_op jit(solution)/shard_map/ppermute | solution.py:376
  245.4 6.0 %collective-permute-start.41 = (bf16[32,2560]{1,0:T(8,128)(2,1)S(1)}, bf16[32,2560]{1,0:T(8,128)(2,1)S(1)}, u32[]{:S(2)}, u32[]{:S(2)}) collective-permute-start(bf16[32,2560]{1,0:T(8,128)(2,1)S(1)} %slice.147), channel_id=1, source_target_pairs={{0,4},{1,5},{2,6},{3,7},{4,0},{5,1},{6,2},{7,3},{8,12},{9,13},{10,... | collective-permute-start | bytes 491528 | tf_op jit(solution)/shard_map/ppermute | solution.py:376
  251.5 9.9 %collective-permute-start.43 = (bf16[16,6144]{1,0:T(8,128)(2,1)S(1)}, bf16[16,6144]{1,0:T(8,128)(2,1)S(1)}, u32[]{:S(2)}, u32[]{:S(2)}) collective-permute-start(bf16[16,6144]{1,0:T(8,128)(2,1)S(1)} %slice.169), channel_id=1, source_target_pairs={{0,8},{1,9},{2,10},{3,11},{4,12},{5,13},{6,14},{7,15},{8,0},{9,1},... | collective-permute-start | bytes 589832 | tf_op jit(solution)/shard_map/ppermute | solution.py:376
  (1 other events, 2.8 us)

commit v3 on v2

--- a/solution.py
+++ b/solution.py
@@ -10,7 +10,7 @@
 half_root = 0.7071067811865476
 inv_root_tau = 0.3989422804014327
 GROUPS = 2
-SPLIT = (18, 20)
+SPLIT = (18, 18)
 OUT_OF = 48
 
 
@@ -463,14 +463,13 @@
         del work[:count]
 
     held = totals[last]
-    advance(1, [half for pair in held for half in pair])
-    late = [stage(pairs, stages - 1, outs[0], len(orders)) for pairs in early]
-    advance(1, [total for summed in late for total in summed])
-    shares = [finish(summed, outs[1]) for summed in late]
+    advance(2, [half for pair in held for half in pair])
+    late = [stage(pairs, stages - 1, outs[1], len(orders)) for pairs in early]
     for at in range(stages):
         summed = stage(held, at, outs[1 - at] if at < 2 else None, 2)
         if at == 0:
             advance(1, summed)
+            shares = [finish(done, outs[0]) for done in late]
         if at < stages - 1:
             summed = lax.optimization_barrier(summed)
         held = [halves(total) for total in summed]

time: 262 us -> 262 us (level)
  starting transfers between devices: 51.2 us -> 42.2 us
  waiting for transfers between devices: 100 us -> 107 us
  local copies, waits for them, and re-layouts: 4.47 us -> 8.12 us
    ppermute x40, starting transfers between devices: 50.1 us -> 41 us  [swap(): return lax.ppermute(value, 'col', [(i, i ^ 1 << bit) for i in range(n)])]
    unnamed x11 -> x15, local copies, waits for them, and re-layouts: 2.89 us -> 6.55 us
    ppermute x40, waiting for transfers between devices: 99.3 us -> 103 us  [swap(): return lax.ppermute(value, 'col', [(i, i ^ 1 << bit) for i in range(n)])]
    ppermute x4, waiting for transfers between devices: 1.18 us -> 4.33 us  [beside(): lax.ppermute(part.astype(jnp.bfloat16), 'row', pairs)]
  transfers between devices with their start and end apart: 44 -> 44, of which waited for: 22 -> 25; matrix products, arithmetic and copies ran while one was open for 2% -> 2% of each run, Pallas kernels for 37% -> 36%
where the time goes in v3:
time: 262 us
  waiting for transfers between devices  107 us (41%)
  Pallas kernels  95.4 us (36%)
  starting transfers between devices  42.2 us (16%)
  other arithmetic  8.21 us (3%)
  local copies, waits for them, and re-layouts  8.12 us (3%)
    ppermute x40, waiting for transfers between devices, swap(): return lax.ppermute(value, 'col', [(i, i ^ 1 << bit) for i in range(n)])  103 us
    ppermute x40, starting transfers between devices, swap(): return lax.ppermute(value, 'col', [(i, i ^ 1 << bit) for i in range(n)])  41 us
    pallas_call x2, Pallas kernels, forward(): pl.pallas_call(functools.partial(forward_kernel, moves, block), in_specs=...  39.8 us
    pallas_call x4, Pallas kernels, call(): pl.pallas_call(functools.partial(grad_kernel, block, factor, (off[0] * ti...  33.3 us
    pallas_call x2, Pallas kernels, backward(): pl.pallas_call(functools.partial(backward_kernel, parts, block), in_specs...  22.3 us
    unnamed x15, local copies, waits for them, and re-layouts  6.55 us
  transfers between devices with their start and end apart: 44, of which 25 were waited for; matrix products, arithmetic and copies ran while one was open for 2% of the time, Pallas kernels for 36%

profile of v3, /device:TPU:0, one launch (start us, length us, event | category | flops | bytes accessed | tf_op | source)
XLA Modules:
  0.0 262.2 jit_solution(9337134161291668941)
XLA Ops:
  0.6 1.3 slice_bitcast_fusion.2
  2.0 4.1 %collective-permute-start = (bf16[2,16,6144]{2,1,0:T(8,128)(2,1)S(1)}, bf16[2,16,6144]{2,1,0:T(8,128)(2,1)S(1)}, u32[]{:S(2)}, u32[]{:S(2)}) collective-permute-start(bf16[2,16,6144]{2,1,0:T(8,128)(2,1)S(1)} %pad_maximum_fusion.12), channel_id=1, source_target_pairs={{0,8},{1,9},{2,10},{3,11},{4,12},{5,13},{6,14},{7,15},{8,0},{9,1},... | collective-permute-start | bytes 1179656 | tf_op jit(solution)/shard_map/ppermute | solution.py:376
  6.1 17.5 %collective-permute-done = bf16[2,16,6144]{2,1,0:T(8,128)(2,1)S(1)} collective-permute-done((bf16[2,16,6144]{2,1,0:T(8,128)(2,1)S(1)}, bf16[2,16,6144]{2,1,0:T(8,128)(2,1)S(1)}, u32[]{:S(2)}, u32[]{:S(2)}) %collective-permute-start) | collective-permute-done | bytes 393248 | tf_op jit(solution)/shard_map/ppermute | solution.py:376
  23.7 1.6 collective-permute-start.1
  25.4 1.6 collective-permute-start.4
  27.7 3.4 %collective-permute-done.4 = bf16[2,32,1536]{2,1,0:T(8,128)(2,1)S(1)} collective-permute-done((bf16[2,32,1536]{2,1,0:T(8,128)(2,1)S(1)}, bf16[2,32,1536]{2,1,0:T(8,128)(2,1)S(1)}, u32[]{:S(2)}, u32[]{:S(2)}) %collective-permute-start.4) | collective-permute-done | bytes 196640 | tf_op jit(solution)/shard_map/ppermute | solution.py:376
  32.3 2.1 collective-permute-done.3
  34.4 3.4 %collective-permute-start.5 = (bf16[2,16,6144]{2,1,0:T(8,128)(2,1)S(1)}, bf16[2,16,6144]{2,1,0:T(8,128)(2,1)S(1)}, u32[]{:S(2)}, u32[]{:S(2)}) collective-permute-start(bf16[2,16,6144]{2,1,0:T(8,128)(2,1)S(1)} %pad_maximum_fusion.13), channel_id=1, source_target_pairs={{0,8},{1,9},{2,10},{3,11},{4,12},{5,13},{6,14},{7,15},{8,0},{9,1},... | collective-permute-start | bytes 1179656 | tf_op jit(solution)/shard_map/ppermute | solution.py:376
  37.8 1.7 collective-permute-start.2
  40.4 14.0 %collective-permute-done.5 = bf16[2,16,6144]{2,1,0:T(8,128)(2,1)S(1)} collective-permute-done((bf16[2,16,6144]{2,1,0:T(8,128)(2,1)S(1)}, bf16[2,16,6144]{2,1,0:T(8,128)(2,1)S(1)}, u32[]{:S(2)}, u32[]{:S(2)}) %collective-permute-start.5) | collective-permute-done | bytes 393248 | tf_op jit(solution)/shard_map/ppermute | solution.py:376
  54.5 4.5 %collective-permute-done.2 = bf16[2,64,2304]{2,1,0:T(8,128)(2,1)S(1)} collective-permute-done((bf16[2,64,2304]{2,1,0:T(8,128)(2,1)S(1)}, bf16[2,64,2304]{2,1,0:T(8,128)(2,1)S(1)}, u32[]{:S(2)}, u32[]{:S(2)}) %collective-permute-start.2) | collective-permute-done | bytes 589856 | tf_op jit(solution)/shard_map/ppermute | solution.py:376
  61.5 1.3 collective-permute-start.10
  62.8 3.2 %collective-permute-done.12 = bf16[2,32,1536]{2,1,0:T(8,128)(2,1)S(1)} collective-permute-done((bf16[2,32,1536]{2,1,0:T(8,128)(2,1)S(1)}, bf16[2,32,1536]{2,1,0:T(8,128)(2,1)S(1)}, u32[]{:S(2)}, u32[]{:S(2)}) %collective-permute-start.12) | collective-permute-done | bytes 196640 | tf_op jit(solution)/shard_map/ppermute | solution.py:376
  66.6 3.7 %collective-permute-done.8 = bf16[2,32,2304]{2,1,0:T(8,128)(2,1)S(1)} collective-permute-done((bf16[2,32,2304]{2,1,0:T(8,128)(2,1)S(1)}, bf16[2,32,2304]{2,1,0:T(8,128)(2,1)S(1)}, u32[]{:S(2)}, u32[]{:S(2)}) %collective-permute-start.8) | collective-permute-done | bytes 294944 | tf_op jit(solution)/shard_map/ppermute | solution.py:376
  71.3 2.5 collective-permute-start.11
  73.8 2.3 collective-permute-done.13
  76.2 4.6 %collective-permute-done.9 = bf16[2,64,2304]{2,1,0:T(8,128)(2,1)S(1)} collective-permute-done((bf16[2,64,2304]{2,1,0:T(8,128)(2,1)S(1)}, bf16[2,64,2304]{2,1,0:T(8,128)(2,1)S(1)}, u32[]{:S(2)}, u32[]{:S(2)}) %collective-permute-start.9) | collective-permute-done | bytes 589856 | tf_op jit(solution)/shard_map/ppermute | solution.py:376
  80.8 1.1 pad_maximum_fusion.2.refs_8_.refs_0_
  82.0 2.0 collective-permute-done.11
  85.0 2.5 collective-permute-start.14
  87.9 1.8 collective-permute-start.19
  89.9 10.0 %collective-permute-done.16.refs_5_ = bf16[2,128,1536]{2,1,0:T(8,128)(2,1)} collective-permute-done((bf16[2,128,1536]{2,1,0:T(8,128)(2,1)S(1)}, bf16[2,128,1536]{2,1,0:T(8,128)(2,1)}, u32[]{:S(2)}, u32[]{:S(2)}) %collective-permute-start.16) | collective-permute-done | bytes 786464 | tf_op jit(solution)/shard_map/ppermute | solution.py:376
  99.8 14.7 %collective-permute-done.14.refs_1_ = bf16[2,128,2304]{2,1,0:T(8,128)(2,1)} collective-permute-done((bf16[2,128,2304]{2,1,0:T(8,128)(2,1)S(1)}, bf16[2,128,2304]{2,1,0:T(8,128)(2,1)}, u32[]{:S(2)}, u32[]{:S(2)}) %collective-permute-start.14) | collective-permute-done | bytes 1179680 | tf_op jit(solution)/shard_map/ppermute | solution.py:376
  114.5 2.2 collective-permute-done.15.refs_3_
  116.7 19.9 %forward.2 = (bf16[2,256,6144]{2,1,0:T(8,128)(2,1)}, bf16[256,1536]{1,0:T(8,128)(2,1)S(1)}, bf16[256,1536]{1,0:T(8,128)(2,1)S(1)}) custom-call(s32[48,12]{1,0:T(8,128)S(1)} %copy.12.up_on.pattern, s32[12,48]{1,0:T(8,128)S(1)} %copy-done.2, bf16[2,128,2304]{2,1,0:T(8,128)(2,1)S(1)} %pad_maximum_fusion.refs_0_, ...), custom_call_target="tpu_custom_call" | custom-call | flops 1572864 | bytes 1572864 | tf_op jit(solution)/shard_map/forward/pallas_call | solution.py:174
  137.4 1.6 collective-permute-done.20
  139.0 1.1 collective-permute-done.17
  141.2 10.9 %backward.2 = (bf16[128,2304]{1,0:T(8,128)(2,1)S(1)}, bf16[128,2304]{1,0:T(8,128)(2,1)S(1)}, bf16[128,2304]{1,0:T(8,128)(2,1)S(1)}, bf16[128,2304]{1,0:T(8,128)(...) custom-call(s32[48,12]{1,0:T(8,128)S(1)} %copy.12.up_on.pattern, ...), custom_call_target="tpu_custom_call" | custom-call | flops 1572864 | bytes 1572864 | tf_op jit(solution)/shard_map/backward/pallas_call | solution.py:250
  152.5 5.1 %collective-permute-done.22.refs_5_ = bf16[2,128,1536]{2,1,0:T(8,128)(2,1)S(1)} collective-permute-done((bf16[2,128,1536]{2,1,0:T(8,128)(2,1)S(1)}, bf16[2,128,1536]{2,1,0:T(8,128)(2,1)S(1)}, u32[]{:S(2)}, u32[]{:S(2)}) %collective-permute-start.22) | collective-permute-done | bytes 786464 | tf_op jit(solution)/shard_map/ppermute | solution.py:376
  158.5 19.9 %forward.3 = (bf16[2,256,6144]{2,1,0:T(8,128)(2,1)}, bf16[256,1536]{1,0:T(8,128)(2,1)S(1)}, bf16[256,1536]{1,0:T(8,128)(2,1)S(1)}) custom-call(s32[48,12]{1,0:T(8,128)S(1)} %copy.12.up_on.pattern, s32[12,48]{1,0:T(8,128)S(1)} %copy-done.2, bf16[2,128,2304]{2,1,0:T(8,128)(2,1)} %pad_maximum_fusion.2.refs_8_.refs_0_, ...), custom_call_target="tpu_custom_call" | custom-call | flops 1572864 | bytes 1572864 | tf_op jit(solution)/shard_map/forward/pallas_call | solution.py:174
  180.8 1.1 collective-permute-done.24
  182.9 3.1 %collective-permute-done.30 = bf16[64,1536]{1,0:T(8,128)(2,1)S(1)} collective-permute-done((bf16[64,1536]{1,0:T(8,128)(2,1)S(1)}, bf16[64,1536]{1,0:T(8,128)(2,1)S(1)}, u32[]{:S(2)}, u32[]{:S(2)}) %collective-permute-start.30) | collective-permute-done | bytes 196640 | tf_op jit(solution)/shard_map/ppermute | solution.py:376
  186.2 2.2 collective-permute-done.23
  189.4 11.4 %backward.3 = (bf16[128,2304]{1,0:T(8,128)(2,1)S(1)}, bf16[128,2304]{1,0:T(8,128)(2,1)S(1)}, bf16[128,2304]{1,0:T(8,128)(2,1)S(1)}, bf16[128,2304]{1,0:T(8,128)(...) custom-call(s32[48,12]{1,0:T(8,128)S(1)} %copy.12.up_on.pattern, ...), custom_call_target="tpu_custom_call" | custom-call | flops 1572864 | bytes 1572864 | tf_op jit(solution)/shard_map/backward/pallas_call | solution.py:250
  201.2 2.2 collective-permute-start.35
  203.3 1.7 collective-permute-start.36
  205.1 2.8 %copy-done = bf16[2,256,6144]{2,1,0:T(8,128)(2,1)S(1)} copy-done((bf16[2,256,6144]{2,1,0:T(8,128)(2,1)S(1)}, bf16[2,256,6144]{2,1,0:T(8,128)(2,1)}, u32[]{:S(2)}) %copy-start) | copy-done | bytes 6291480
  207.8 8.1 %grad.4.refs_7_ = bf16[1536,6144]{1,0:T(8,128)(2,1)} custom-call(s32[12,48]{1,0:T(8,128)S(1)} %copy-done.2, bf16[256,1536]{1,0:T(8,128)(2,1)S(1)} %get-tuple-element.95.refs_0_, bf16[256,1536]{1,0:T(8,128)(2,1)S(1)} %get-tuple-element.93.refs_1_, bf16[2,256,6144]{2,1,0:T(8,128)(2,1)S(1)} %bitcast.9, bf16[2,256,6144]{2,1,0:T(8,128)(2,1)S(1)} %copy-done, ...), custom_call_target="tpu_custom_call" | custom-call | flops 4718592 | bytes 1572864 | tf_op jit(solution)/shard_map/grad/pallas_call | solution.py:323
  216.4 2.8 %copy-done.1 = bf16[2,256,6144]{2,1,0:T(8,128)(2,1)S(1)} copy-done((bf16[2,256,6144]{2,1,0:T(8,128)(2,1)S(1)}, bf16[2,256,6144]{2,1,0:T(8,128)(2,1)}, u32[]{:S(2)}) %copy-start.1) | copy-done | bytes 6291480
  219.2 8.7 %grad.5.refs_7_ = bf16[6144,1536]{1,0:T(8,128)(2,1)} custom-call(s32[48,12]{1,0:T(8,128)S(1)} %copy.12.up_on.pattern, bf16[2,256,6144]{2,1,0:T(8,128)(2,1)S(1)} %bitcast.9, bf16[2,256,6144]{2,1,0:T(8,128)(2,1)S(1)} %copy-done.1, bf16[256,1536]{1,0:T(8,128)(2,1)S(1)} %get-tuple-element.96.dhid_ref.refs_2_, ...), custom_call_target="tpu_custom_call" | custom-call | flops 4718592 | bytes 393216 | tf_op jit(solution)/shard_map/grad/pallas_call | solution.py:323
  228.4 2.1 collective-permute-start.39
  230.5 1.9 collective-permute-start.33
  232.4 2.0 collective-permute-start.37
  234.4 1.8 collective-permute-start.38
  236.2 8.4 %grad.6 = bf16[6144,1536]{1,0:T(8,128)(2,1)} custom-call(s32[48,12]{1,0:T(8,128)S(1)} %copy.12.up_on.pattern, bf16[2,256,6144]{2,1,0:T(8,128)(2,1)S(1)} %bitcast.9, bf16[2,256,6144]{2,1,0:T(8,128)(2,1)S(1)} %copy-done.1, bf16[256,1536]{1,0:T(8,128)(2,1)S(1)} %get-tuple-element.96.dhid_ref.refs_2_, ...), custom_call_target="tpu_custom_call", output_to_operand_aliasing={{}: (8, {})} | custom-call | flops 4718592 | bytes 393216 | tf_op jit(solution)/shard_map/grad/pallas_call | solution.py:323
  245.5 4.0 %collective-permute-done.42 = bf16[32,1536]{1,0:T(8,128)(2,1)S(1)} collective-permute-done((bf16[32,1536]{1,0:T(8,128)(2,1)S(1)}, bf16[32,1536]{1,0:T(8,128)(2,1)S(1)}, u32[]{:S(2)}, u32[]{:S(2)}) %collective-permute-start.42) | collective-permute-done | bytes 98336 | tf_op jit(solution)/shard_map/ppermute | solution.py:376
  249.6 2.5 collective-permute-done.41
  253.2 8.1 %grad.7 = bf16[1536,6144]{1,0:T(8,128)(2,1)} custom-call(s32[12,48]{1,0:T(8,128)S(1)} %copy-done.2, bf16[256,1536]{1,0:T(8,128)(2,1)S(1)} %get-tuple-element.95.refs_0_, bf16[256,1536]{1,0:T(8,128)(2,1)S(1)} %get-tuple-element.93.refs_1_, bf16[2,256,6144]{2,1,0:T(8,128)(2,1)S(1)} %bitcast.9, ...), custom_call_target="tpu_custom_call", output_to_operand_aliasing={{}: (8, {})} | custom-call | flops 4718592 | bytes 1572864 | tf_op jit(solution)/shard_map/grad/pallas_call | solution.py:323
  (124 shorter events, 20.5 us)
Async XLA Ops:
  2.0 21.6 %collective-permute-start = (bf16[2,16,6144]{2,1,0:T(8,128)(2,1)S(1)}, bf16[2,16,6144]{2,1,0:T(8,128)(2,1)S(1)}, u32[]{:S(2)}, u32[]{:S(2)}) collective-permute-start(bf16[2,16,6144]{2,1,0:T(8,128)(2,1)S(1)} %pad_maximum_fusion.12), channel_id=1, source_target_pairs={{0,8},{1,9},{2,10},{3,11},{4,12},{5,13},{6,14},{7,15},{8,0},{9,1},... | collective-permute-start | bytes 1179656 | tf_op jit(solution)/shard_map/ppermute | solution.py:376
  23.7 8.5 %collective-permute-start.1 = (bf16[2,32,2304]{2,1,0:T(8,128)(2,1)S(1)}, bf16[2,32,2304]{2,1,0:T(8,128)(2,1)S(1)}, u32[]{:S(2)}, u32[]{:S(2)}) collective-permute-start(bf16[2,32,2304]{2,1,0:T(8,128)(2,1)S(1)} %get-tuple-element.100), channel_id=1, source_target_pairs={{0,2},{1,3},{2,0},{3,1},{4,6},{5,7},{6,4},{7,5},{8,10},{9,11},{10,... | collective-permute-start | bytes 884744 | tf_op jit(solution)/shard_map/ppermute | solution.py:376
  25.4 5.7 %collective-permute-start.4 = (bf16[2,32,1536]{2,1,0:T(8,128)(2,1)S(1)}, bf16[2,32,1536]{2,1,0:T(8,128)(2,1)S(1)}, u32[]{:S(2)}, u32[]{:S(2)}) collective-permute-start(bf16[2,32,1536]{2,1,0:T(8,128)(2,1)S(1)} %pad_maximum_fusion.19), channel_id=1, source_target_pairs={{0,1},{1,0},{2,3},{3,2},{4,5},{5,4},{6,7},{7,6},{8,9},{9,8},{10,11... | collective-permute-start | bytes 589832 | tf_op jit(solution)/shard_map/ppermute | solution.py:376
  26.9 7.4 %collective-permute-start.3 = (bf16[2,32,2304]{2,1,0:T(8,128)(2,1)S(1)}, bf16[2,32,2304]{2,1,0:T(8,128)(2,1)S(1)}, u32[]{:S(2)}, u32[]{:S(2)}) collective-permute-start(bf16[2,32,2304]{2,1,0:T(8,128)(2,1)S(1)} %get-tuple-element.99), channel_id=1, source_target_pairs={{0,4},{1,5},{2,6},{3,7},{4,0},{5,1},{6,2},{7,3},{8,12},{9,13},{10,... | collective-permute-start | bytes 884744 | tf_op jit(solution)/shard_map/ppermute | solution.py:376
  31.1 9.3 %collective-permute-start.7 = (bf16[2,64,1536]{2,1,0:T(8,128)(2,1)S(1)}, bf16[2,64,1536]{2,1,0:T(8,128)(2,1)S(1)}, u32[]{:S(2)}, u32[]{:S(2)}) collective-permute-start(bf16[2,64,1536]{2,1,0:T(8,128)(2,1)S(1)} %pad_maximum_fusion.14), channel_id=1, source_target_pairs={{0,2},{1,3},{2,0},{3,1},{4,6},{5,7},{6,4},{7,5},{8,10},{9,11},{10,... | collective-permute-start | bytes 1179656 | tf_op jit(solution)/shard_map/ppermute | solution.py:376
  34.4 20.1 %collective-permute-start.5 = (bf16[2,16,6144]{2,1,0:T(8,128)(2,1)S(1)}, bf16[2,16,6144]{2,1,0:T(8,128)(2,1)S(1)}, u32[]{:S(2)}, u32[]{:S(2)}) collective-permute-start(bf16[2,16,6144]{2,1,0:T(8,128)(2,1)S(1)} %pad_maximum_fusion.13), channel_id=1, source_target_pairs={{0,8},{1,9},{2,10},{3,11},{4,12},{5,13},{6,14},{7,15},{8,0},{9,1},... | collective-permute-start | bytes 1179656 | tf_op jit(solution)/shard_map/ppermute | solution.py:376
  37.8 21.3 %collective-permute-start.2 = (bf16[2,64,2304]{2,1,0:T(8,128)(2,1)S(1)}, bf16[2,64,2304]{2,1,0:T(8,128)(2,1)S(1)}, u32[]{:S(2)}, u32[]{:S(2)}) collective-permute-start(bf16[2,64,2304]{2,1,0:T(8,128)(2,1)S(1)} %pad_maximum_fusion.8), channel_id=1, source_target_pairs={{0,4},{1,5},{2,6},{3,7},{4,0},{5,1},{6,2},{7,3},{8,12},{9,13},{10,... | collective-permute-start | bytes 1769480 | tf_op jit(solution)/shard_map/ppermute | solution.py:376
  39.5 19.6 %collective-permute-start.6 = (bf16[2,64,2304]{2,1,0:T(8,128)(2,1)S(1)}, bf16[2,64,2304]{2,1,0:T(8,128)(2,1)S(1)}, u32[]{:S(2)}, u32[]{:S(2)}) collective-permute-start(bf16[2,64,2304]{2,1,0:T(8,128)(2,1)S(1)} %pad_maximum_fusion.9), channel_id=1, source_target_pairs={{0,1},{1,0},{2,3},{3,2},{4,5},{5,4},{6,7},{7,6},{8,9},{9,8},{10,11... | collective-permute-start | bytes 1769480 | tf_op jit(solution)/shard_map/ppermute | solution.py:376
  60.3 5.7 %collective-permute-start.12 = (bf16[2,32,1536]{2,1,0:T(8,128)(2,1)S(1)}, bf16[2,32,1536]{2,1,0:T(8,128)(2,1)S(1)}, u32[]{:S(2)}, u32[]{:S(2)}) collective-permute-start(bf16[2,32,1536]{2,1,0:T(8,128)(2,1)S(1)} %slice.123), channel_id=1, source_target_pairs={{0,1},{1,0},{2,3},{3,2},{4,5},{5,4},{6,7},{7,6},{8,9},{9,8},{10,11... | collective-permute-start | bytes 589832 | tf_op jit(solution)/shard_map/ppermute | solution.py:376
  60.9 9.3 %collective-permute-start.8 = (bf16[2,32,2304]{2,1,0:T(8,128)(2,1)S(1)}, bf16[2,32,2304]{2,1,0:T(8,128)(2,1)S(1)}, u32[]{:S(2)}, u32[]{:S(2)}) collective-permute-start(bf16[2,32,2304]{2,1,0:T(8,128)(2,1)S(1)} %get-tuple-element.98), channel_id=1, source_target_pairs={{0,2},{1,3},{2,0},{3,1},{4,6},{5,7},{6,4},{7,5},{8,10},{9,11},{10,... | collective-permute-start | bytes 884744 | tf_op jit(solution)/shard_map/ppermute | solution.py:376
  61.5 9.8 %collective-permute-start.10 = (bf16[2,32,2304]{2,1,0:T(8,128)(2,1)S(1)}, bf16[2,32,2304]{2,1,0:T(8,128)(2,1)S(1)}, u32[]{:S(2)}, u32[]{:S(2)}) collective-permute-start(bf16[2,32,2304]{2,1,0:T(8,128)(2,1)S(1)} %get-tuple-element.97), channel_id=1, source_target_pairs={{0,4},{1,5},{2,6},{3,7},{4,0},{5,1},{6,2},{7,3},{8,12},{9,13},{10,... | collective-permute-start | bytes 884744 | tf_op jit(solution)/shard_map/ppermute | solution.py:376
  66.0 10.1 %collective-permute-start.13 = (bf16[2,64,1536]{2,1,0:T(8,128)(2,1)S(1)}, bf16[2,64,1536]{2,1,0:T(8,128)(2,1)S(1)}, u32[]{:S(2)}, u32[]{:S(2)}) collective-permute-start(bf16[2,64,1536]{2,1,0:T(8,128)(2,1)S(1)} %pad_maximum_fusion.15), channel_id=1, source_target_pairs={{0,2},{1,3},{2,0},{3,1},{4,6},{5,7},{6,4},{7,5},{8,10},{9,11},{10,... | collective-permute-start | bytes 1179656 | tf_op jit(solution)/shard_map/ppermute | solution.py:376
  70.3 10.5 %collective-permute-start.9 = (bf16[2,64,2304]{2,1,0:T(8,128)(2,1)S(1)}, bf16[2,64,2304]{2,1,0:T(8,128)(2,1)S(1)}, u32[]{:S(2)}, u32[]{:S(2)}) collective-permute-start(bf16[2,64,2304]{2,1,0:T(8,128)(2,1)S(1)} %pad_maximum_fusion.10), channel_id=1, source_target_pairs={{0,4},{1,5},{2,6},{3,7},{4,0},{5,1},{6,2},{7,3},{8,12},{9,13},{10,... | collective-permute-start | bytes 1769480 | tf_op jit(solution)/shard_map/ppermute | solution.py:376
  71.3 12.6 %collective-permute-start.11 = (bf16[2,64,2304]{2,1,0:T(8,128)(2,1)S(1)}, bf16[2,64,2304]{2,1,0:T(8,128)(2,1)S(1)}, u32[]{:S(2)}, u32[]{:S(2)}) collective-permute-start(bf16[2,64,2304]{2,1,0:T(8,128)(2,1)S(1)} %pad_maximum_fusion.11), channel_id=1, source_target_pairs={{0,1},{1,0},{2,3},{3,2},{4,5},{5,4},{6,7},{7,6},{8,9},{9,8},{10,11... | collective-permute-start | bytes 1769480 | tf_op jit(solution)/shard_map/ppermute | solution.py:376
  82.0 7.8 %copy-start.4 = (s32[48,12]{0,1:T(8,128)S(1)}, s32[48,12]{0,1:T(8,128)}, u32[]{:S(2)}) copy-start(s32[48,12]{0,1:T(8,128)} %param.10) | copy-start | bytes 6916
  82.0 34.8 %copy-start.2 = (s32[12,48]{1,0:T(8,128)S(1)}, s32[12,48]{1,0:T(8,128)}, u32[]{:S(2)}) copy-start(s32[12,48]{1,0:T(8,128)} %pattern.5) | copy-start | bytes 6916
  85.0 29.5 %collective-permute-start.14 = (bf16[2,128,2304]{2,1,0:T(8,128)(2,1)S(1)}, bf16[2,128,2304]{2,1,0:T(8,128)(2,1)}, u32[]{:S(2)}, u32[]{:S(2)}) collective-permute-start(bf16[2,128,2304]{2,1,0:T(8,128)(2,1)S(1)} %pad_maximum_fusion.refs_0_), channel_id=1, source_target_pairs={{0,1},{1,0},{2,3},{3,2},{4,5},{5,4},{6,7},{7,6},{8,9},{9,8},{10,11... | collective-permute-start | bytes 3538952 | tf_op jit(solution)/shard_map/ppermute | solution.py:376
  87.5 29.2 %collective-permute-start.15 = (bf16[2,128,2304]{2,1,0:T(8,128)(2,1)}, bf16[2,128,2304]{2,1,0:T(8,128)(2,1)}, u32[]{:S(2)}, u32[]{:S(2)}) collective-permute-start(bf16[2,128,2304]{2,1,0:T(8,128)(2,1)} %pad_maximum_fusion.1.refs_2_), channel_id=1, source_target_pairs={{0,2},{1,3},{2,0},{3,1},{4,6},{5,7},{6,4},{7,5},{8,10},{9,11},{10,... | collective-permute-start | bytes 3538952 | tf_op jit(solution)/shard_map/ppermute | solution.py:376
  87.5 12.3 %collective-permute-start.16 = (bf16[2,128,1536]{2,1,0:T(8,128)(2,1)S(1)}, bf16[2,128,1536]{2,1,0:T(8,128)(2,1)}, u32[]{:S(2)}, u32[]{:S(2)}) collective-permute-start(bf16[2,128,1536]{2,1,0:T(8,128)(2,1)S(1)} %pad_maximum_fusion.6.refs_4_), channel_id=1, source_target_pairs={{0,4},{1,5},{2,6},{3,7},{4,0},{5,1},{6,2},{7,3},{8,12},{9,13},{10,... | collective-permute-start | bytes 2359304 | tf_op jit(solution)/shard_map/ppermute | solution.py:376
  87.7 49.7 %collective-permute-start.18 = (bf16[2,128,2304]{2,1,0:T(8,128)(2,1)}, bf16[2,128,2304]{2,1,0:T(8,128)(2,1)}, u32[]{:S(2)}, u32[]{:S(2)}) collective-permute-start(bf16[2,128,2304]{2,1,0:T(8,128)(2,1)} %pad_maximum_fusion.2.refs_8_.refs_0_), channel_id=1, source_target_pairs={{0,1},{1,0},{2,3},{3,2},{4,5},{5,4},{6,7},{7,6},{8,9},{9,8},{10,11... | collective-permute-start | bytes 3538952 | tf_op jit(solution)/shard_map/ppermute | solution.py:376
  87.9 49.5 %collective-permute-start.19 = (bf16[2,128,2304]{2,1,0:T(8,128)(2,1)}, bf16[2,128,2304]{2,1,0:T(8,128)(2,1)}, u32[]{:S(2)}, u32[]{:S(2)}) collective-permute-start(bf16[2,128,2304]{2,1,0:T(8,128)(2,1)} %pad_maximum_fusion.3.refs_9_.refs_2_), channel_id=1, source_target_pairs={{0,2},{1,3},{2,0},{3,1},{4,6},{5,7},{6,4},{7,5},{8,10},{9,11},{10,... | collective-permute-start | bytes 3538952 | tf_op jit(solution)/shard_map/ppermute | solution.py:376
  136.6 2.4 collective-permute-start.20
  136.7 3.4 %collective-permute-start.17 = (bf16[256,1536]{1,0:T(8,128)(2,1)S(1)}, bf16[256,1536]{1,0:T(8,128)(2,1)S(1)}, u32[]{:S(2)}, u32[]{:S(2)}) collective-permute-start(bf16[256,1536]{1,0:T(8,128)(2,1)S(1)} %get-tuple-element.53), channel_id=1, source_target_pairs={{0,16},{16,0},{1,17},{17,1},{2,18},{18,2},{3,19},{19,3},{4,20},{20... | collective-permute-start | bytes 2359304 | tf_op jit(solution)/shard_map/ppermute | solution.py:384
  137.2 20.4 %collective-permute-start.22 = (bf16[2,128,1536]{2,1,0:T(8,128)(2,1)S(1)}, bf16[2,128,1536]{2,1,0:T(8,128)(2,1)S(1)}, u32[]{:S(2)}, u32[]{:S(2)}) collective-permute-start(bf16[2,128,1536]{2,1,0:T(8,128)(2,1)S(1)} %pad_maximum_fusion.7.refs_10_.refs_4_), channel_id=1, source_target_pairs={{0,4},{1,5},{2,6},{3,7},{4,0},{5,1},{6,2},{7,3},{8,12},{9,13},{10,... | collective-permute-start | bytes 2359304 | tf_op jit(solution)/shard_map/ppermute | solution.py:376
  152.1 27.0 %collective-permute-start.29 = (bf16[128,1536]{1,0:T(8,128)(2,1)S(1)}, bf16[128,1536]{1,0:T(8,128)(2,1)S(1)}, u32[]{:S(2)}, u32[]{:S(2)}) collective-permute-start(bf16[128,1536]{1,0:T(8,128)(2,1)S(1)} %get-tuple-element.62.refs_13_), channel_id=1, source_target_pairs={{0,4},{1,5},{2,6},{3,7},{4,0},{5,1},{6,2},{7,3},{8,12},{9,13},{10,... | collective-permute-start | bytes 1179656 | tf_op jit(solution)/shard_map/ppermute | solution.py:376
  152.3 26.9 %collective-permute-start.21 = (bf16[128,2304]{1,0:T(8,128)(2,1)S(1)}, bf16[128,2304]{1,0:T(8,128)(2,1)S(1)}, u32[]{:S(2)}, u32[]{:S(2)}) collective-permute-start(bf16[128,2304]{1,0:T(8,128)(2,1)S(1)} %get-tuple-element.58.refs_9_), channel_id=1, source_target_pairs={{0,1},{1,0},{2,3},{3,2},{4,5},{5,4},{6,7},{7,6},{8,9},{9,8},{10,11... | collective-permute-start | bytes 1769480 | tf_op jit(solution)/shard_map/ppermute | solution.py:376
  152.3 27.3 %collective-permute-start.27 = (bf16[128,2304]{1,0:T(8,128)(2,1)S(1)}, bf16[128,2304]{1,0:T(8,128)(2,1)S(1)}, u32[]{:S(2)}, u32[]{:S(2)}) collective-permute-start(bf16[128,2304]{1,0:T(8,128)(2,1)S(1)} %get-tuple-element.60.refs_11_), channel_id=1, source_target_pairs={{0,2},{1,3},{2,0},{3,1},{4,6},{5,7},{6,4},{7,5},{8,10},{9,11},{10,... | collective-permute-start | bytes 1769480 | tf_op jit(solution)/shard_map/ppermute | solution.py:376
  178.4 2.4 collective-permute-start.25
  178.5 3.4 %collective-permute-start.24 = (bf16[256,1536]{1,0:T(8,128)(2,1)S(1)}, bf16[256,1536]{1,0:T(8,128)(2,1)S(1)}, u32[]{:S(2)}, u32[]{:S(2)}) collective-permute-start(bf16[256,1536]{1,0:T(8,128)(2,1)S(1)} %get-tuple-element.63), channel_id=1, source_target_pairs={{0,16},{16,0},{1,17},{17,1},{2,18},{18,2},{3,19},{19,3},{4,20},{20... | collective-permute-start | bytes 2359304 | tf_op jit(solution)/shard_map/ppermute | solution.py:384
  179.1 7.0 %collective-permute-start.30 = (bf16[64,1536]{1,0:T(8,128)(2,1)S(1)}, bf16[64,1536]{1,0:T(8,128)(2,1)S(1)}, u32[]{:S(2)}, u32[]{:S(2)}) collective-permute-start(bf16[64,1536]{1,0:T(8,128)(2,1)S(1)} %slice.161), channel_id=1, source_target_pairs={{0,2},{1,3},{2,0},{3,1},{4,6},{5,7},{6,4},{7,5},{8,10},{9,11},{10,... | collective-permute-start | bytes 589832 | tf_op jit(solution)/shard_map/ppermute | solution.py:376
  179.4 9.1 %collective-permute-start.23 = (bf16[64,2304]{1,0:T(8,128)(2,1)S(1)}, bf16[64,2304]{1,0:T(8,128)(2,1)S(1)}, u32[]{:S(2)}, u32[]{:S(2)}) collective-permute-start(bf16[64,2304]{1,0:T(8,128)(2,1)S(1)} %slice.155), channel_id=1, source_target_pairs={{0,4},{1,5},{2,6},{3,7},{4,0},{5,1},{6,2},{7,3},{8,12},{9,13},{10,... | collective-permute-start | bytes 884744 | tf_op jit(solution)/shard_map/ppermute | solution.py:376
  179.8 9.5 %collective-permute-start.28 = (bf16[64,2304]{1,0:T(8,128)(2,1)S(1)}, bf16[64,2304]{1,0:T(8,128)(2,1)S(1)}, u32[]{:S(2)}, u32[]{:S(2)}) collective-permute-start(bf16[64,2304]{1,0:T(8,128)(2,1)S(1)} %slice.159), channel_id=1, source_target_pairs={{0,1},{1,0},{2,3},{3,2},{4,5},{5,4},{6,7},{7,6},{8,9},{9,8},{10,11... | collective-permute-start | bytes 884744 | tf_op jit(solution)/shard_map/ppermute | solution.py:376
  186.1 29.8 %collective-permute-start.32 = (bf16[32,1536]{1,0:T(8,128)(2,1)S(1)}, bf16[32,1536]{1,0:T(8,128)(2,1)S(1)}, u32[]{:S(2)}, u32[]{:S(2)}) collective-permute-start(bf16[32,1536]{1,0:T(8,128)(2,1)S(1)} %slice.165), channel_id=1, source_target_pairs={{0,1},{1,0},{2,3},{3,2},{4,5},{5,4},{6,7},{7,6},{8,9},{9,8},{10,11... | collective-permute-start | bytes 294920 | tf_op jit(solution)/shard_map/ppermute | solution.py:376
  189.4 15.7 %slice-start = ((s8[6291456]{0:T(1024)(128)(4,1)}), s8[4194304]{0:T(1024)(128)(4,1)S(1)}, s32[]{:S(2)}) async-start(s8[6291456]{0:T(1024)(128)(4,1)} %bitcast.8), calls=%async_computation | async-start | bytes 8388608
  189.4 15.6 %slice-start.1 = ((s8[6291456]{0:T(1024)(128)(4,1)}), s8[2097152]{0:T(1024)(128)(4,1)S(1)}, s32[]{:S(2)}) async-start(s8[6291456]{0:T(1024)(128)(4,1)} %bitcast.8), calls=%async_computation.1 | async-start | bytes 4194304
  200.8 27.3 %collective-permute-start.34 = (bf16[128,2304]{1,0:T(8,128)(2,1)S(1)}, bf16[128,2304]{1,0:T(8,128)(2,1)S(1)}, u32[]{:S(2)}, u32[]{:S(2)}) collective-permute-start(bf16[128,2304]{1,0:T(8,128)(2,1)S(1)} %get-tuple-element.74.refs_5_), channel_id=1, source_target_pairs={{0,1},{1,0},{2,3},{3,2},{4,5},{5,4},{6,7},{7,6},{8,9},{9,8},{10,11... | collective-permute-start | bytes 1769480 | tf_op jit(solution)/shard_map/ppermute | solution.py:376
  201.2 27.1 %collective-permute-start.35 = (bf16[128,2304]{1,0:T(8,128)(2,1)S(1)}, bf16[128,2304]{1,0:T(8,128)(2,1)S(1)}, u32[]{:S(2)}, u32[]{:S(2)}) collective-permute-start(bf16[128,2304]{1,0:T(8,128)(2,1)S(1)} %get-tuple-element.76.refs_7_), channel_id=1, source_target_pairs={{0,2},{1,3},{2,0},{3,1},{4,6},{5,7},{6,4},{7,5},{8,10},{9,11},{10,... | collective-permute-start | bytes 1769480 | tf_op jit(solution)/shard_map/ppermute | solution.py:376
  203.3 24.6 %collective-permute-start.36 = (bf16[128,1536]{1,0:T(8,128)(2,1)S(1)}, bf16[128,1536]{1,0:T(8,128)(2,1)S(1)}, u32[]{:S(2)}, u32[]{:S(2)}) collective-permute-start(bf16[128,1536]{1,0:T(8,128)(2,1)S(1)} %get-tuple-element.78.refs_9_), channel_id=1, source_target_pairs={{0,4},{1,5},{2,6},{3,7},{4,0},{5,1},{6,2},{7,3},{8,12},{9,13},{10,... | collective-permute-start | bytes 1179656 | tf_op jit(solution)/shard_map/ppermute | solution.py:376
  216.0 11.9 %collective-permute-start.31 = (bf16[32,2304]{1,0:T(8,128)(2,1)S(1)}, bf16[32,2304]{1,0:T(8,128)(2,1)S(1)}, u32[]{:S(2)}, u32[]{:S(2)}) collective-permute-start(bf16[32,2304]{1,0:T(8,128)(2,1)S(1)} %slice.163), channel_id=1, source_target_pairs={{0,4},{1,5},{2,6},{3,7},{4,0},{5,1},{6,2},{7,3},{8,12},{9,13},{10,... | collective-permute-start | bytes 442376 | tf_op jit(solution)/shard_map/ppermute | solution.py:376
  216.3 11.6 %collective-permute-start.26 = (bf16[32,2304]{1,0:T(8,128)(2,1)S(1)}, bf16[32,2304]{1,0:T(8,128)(2,1)S(1)}, u32[]{:S(2)}, u32[]{:S(2)}) collective-permute-start(bf16[32,2304]{1,0:T(8,128)(2,1)S(1)} %slice.157), channel_id=1, source_target_pairs={{0,2},{1,3},{2,0},{3,1},{4,6},{5,7},{6,4},{7,5},{8,10},{9,11},{10,... | collective-permute-start | bytes 442376 | tf_op jit(solution)/shard_map/ppermute | solution.py:376
  228.4 16.2 %collective-permute-start.39 = (bf16[64,1536]{1,0:T(8,128)(2,1)S(1)}, bf16[64,1536]{1,0:T(8,128)(2,1)S(1)}, u32[]{:S(2)}, u32[]{:S(2)}) collective-permute-start(bf16[64,1536]{1,0:T(8,128)(2,1)S(1)} %slice.143), channel_id=1, source_target_pairs={{0,2},{1,3},{2,0},{3,1},{4,6},{5,7},{6,4},{7,5},{8,10},{9,11},{10,... | collective-permute-start | bytes 589832 | tf_op jit(solution)/shard_map/ppermute | solution.py:376
  230.5 14.7 %collective-permute-start.33 = (bf16[16,6144]{1,0:T(8,128)(2,1)S(1)}, bf16[16,6144]{1,0:T(8,128)(2,1)S(1)}, u32[]{:S(2)}, u32[]{:S(2)}) collective-permute-start(bf16[16,6144]{1,0:T(8,128)(2,1)S(1)} %slice.167), channel_id=1, source_target_pairs={{0,8},{1,9},{2,10},{3,11},{4,12},{5,13},{6,14},{7,15},{8,0},{9,1},... | collective-permute-start | bytes 589832 | tf_op jit(solution)/shard_map/ppermute | solution.py:376
  232.4 12.2 %collective-permute-start.37 = (bf16[64,2304]{1,0:T(8,128)(2,1)S(1)}, bf16[64,2304]{1,0:T(8,128)(2,1)S(1)}, u32[]{:S(2)}, u32[]{:S(2)}) collective-permute-start(bf16[64,2304]{1,0:T(8,128)(2,1)S(1)} %slice.139), channel_id=1, source_target_pairs={{0,4},{1,5},{2,6},{3,7},{4,0},{5,1},{6,2},{7,3},{8,12},{9,13},{10,... | collective-permute-start | bytes 884744 | tf_op jit(solution)/shard_map/ppermute | solution.py:376
  234.4 10.3 %collective-permute-start.38 = (bf16[64,2304]{1,0:T(8,128)(2,1)S(1)}, bf16[64,2304]{1,0:T(8,128)(2,1)S(1)}, u32[]{:S(2)}, u32[]{:S(2)}) collective-permute-start(bf16[64,2304]{1,0:T(8,128)(2,1)S(1)} %slice.141), channel_id=1, source_target_pairs={{0,1},{1,0},{2,3},{3,2},{4,5},{5,4},{6,7},{7,6},{8,9},{9,8},{10,11... | collective-permute-start | bytes 884744 | tf_op jit(solution)/shard_map/ppermute | solution.py:376
  244.8 4.7 %collective-permute-start.42 = (bf16[32,1536]{1,0:T(8,128)(2,1)S(1)}, bf16[32,1536]{1,0:T(8,128)(2,1)S(1)}, u32[]{:S(2)}, u32[]{:S(2)}) collective-permute-start(bf16[32,1536]{1,0:T(8,128)(2,1)S(1)} %slice.149), channel_id=1, source_target_pairs={{0,1},{1,0},{2,3},{3,2},{4,5},{5,4},{6,7},{7,6},{8,9},{9,8},{10,11... | collective-permute-start | bytes 294920 | tf_op jit(solution)/shard_map/ppermute | solution.py:376
  245.2 6.9 %collective-permute-start.41 = (bf16[32,2304]{1,0:T(8,128)(2,1)S(1)}, bf16[32,2304]{1,0:T(8,128)(2,1)S(1)}, u32[]{:S(2)}, u32[]{:S(2)}) collective-permute-start(bf16[32,2304]{1,0:T(8,128)(2,1)S(1)} %slice.147), channel_id=1, source_target_pairs={{0,4},{1,5},{2,6},{3,7},{4,0},{5,1},{6,2},{7,3},{8,12},{9,13},{10,... | collective-permute-start | bytes 442376 | tf_op jit(solution)/shard_map/ppermute | solution.py:376
  245.4 6.7 %collective-permute-start.40 = (bf16[32,2304]{1,0:T(8,128)(2,1)S(1)}, bf16[32,2304]{1,0:T(8,128)(2,1)S(1)}, u32[]{:S(2)}, u32[]{:S(2)}) collective-permute-start(bf16[32,2304]{1,0:T(8,128)(2,1)S(1)} %slice.145), channel_id=1, source_target_pairs={{0,2},{1,3},{2,0},{3,1},{4,6},{5,7},{6,4},{7,5},{8,10},{9,11},{10,... | collective-permute-start | bytes 442376 | tf_op jit(solution)/shard_map/ppermute | solution.py:376
  252.3 9.1 %collective-permute-start.43 = (bf16[16,6144]{1,0:T(8,128)(2,1)S(1)}, bf16[16,6144]{1,0:T(8,128)(2,1)S(1)}, u32[]{:S(2)}, u32[]{:S(2)}) collective-permute-start(bf16[16,6144]{1,0:T(8,128)(2,1)S(1)} %slice.169), channel_id=1, source_target_pairs={{0,8},{1,9},{2,10},{3,11},{4,12},{5,13},{6,14},{7,15},{8,0},{9,1},... | collective-permute-start | bytes 589832 | tf_op jit(solution)/shard_map/ppermute | solution.py:376
  (3 other events, 6.5 us)

commit v4 on v3

--- a/solution.py
+++ b/solution.py
@@ -10,7 +10,7 @@
 half_root = 0.7071067811865476
 inv_root_tau = 0.3989422804014327
 GROUPS = 2
-SPLIT = (18, 18)
+SPLIT = (18, 20)
 OUT_OF = 48
 
 

time: 262 us -> 260 us (level)
  waiting for transfers between devices: 107 us -> 97 us
  starting transfers between devices: 42.2 us -> 49.7 us
    ppermute x40, starting transfers between devices: 41 us -> 48.6 us  [swap(): return lax.ppermute(value, 'col', [(i, i ^ 1 << bit) for i in range(n)])]
    ppermute x40, waiting for transfers between devices: 103 us -> 95.8 us  [swap(): return lax.ppermute(value, 'col', [(i, i ^ 1 << bit) for i in range(n)])]
    ppermute x4, waiting for transfers between devices: 4.33 us -> 1.19 us  [beside(): lax.ppermute(part.astype(jnp.bfloat16), 'row', pairs)]
    unnamed x15 -> x13, local copies, waits for them, and re-layouts: 6.55 us -> 5.68 us
  transfers between devices with their start and end apart: 44 -> 44, of which waited for: 25 -> 22; matrix products, arithmetic and copies ran while one was open for 2% -> 2% of each run, Pallas kernels for 36% -> 37%
where the time goes in v4:
time: 260 us
  waiting for transfers between devices  97 us (37%)
  Pallas kernels  96.5 us (37%)
  starting transfers between devices  49.7 us (19%)
  other arithmetic  8.42 us (3%)
  local copies, waits for them, and re-layouts  7.25 us (3%)
    ppermute x40, waiting for transfers between devices, swap(): return lax.ppermute(value, 'col', [(i, i ^ 1 << bit) for i in range(n)])  95.8 us
    ppermute x40, starting transfers between devices, swap(): return lax.ppermute(value, 'col', [(i, i ^ 1 << bit) for i in range(n)])  48.6 us
    pallas_call x2, Pallas kernels, forward(): pl.pallas_call(functools.partial(forward_kernel, moves, block), in_specs=...  39.3 us
    pallas_call x4, Pallas kernels, call(): pl.pallas_call(functools.partial(grad_kernel, block, factor, (off[0] * ti...  33.3 us
    pallas_call x2, Pallas kernels, backward(): pl.pallas_call(functools.partial(backward_kernel, parts, block), in_specs...  23.9 us
    unnamed x13, local copies, waits for them, and re-layouts  5.68 us
  transfers between devices with their start and end apart: 44, of which 22 were waited for; matrix products, arithmetic and copies ran while one was open for 2% of the time, Pallas kernels for 37%

profile of v4, /device:TPU:0, one launch (start us, length us, event | category | flops | bytes accessed | tf_op | source)
XLA Modules:
  0.0 260.0 jit_solution(16136746019483326627)
XLA Ops:
  0.6 1.3 slice_bitcast_fusion.2
  2.0 4.1 %collective-permute-start = (bf16[2,16,6144]{2,1,0:T(8,128)(2,1)S(1)}, bf16[2,16,6144]{2,1,0:T(8,128)(2,1)S(1)}, u32[]{:S(2)}, u32[]{:S(2)}) collective-permute-start(bf16[2,16,6144]{2,1,0:T(8,128)(2,1)S(1)} %pad_maximum_fusion.12), channel_id=1, source_target_pairs={{0,8},{1,9},{2,10},{3,11},{4,12},{5,13},{6,14},{7,15},{8,0},{9,1},... | collective-permute-start | bytes 1179656 | tf_op jit(solution)/shard_map/ppermute | solution.py:376
  6.1 17.5 %collective-permute-done = bf16[2,16,6144]{2,1,0:T(8,128)(2,1)S(1)} collective-permute-done((bf16[2,16,6144]{2,1,0:T(8,128)(2,1)S(1)}, bf16[2,16,6144]{2,1,0:T(8,128)(2,1)S(1)}, u32[]{:S(2)}, u32[]{:S(2)}) %collective-permute-start) | collective-permute-done | bytes 393248 | tf_op jit(solution)/shard_map/ppermute | solution.py:376
  23.7 1.6 collective-permute-start.1
  25.3 1.6 collective-permute-start.4
  27.7 3.0 %collective-permute-done.4 = bf16[2,32,1280]{2,1,0:T(8,128)(2,1)S(1)} collective-permute-done((bf16[2,32,1280]{2,1,0:T(8,128)(2,1)S(1)}, bf16[2,32,1280]{2,1,0:T(8,128)(2,1)S(1)}, u32[]{:S(2)}, u32[]{:S(2)}) %collective-permute-start.4) | collective-permute-done | bytes 163872 | tf_op jit(solution)/shard_map/ppermute | solution.py:376
  31.3 1.3 collective-permute-done.1
  32.6 2.5 collective-permute-done.3
  35.1 3.4 %collective-permute-start.5 = (bf16[2,16,6144]{2,1,0:T(8,128)(2,1)S(1)}, bf16[2,16,6144]{2,1,0:T(8,128)(2,1)S(1)}, u32[]{:S(2)}, u32[]{:S(2)}) collective-permute-start(bf16[2,16,6144]{2,1,0:T(8,128)(2,1)S(1)} %pad_maximum_fusion.13), channel_id=1, source_target_pairs={{0,8},{1,9},{2,10},{3,11},{4,12},{5,13},{6,14},{7,15},{8,0},{9,1},... | collective-permute-start | bytes 1179656 | tf_op jit(solution)/shard_map/ppermute | solution.py:376
  38.5 1.7 collective-permute-start.2
  40.9 14.3 %collective-permute-done.5 = bf16[2,16,6144]{2,1,0:T(8,128)(2,1)S(1)} collective-permute-done((bf16[2,16,6144]{2,1,0:T(8,128)(2,1)S(1)}, bf16[2,16,6144]{2,1,0:T(8,128)(2,1)S(1)}, u32[]{:S(2)}, u32[]{:S(2)}) %collective-permute-start.5) | collective-permute-done | bytes 393248 | tf_op jit(solution)/shard_map/ppermute | solution.py:376
  55.2 4.5 %collective-permute-done.2 = bf16[2,64,2304]{2,1,0:T(8,128)(2,1)S(1)} collective-permute-done((bf16[2,64,2304]{2,1,0:T(8,128)(2,1)S(1)}, bf16[2,64,2304]{2,1,0:T(8,128)(2,1)S(1)}, u32[]{:S(2)}, u32[]{:S(2)}) %collective-permute-start.2) | collective-permute-done | bytes 589856 | tf_op jit(solution)/shard_map/ppermute | solution.py:376
  62.3 1.4 collective-permute-start.10
  63.6 2.8 %collective-permute-done.12 = bf16[2,32,1280]{2,1,0:T(8,128)(2,1)S(1)} collective-permute-done((bf16[2,32,1280]{2,1,0:T(8,128)(2,1)S(1)}, bf16[2,32,1280]{2,1,0:T(8,128)(2,1)S(1)}, u32[]{:S(2)}, u32[]{:S(2)}) %collective-permute-start.12) | collective-permute-done | bytes 163872 | tf_op jit(solution)/shard_map/ppermute | solution.py:376
  67.0 4.3 %collective-permute-done.8 = bf16[2,32,2304]{2,1,0:T(8,128)(2,1)S(1)} collective-permute-done((bf16[2,32,2304]{2,1,0:T(8,128)(2,1)S(1)}, bf16[2,32,2304]{2,1,0:T(8,128)(2,1)S(1)}, u32[]{:S(2)}, u32[]{:S(2)}) %collective-permute-start.8) | collective-permute-done | bytes 294944 | tf_op jit(solution)/shard_map/ppermute | solution.py:376
  72.5 2.2 collective-permute-start.11
  75.5 6.5 %collective-permute-done.9 = bf16[2,64,2304]{2,1,0:T(8,128)(2,1)S(1)} collective-permute-done((bf16[2,64,2304]{2,1,0:T(8,128)(2,1)S(1)}, bf16[2,64,2304]{2,1,0:T(8,128)(2,1)S(1)}, u32[]{:S(2)}, u32[]{:S(2)}) %collective-permute-start.9) | collective-permute-done | bytes 589856 | tf_op jit(solution)/shard_map/ppermute | solution.py:376
  83.3 1.2 pad_maximum_fusion.1.refs_9_.refs_2_
  84.4 1.5 collective-permute-start.15
  85.9 1.7 collective-permute-start.14
  89.8 8.9 %collective-permute-done.16.refs_5_ = bf16[2,128,1280]{2,1,0:T(8,128)(2,1)S(1)} collective-permute-done((bf16[2,128,1280]{2,1,0:T(8,128)(2,1)S(1)}, bf16[2,128,1280]{2,1,0:T(8,128)(2,1)S(1)}, u32[]{:S(2)}, u32[]{:S(2)}) %collective-permute-start.16) | collective-permute-done | bytes 655392 | tf_op jit(solution)/shard_map/ppermute | solution.py:376
  98.8 16.2 %collective-permute-done.14.refs_1_ = bf16[2,128,2304]{2,1,0:T(8,128)(2,1)} collective-permute-done((bf16[2,128,2304]{2,1,0:T(8,128)(2,1)S(1)}, bf16[2,128,2304]{2,1,0:T(8,128)(2,1)}, u32[]{:S(2)}, u32[]{:S(2)}) %collective-permute-start.14) | collective-permute-done | bytes 1179680 | tf_op jit(solution)/shard_map/ppermute | solution.py:376
  114.9 1.5 collective-permute-done.15.refs_3_
  116.5 19.7 %forward.2 = (bf16[2,256,6144]{2,1,0:T(8,128)(2,1)}, bf16[256,1536]{1,0:T(8,128)(2,1)S(1)}, bf16[256,1536]{1,0:T(8,128)(2,1)S(1)}) custom-call(s32[48,12]{1,0:T(8,128)S(1)} %copy.12.up_on.pattern, s32[12,48]{1,0:T(8,128)S(1)} %copy-done.2, bf16[2,128,2304]{2,1,0:T(8,128)(2,1)S(1)} %pad_maximum_fusion.2.refs_0_, ...), custom_call_target="tpu_custom_call" | custom-call | flops 1572864 | bytes 1572864 | tf_op jit(solution)/shard_map/forward/pallas_call | solution.py:174
  136.8 1.2 collective-permute-start.22
  140.7 11.7 %backward.2 = (bf16[128,2304]{1,0:T(8,128)(2,1)S(1)}, bf16[128,2304]{1,0:T(8,128)(2,1)S(1)}, bf16[128,2560]{1,0:T(8,128)(2,1)S(1)}, bf16[128,2560]{1,0:T(8,128)(...) custom-call(s32[48,12]{1,0:T(8,128)S(1)} %copy.12.up_on.pattern, ...), custom_call_target="tpu_custom_call" | custom-call | flops 1572864 | bytes 1572864 | tf_op jit(solution)/shard_map/backward/pallas_call | solution.py:250
  152.4 1.3 collective-permute-start.29
  153.8 1.5 collective-permute-start.21
  155.3 1.6 collective-permute-start.27
  156.8 19.5 %forward.3 = (bf16[2,256,6144]{2,1,0:T(8,128)(2,1)}, bf16[256,1536]{1,0:T(8,128)(2,1)S(1)}, bf16[256,1536]{1,0:T(8,128)(2,1)S(1)}) custom-call(s32[48,12]{1,0:T(8,128)S(1)} %copy.12.up_on.pattern, s32[12,48]{1,0:T(8,128)S(1)} %copy-done.2, bf16[2,128,2304]{2,1,0:T(8,128)(2,1)} %pad_maximum_fusion.3.refs_8_.refs_0_, ...), custom_call_target="tpu_custom_call" | custom-call | flops 1572864 | bytes 1572864 | tf_op jit(solution)/shard_map/forward/pallas_call | solution.py:174
  177.8 1.6 collective-permute-start.23
  180.9 2.4 collective-permute-done.30
  183.9 2.6 %collective-permute-done.23 = bf16[64,2304]{1,0:T(8,128)(2,1)S(1)} collective-permute-done((bf16[64,2304]{1,0:T(8,128)(2,1)S(1)}, bf16[64,2304]{1,0:T(8,128)(2,1)S(1)}, u32[]{:S(2)}, u32[]{:S(2)}) %collective-permute-start.23) | collective-permute-done | bytes 294944 | tf_op jit(solution)/shard_map/ppermute | solution.py:376
  186.6 1.6 collective-permute-start.26
  188.3 1.3 collective-permute-done.28
  189.7 12.2 %backward.3 = (bf16[128,2304]{1,0:T(8,128)(2,1)S(1)}, bf16[128,2304]{1,0:T(8,128)(2,1)S(1)}, bf16[128,2560]{1,0:T(8,128)(2,1)S(1)}, bf16[128,2560]{1,0:T(8,128)(...) custom-call(s32[48,12]{1,0:T(8,128)S(1)} %copy.12.up_on.pattern, ...), custom_call_target="tpu_custom_call" | custom-call | flops 1572864 | bytes 1572864 | tf_op jit(solution)/shard_map/backward/pallas_call | solution.py:250
  203.3 1.3 collective-permute-start.36
  204.5 2.8 %copy-done = bf16[2,256,6144]{2,1,0:T(8,128)(2,1)S(1)} copy-done((bf16[2,256,6144]{2,1,0:T(8,128)(2,1)S(1)}, bf16[2,256,6144]{2,1,0:T(8,128)(2,1)}, u32[]{:S(2)}) %copy-start) | copy-done | bytes 6291480
  207.3 8.4 %grad.4.refs_7_ = bf16[1536,6144]{1,0:T(8,128)(2,1)} custom-call(s32[12,48]{1,0:T(8,128)S(1)} %copy-done.2, bf16[256,1536]{1,0:T(8,128)(2,1)S(1)} %get-tuple-element.95.refs_0_, bf16[256,1536]{1,0:T(8,128)(2,1)S(1)} %get-tuple-element.93.refs_1_, bf16[2,256,6144]{2,1,0:T(8,128)(2,1)S(1)} %bitcast.9, bf16[2,256,6144]{2,1,0:T(8,128)(2,1)S(1)} %copy-done, ...), custom_call_target="tpu_custom_call" | custom-call | flops 4718592 | bytes 1572864 | tf_op jit(solution)/shard_map/grad/pallas_call | solution.py:323
  216.6 2.8 %copy-done.1 = bf16[2,256,6144]{2,1,0:T(8,128)(2,1)S(1)} copy-done((bf16[2,256,6144]{2,1,0:T(8,128)(2,1)S(1)}, bf16[2,256,6144]{2,1,0:T(8,128)(2,1)}, u32[]{:S(2)}) %copy-start.1) | copy-done | bytes 6291480
  219.4 8.4 %grad.5.refs_7_ = bf16[6144,1536]{1,0:T(8,128)(2,1)} custom-call(s32[48,12]{1,0:T(8,128)S(1)} %copy.12.up_on.pattern, bf16[2,256,6144]{2,1,0:T(8,128)(2,1)S(1)} %bitcast.9, bf16[2,256,6144]{2,1,0:T(8,128)(2,1)S(1)} %copy-done.1, bf16[256,1536]{1,0:T(8,128)(2,1)S(1)} %get-tuple-element.96.dhid_ref.refs_2_, ...), custom_call_target="tpu_custom_call" | custom-call | flops 4718592 | bytes 393216 | tf_op jit(solution)/shard_map/grad/pallas_call | solution.py:323
  229.5 2.1 collective-permute-start.33
  232.0 1.8 collective-permute-start.38
  233.8 8.4 %grad.6 = bf16[6144,1536]{1,0:T(8,128)(2,1)} custom-call(s32[48,12]{1,0:T(8,128)S(1)} %copy.12.up_on.pattern, bf16[2,256,6144]{2,1,0:T(8,128)(2,1)S(1)} %bitcast.9, bf16[2,256,6144]{2,1,0:T(8,128)(2,1)S(1)} %copy-done.1, bf16[256,1536]{1,0:T(8,128)(2,1)S(1)} %get-tuple-element.96.dhid_ref.refs_2_, ...), custom_call_target="tpu_custom_call", output_to_operand_aliasing={{}: (8, {})} | custom-call | flops 4718592 | bytes 393216 | tf_op jit(solution)/shard_map/grad/pallas_call | solution.py:323
  242.8 1.8 collective-permute-start.41
  245.4 1.5 collective-permute-done.42
  247.0 2.8 %collective-permute-done.40 = bf16[32,2304]{1,0:T(8,128)(2,1)S(1)} collective-permute-done((bf16[32,2304]{1,0:T(8,128)(2,1)S(1)}, bf16[32,2304]{1,0:T(8,128)(2,1)S(1)}, u32[]{:S(2)}, u32[]{:S(2)}) %collective-permute-start.40) | collective-permute-done | bytes 147488 | tf_op jit(solution)/shard_map/ppermute | solution.py:376
  251.0 8.1 %grad.7 = bf16[1536,6144]{1,0:T(8,128)(2,1)} custom-call(s32[12,48]{1,0:T(8,128)S(1)} %copy-done.2, bf16[256,1536]{1,0:T(8,128)(2,1)S(1)} %get-tuple-element.95.refs_0_, bf16[256,1536]{1,0:T(8,128)(2,1)S(1)} %get-tuple-element.93.refs_1_, bf16[2,256,6144]{2,1,0:T(8,128)(2,1)S(1)} %bitcast.9, ...), custom_call_target="tpu_custom_call", output_to_operand_aliasing={{}: (8, {})} | custom-call | flops 4718592 | bytes 1572864 | tf_op jit(solution)/shard_map/grad/pallas_call | solution.py:323
  (124 shorter events, 25.3 us)
Async XLA Ops:
  2.0 21.6 %collective-permute-start = (bf16[2,16,6144]{2,1,0:T(8,128)(2,1)S(1)}, bf16[2,16,6144]{2,1,0:T(8,128)(2,1)S(1)}, u32[]{:S(2)}, u32[]{:S(2)}) collective-permute-start(bf16[2,16,6144]{2,1,0:T(8,128)(2,1)S(1)} %pad_maximum_fusion.12), channel_id=1, source_target_pairs={{0,8},{1,9},{2,10},{3,11},{4,12},{5,13},{6,14},{7,15},{8,0},{9,1},... | collective-permute-start | bytes 1179656 | tf_op jit(solution)/shard_map/ppermute | solution.py:376
  23.7 8.9 %collective-permute-start.1 = (bf16[2,32,2304]{2,1,0:T(8,128)(2,1)S(1)}, bf16[2,32,2304]{2,1,0:T(8,128)(2,1)S(1)}, u32[]{:S(2)}, u32[]{:S(2)}) collective-permute-start(bf16[2,32,2304]{2,1,0:T(8,128)(2,1)S(1)} %slice.152), channel_id=1, source_target_pairs={{0,2},{1,3},{2,0},{3,1},{4,6},{5,7},{6,4},{7,5},{8,10},{9,11},{10,... | collective-permute-start | bytes 884744 | tf_op jit(solution)/shard_map/ppermute | solution.py:376
  25.3 5.4 %collective-permute-start.4 = (bf16[2,32,1280]{2,1,0:T(8,128)(2,1)S(1)}, bf16[2,32,1280]{2,1,0:T(8,128)(2,1)S(1)}, u32[]{:S(2)}, u32[]{:S(2)}) collective-permute-start(bf16[2,32,1280]{2,1,0:T(8,128)(2,1)S(1)} %pad_maximum_fusion.19), channel_id=1, source_target_pairs={{0,1},{1,0},{2,3},{3,2},{4,5},{5,4},{6,7},{7,6},{8,9},{9,8},{10,11... | collective-permute-start | bytes 491528 | tf_op jit(solution)/shard_map/ppermute | solution.py:376
  27.0 8.1 %collective-permute-start.3 = (bf16[2,32,2560]{2,1,0:T(8,128)(2,1)S(1)}, bf16[2,32,2560]{2,1,0:T(8,128)(2,1)S(1)}, u32[]{:S(2)}, u32[]{:S(2)}) collective-permute-start(bf16[2,32,2560]{2,1,0:T(8,128)(2,1)S(1)} %slice.153), channel_id=1, source_target_pairs={{0,4},{1,5},{2,6},{3,7},{4,0},{5,1},{6,2},{7,3},{8,12},{9,13},{10,... | collective-permute-start | bytes 983048 | tf_op jit(solution)/shard_map/ppermute | solution.py:376
  30.7 10.1 %collective-permute-start.7 = (bf16[2,64,1280]{2,1,0:T(8,128)(2,1)S(1)}, bf16[2,64,1280]{2,1,0:T(8,128)(2,1)S(1)}, u32[]{:S(2)}, u32[]{:S(2)}) collective-permute-start(bf16[2,64,1280]{2,1,0:T(8,128)(2,1)S(1)} %pad_maximum_fusion.17), channel_id=1, source_target_pairs={{0,2},{1,3},{2,0},{3,1},{4,6},{5,7},{6,4},{7,5},{8,10},{9,11},{10,... | collective-permute-start | bytes 983048 | tf_op jit(solution)/shard_map/ppermute | solution.py:376
  35.1 20.1 %collective-permute-start.5 = (bf16[2,16,6144]{2,1,0:T(8,128)(2,1)S(1)}, bf16[2,16,6144]{2,1,0:T(8,128)(2,1)S(1)}, u32[]{:S(2)}, u32[]{:S(2)}) collective-permute-start(bf16[2,16,6144]{2,1,0:T(8,128)(2,1)S(1)} %pad_maximum_fusion.13), channel_id=1, source_target_pairs={{0,8},{1,9},{2,10},{3,11},{4,12},{5,13},{6,14},{7,15},{8,0},{9,1},... | collective-permute-start | bytes 1179656 | tf_op jit(solution)/shard_map/ppermute | solution.py:376
  38.5 21.3 %collective-permute-start.2 = (bf16[2,64,2304]{2,1,0:T(8,128)(2,1)S(1)}, bf16[2,64,2304]{2,1,0:T(8,128)(2,1)S(1)}, u32[]{:S(2)}, u32[]{:S(2)}) collective-permute-start(bf16[2,64,2304]{2,1,0:T(8,128)(2,1)S(1)} %pad_maximum_fusion.10), channel_id=1, source_target_pairs={{0,4},{1,5},{2,6},{3,7},{4,0},{5,1},{6,2},{7,3},{8,12},{9,13},{10,... | collective-permute-start | bytes 1769480 | tf_op jit(solution)/shard_map/ppermute | solution.py:376
  40.3 19.6 %collective-permute-start.6 = (bf16[2,64,2560]{2,1,0:T(8,128)(2,1)S(1)}, bf16[2,64,2560]{2,1,0:T(8,128)(2,1)S(1)}, u32[]{:S(2)}, u32[]{:S(2)}) collective-permute-start(bf16[2,64,2560]{2,1,0:T(8,128)(2,1)S(1)} %pad_maximum_fusion.6), channel_id=1, source_target_pairs={{0,1},{1,0},{2,3},{3,2},{4,5},{5,4},{6,7},{7,6},{8,9},{9,8},{10,11... | collective-permute-start | bytes 1966088 | tf_op jit(solution)/shard_map/ppermute | solution.py:376
  61.0 5.4 %collective-permute-start.12 = (bf16[2,32,1280]{2,1,0:T(8,128)(2,1)S(1)}, bf16[2,32,1280]{2,1,0:T(8,128)(2,1)S(1)}, u32[]{:S(2)}, u32[]{:S(2)}) collective-permute-start(bf16[2,32,1280]{2,1,0:T(8,128)(2,1)S(1)} %slice.123), channel_id=1, source_target_pairs={{0,1},{1,0},{2,3},{3,2},{4,5},{5,4},{6,7},{7,6},{8,9},{9,8},{10,11... | collective-permute-start | bytes 491528 | tf_op jit(solution)/shard_map/ppermute | solution.py:376
  61.7 9.6 %collective-permute-start.8 = (bf16[2,32,2304]{2,1,0:T(8,128)(2,1)S(1)}, bf16[2,32,2304]{2,1,0:T(8,128)(2,1)S(1)}, u32[]{:S(2)}, u32[]{:S(2)}) collective-permute-start(bf16[2,32,2304]{2,1,0:T(8,128)(2,1)S(1)} %slice.121), channel_id=1, source_target_pairs={{0,2},{1,3},{2,0},{3,1},{4,6},{5,7},{6,4},{7,5},{8,10},{9,11},{10,... | collective-permute-start | bytes 884744 | tf_op jit(solution)/shard_map/ppermute | solution.py:376
  62.3 10.2 %collective-permute-start.10 = (bf16[2,32,2560]{2,1,0:T(8,128)(2,1)S(1)}, bf16[2,32,2560]{2,1,0:T(8,128)(2,1)S(1)}, u32[]{:S(2)}, u32[]{:S(2)}) collective-permute-start(bf16[2,32,2560]{2,1,0:T(8,128)(2,1)S(1)} %slice.122), channel_id=1, source_target_pairs={{0,4},{1,5},{2,6},{3,7},{4,0},{5,1},{6,2},{7,3},{8,12},{9,13},{10,... | collective-permute-start | bytes 983048 | tf_op jit(solution)/shard_map/ppermute | solution.py:376
  66.5 9.0 %collective-permute-start.13 = (bf16[2,64,1280]{2,1,0:T(8,128)(2,1)S(1)}, bf16[2,64,1280]{2,1,0:T(8,128)(2,1)S(1)}, u32[]{:S(2)}, u32[]{:S(2)}) collective-permute-start(bf16[2,64,1280]{2,1,0:T(8,128)(2,1)S(1)} %pad_maximum_fusion.18), channel_id=1, source_target_pairs={{0,2},{1,3},{2,0},{3,1},{4,6},{5,7},{6,4},{7,5},{8,10},{9,11},{10,... | collective-permute-start | bytes 983048 | tf_op jit(solution)/shard_map/ppermute | solution.py:376
  71.3 10.7 %collective-permute-start.9 = (bf16[2,64,2304]{2,1,0:T(8,128)(2,1)S(1)}, bf16[2,64,2304]{2,1,0:T(8,128)(2,1)S(1)}, u32[]{:S(2)}, u32[]{:S(2)}) collective-permute-start(bf16[2,64,2304]{2,1,0:T(8,128)(2,1)S(1)} %pad_maximum_fusion.11), channel_id=1, source_target_pairs={{0,4},{1,5},{2,6},{3,7},{4,0},{5,1},{6,2},{7,3},{8,12},{9,13},{10,... | collective-permute-start | bytes 1769480 | tf_op jit(solution)/shard_map/ppermute | solution.py:376
  72.5 10.8 %collective-permute-start.11 = (bf16[2,64,2560]{2,1,0:T(8,128)(2,1)S(1)}, bf16[2,64,2560]{2,1,0:T(8,128)(2,1)S(1)}, u32[]{:S(2)}, u32[]{:S(2)}) collective-permute-start(bf16[2,64,2560]{2,1,0:T(8,128)(2,1)S(1)} %pad_maximum_fusion.8), channel_id=1, source_target_pairs={{0,1},{1,0},{2,3},{3,2},{4,5},{5,4},{6,7},{7,6},{8,9},{9,8},{10,11... | collective-permute-start | bytes 1966088 | tf_op jit(solution)/shard_map/ppermute | solution.py:376
  83.2 6.5 %copy-start.3 = (s32[48,12]{0,1:T(8,128)S(1)}, s32[48,12]{0,1:T(8,128)}, u32[]{:S(2)}) copy-start(s32[48,12]{0,1:T(8,128)} %param.10) | copy-start | bytes 6916
  83.2 33.3 %copy-start.2 = (s32[12,48]{1,0:T(8,128)S(1)}, s32[12,48]{1,0:T(8,128)}, u32[]{:S(2)}) copy-start(s32[12,48]{1,0:T(8,128)} %pattern.5) | copy-start | bytes 6916
  84.4 32.0 %collective-permute-start.15 = (bf16[2,128,2560]{2,1,0:T(8,128)(2,1)}, bf16[2,128,2560]{2,1,0:T(8,128)(2,1)}, u32[]{:S(2)}, u32[]{:S(2)}) collective-permute-start(bf16[2,128,2560]{2,1,0:T(8,128)(2,1)} %pad_maximum_fusion.refs_2_), channel_id=1, source_target_pairs={{0,2},{1,3},{2,0},{3,1},{4,6},{5,7},{6,4},{7,5},{8,10},{9,11},{10,... | collective-permute-start | bytes 3932168 | tf_op jit(solution)/shard_map/ppermute | solution.py:376
  85.9 29.0 %collective-permute-start.14 = (bf16[2,128,2304]{2,1,0:T(8,128)(2,1)S(1)}, bf16[2,128,2304]{2,1,0:T(8,128)(2,1)}, u32[]{:S(2)}, u32[]{:S(2)}) collective-permute-start(bf16[2,128,2304]{2,1,0:T(8,128)(2,1)S(1)} %pad_maximum_fusion.2.refs_0_), channel_id=1, source_target_pairs={{0,1},{1,0},{2,3},{3,2},{4,5},{5,4},{6,7},{7,6},{8,9},{9,8},{10,11... | collective-permute-start | bytes 3538952 | tf_op jit(solution)/shard_map/ppermute | solution.py:376
  87.6 11.1 %collective-permute-start.16 = (bf16[2,128,1280]{2,1,0:T(8,128)(2,1)S(1)}, bf16[2,128,1280]{2,1,0:T(8,128)(2,1)S(1)}, u32[]{:S(2)}, u32[]{:S(2)}) collective-permute-start(bf16[2,128,1280]{2,1,0:T(8,128)(2,1)S(1)} %pad_maximum_fusion.7.refs_4_), channel_id=1, source_target_pairs={{0,4},{1,5},{2,6},{3,7},{4,0},{5,1},{6,2},{7,3},{8,12},{9,13},{10,... | collective-permute-start | bytes 1966088 | tf_op jit(solution)/shard_map/ppermute | solution.py:376
  88.7 50.0 %collective-permute-start.19 = (bf16[2,128,2560]{2,1,0:T(8,128)(2,1)}, bf16[2,128,2560]{2,1,0:T(8,128)(2,1)}, u32[]{:S(2)}, u32[]{:S(2)}) collective-permute-start(bf16[2,128,2560]{2,1,0:T(8,128)(2,1)} %pad_maximum_fusion.1.refs_9_.refs_2_), channel_id=1, source_target_pairs={{0,2},{1,3},{2,0},{3,1},{4,6},{5,7},{6,4},{7,5},{8,10},{9,11},{10,... | collective-permute-start | bytes 3932168 | tf_op jit(solution)/shard_map/ppermute | solution.py:376
  89.2 48.8 %collective-permute-start.18 = (bf16[2,128,2304]{2,1,0:T(8,128)(2,1)}, bf16[2,128,2304]{2,1,0:T(8,128)(2,1)}, u32[]{:S(2)}, u32[]{:S(2)}) collective-permute-start(bf16[2,128,2304]{2,1,0:T(8,128)(2,1)} %pad_maximum_fusion.3.refs_8_.refs_0_), channel_id=1, source_target_pairs={{0,1},{1,0},{2,3},{3,2},{4,5},{5,4},{6,7},{7,6},{8,9},{9,8},{10,11... | collective-permute-start | bytes 3538952 | tf_op jit(solution)/shard_map/ppermute | solution.py:376
  136.2 2.5 collective-permute-start.20
  136.3 3.4 %collective-permute-start.17 = (bf16[256,1536]{1,0:T(8,128)(2,1)S(1)}, bf16[256,1536]{1,0:T(8,128)(2,1)S(1)}, u32[]{:S(2)}, u32[]{:S(2)}) collective-permute-start(bf16[256,1536]{1,0:T(8,128)(2,1)S(1)} %get-tuple-element.53), channel_id=1, source_target_pairs={{0,16},{16,0},{1,17},{17,1},{2,18},{18,2},{3,19},{19,3},{4,20},{20... | collective-permute-start | bytes 2359304 | tf_op jit(solution)/shard_map/ppermute | solution.py:384
  136.8 20.0 %collective-permute-start.22 = (bf16[2,128,1280]{2,1,0:T(8,128)(2,1)S(1)}, bf16[2,128,1280]{2,1,0:T(8,128)(2,1)S(1)}, u32[]{:S(2)}, u32[]{:S(2)}) collective-permute-start(bf16[2,128,1280]{2,1,0:T(8,128)(2,1)S(1)} %pad_maximum_fusion.9.refs_10_.refs_4_), channel_id=1, source_target_pairs={{0,4},{1,5},{2,6},{3,7},{4,0},{5,1},{6,2},{7,3},{8,12},{9,13},{10,... | collective-permute-start | bytes 1966088 | tf_op jit(solution)/shard_map/ppermute | solution.py:376
  152.4 24.5 %collective-permute-start.29 = (bf16[128,1280]{1,0:T(8,128)(2,1)S(1)}, bf16[128,1280]{1,0:T(8,128)(2,1)S(1)}, u32[]{:S(2)}, u32[]{:S(2)}) collective-permute-start(bf16[128,1280]{1,0:T(8,128)(2,1)S(1)} %get-tuple-element.62.refs_13_), channel_id=1, source_target_pairs={{0,4},{1,5},{2,6},{3,7},{4,0},{5,1},{6,2},{7,3},{8,12},{9,13},{10,... | collective-permute-start | bytes 983048 | tf_op jit(solution)/shard_map/ppermute | solution.py:376
  153.8 23.8 %collective-permute-start.21 = (bf16[128,2304]{1,0:T(8,128)(2,1)S(1)}, bf16[128,2304]{1,0:T(8,128)(2,1)S(1)}, u32[]{:S(2)}, u32[]{:S(2)}) collective-permute-start(bf16[128,2304]{1,0:T(8,128)(2,1)S(1)} %get-tuple-element.58.refs_9_), channel_id=1, source_target_pairs={{0,1},{1,0},{2,3},{3,2},{4,5},{5,4},{6,7},{7,6},{8,9},{9,8},{10,11... | collective-permute-start | bytes 1769480 | tf_op jit(solution)/shard_map/ppermute | solution.py:376
  155.3 24.1 %collective-permute-start.27 = (bf16[128,2560]{1,0:T(8,128)(2,1)S(1)}, bf16[128,2560]{1,0:T(8,128)(2,1)S(1)}, u32[]{:S(2)}, u32[]{:S(2)}) collective-permute-start(bf16[128,2560]{1,0:T(8,128)(2,1)S(1)} %get-tuple-element.60.refs_11_), channel_id=1, source_target_pairs={{0,2},{1,3},{2,0},{3,1},{4,6},{5,7},{6,4},{7,5},{8,10},{9,11},{10,... | collective-permute-start | bytes 1966088 | tf_op jit(solution)/shard_map/ppermute | solution.py:376
  176.4 3.2 %collective-permute-start.25 = (bf16[256,1536]{1,0:T(8,128)(2,1)S(1)}, bf16[256,1536]{1,0:T(8,128)(2,1)S(1)}, u32[]{:S(2)}, u32[]{:S(2)}) collective-permute-start(bf16[256,1536]{1,0:T(8,128)(2,1)S(1)} %get-tuple-element.65), channel_id=1, source_target_pairs={{0,16},{16,0},{1,17},{17,1},{2,18},{18,2},{3,19},{19,3},{4,20},{20... | collective-permute-start | bytes 2359304 | tf_op jit(solution)/shard_map/ppermute | solution.py:384
  176.5 3.4 %collective-permute-start.24 = (bf16[256,1536]{1,0:T(8,128)(2,1)S(1)}, bf16[256,1536]{1,0:T(8,128)(2,1)S(1)}, u32[]{:S(2)}, u32[]{:S(2)}) collective-permute-start(bf16[256,1536]{1,0:T(8,128)(2,1)S(1)} %get-tuple-element.63), channel_id=1, source_target_pairs={{0,16},{16,0},{1,17},{17,1},{2,18},{18,2},{3,19},{19,3},{4,20},{20... | collective-permute-start | bytes 2359304 | tf_op jit(solution)/shard_map/ppermute | solution.py:384
  177.1 6.2 %collective-permute-start.30 = (bf16[64,1280]{1,0:T(8,128)(2,1)S(1)}, bf16[64,1280]{1,0:T(8,128)(2,1)S(1)}, u32[]{:S(2)}, u32[]{:S(2)}) collective-permute-start(bf16[64,1280]{1,0:T(8,128)(2,1)S(1)} %slice.161), channel_id=1, source_target_pairs={{0,2},{1,3},{2,0},{3,1},{4,6},{5,7},{6,4},{7,5},{8,10},{9,11},{10,... | collective-permute-start | bytes 491528 | tf_op jit(solution)/shard_map/ppermute | solution.py:376
  177.8 8.8 %collective-permute-start.23 = (bf16[64,2304]{1,0:T(8,128)(2,1)S(1)}, bf16[64,2304]{1,0:T(8,128)(2,1)S(1)}, u32[]{:S(2)}, u32[]{:S(2)}) collective-permute-start(bf16[64,2304]{1,0:T(8,128)(2,1)S(1)} %slice.155), channel_id=1, source_target_pairs={{0,4},{1,5},{2,6},{3,7},{4,0},{5,1},{6,2},{7,3},{8,12},{9,13},{10,... | collective-permute-start | bytes 884744 | tf_op jit(solution)/shard_map/ppermute | solution.py:376
  179.5 10.1 %collective-permute-start.28 = (bf16[64,2560]{1,0:T(8,128)(2,1)S(1)}, bf16[64,2560]{1,0:T(8,128)(2,1)S(1)}, u32[]{:S(2)}, u32[]{:S(2)}) collective-permute-start(bf16[64,2560]{1,0:T(8,128)(2,1)S(1)} %slice.159), channel_id=1, source_target_pairs={{0,1},{1,0},{2,3},{3,2},{4,5},{5,4},{6,7},{7,6},{8,9},{9,8},{10,11... | collective-permute-start | bytes 983048 | tf_op jit(solution)/shard_map/ppermute | solution.py:376
  183.4 32.4 %collective-permute-start.32 = (bf16[32,1280]{1,0:T(8,128)(2,1)S(1)}, bf16[32,1280]{1,0:T(8,128)(2,1)S(1)}, u32[]{:S(2)}, u32[]{:S(2)}) collective-permute-start(bf16[32,1280]{1,0:T(8,128)(2,1)S(1)} %slice.165), channel_id=1, source_target_pairs={{0,1},{1,0},{2,3},{3,2},{4,5},{5,4},{6,7},{7,6},{8,9},{9,8},{10,11... | collective-permute-start | bytes 245768 | tf_op jit(solution)/shard_map/ppermute | solution.py:376
  186.6 41.1 %collective-permute-start.26 = (bf16[32,2304]{1,0:T(8,128)(2,1)S(1)}, bf16[32,2304]{1,0:T(8,128)(2,1)S(1)}, u32[]{:S(2)}, u32[]{:S(2)}) collective-permute-start(bf16[32,2304]{1,0:T(8,128)(2,1)S(1)} %slice.157), channel_id=1, source_target_pairs={{0,2},{1,3},{2,0},{3,1},{4,6},{5,7},{6,4},{7,5},{8,10},{9,11},{10,... | collective-permute-start | bytes 442376 | tf_op jit(solution)/shard_map/ppermute | solution.py:376
  189.6 14.9 %slice-start = ((s8[6291456]{0:T(1024)(128)(4,1)}), s8[4194304]{0:T(1024)(128)(4,1)S(1)}, s32[]{:S(2)}) async-start(s8[6291456]{0:T(1024)(128)(4,1)} %bitcast.8), calls=%async_computation | async-start | bytes 8388608
  189.7 14.9 %slice-start.1 = ((s8[6291456]{0:T(1024)(128)(4,1)}), s8[2097152]{0:T(1024)(128)(4,1)S(1)}, s32[]{:S(2)}) async-start(s8[6291456]{0:T(1024)(128)(4,1)} %bitcast.8), calls=%async_computation.1 | async-start | bytes 4194304
  201.9 26.1 %collective-permute-start.34 = (bf16[128,2304]{1,0:T(8,128)(2,1)S(1)}, bf16[128,2304]{1,0:T(8,128)(2,1)S(1)}, u32[]{:S(2)}, u32[]{:S(2)}) collective-permute-start(bf16[128,2304]{1,0:T(8,128)(2,1)S(1)} %get-tuple-element.74.refs_5_), channel_id=1, source_target_pairs={{0,1},{1,0},{2,3},{3,2},{4,5},{5,4},{6,7},{7,6},{8,9},{9,8},{10,11... | collective-permute-start | bytes 1769480 | tf_op jit(solution)/shard_map/ppermute | solution.py:376
  202.3 25.9 %collective-permute-start.35 = (bf16[128,2560]{1,0:T(8,128)(2,1)S(1)}, bf16[128,2560]{1,0:T(8,128)(2,1)S(1)}, u32[]{:S(2)}, u32[]{:S(2)}) collective-permute-start(bf16[128,2560]{1,0:T(8,128)(2,1)S(1)} %get-tuple-element.76.refs_7_), channel_id=1, source_target_pairs={{0,2},{1,3},{2,0},{3,1},{4,6},{5,7},{6,4},{7,5},{8,10},{9,11},{10,... | collective-permute-start | bytes 1966088 | tf_op jit(solution)/shard_map/ppermute | solution.py:376
  203.3 24.6 %collective-permute-start.36 = (bf16[128,1280]{1,0:T(8,128)(2,1)S(1)}, bf16[128,1280]{1,0:T(8,128)(2,1)S(1)}, u32[]{:S(2)}, u32[]{:S(2)}) collective-permute-start(bf16[128,1280]{1,0:T(8,128)(2,1)S(1)} %get-tuple-element.78.refs_9_), channel_id=1, source_target_pairs={{0,4},{1,5},{2,6},{3,7},{4,0},{5,1},{6,2},{7,3},{8,12},{9,13},{10,... | collective-permute-start | bytes 983048 | tf_op jit(solution)/shard_map/ppermute | solution.py:376
  215.8 12.0 %collective-permute-start.31 = (bf16[32,2560]{1,0:T(8,128)(2,1)S(1)}, bf16[32,2560]{1,0:T(8,128)(2,1)S(1)}, u32[]{:S(2)}, u32[]{:S(2)}) collective-permute-start(bf16[32,2560]{1,0:T(8,128)(2,1)S(1)} %slice.163), channel_id=1, source_target_pairs={{0,4},{1,5},{2,6},{3,7},{4,0},{5,1},{6,2},{7,3},{8,12},{9,13},{10,... | collective-permute-start | bytes 491528 | tf_op jit(solution)/shard_map/ppermute | solution.py:376
  228.4 13.8 %collective-permute-start.39 = (bf16[64,1280]{1,0:T(8,128)(2,1)S(1)}, bf16[64,1280]{1,0:T(8,128)(2,1)S(1)}, u32[]{:S(2)}, u32[]{:S(2)}) collective-permute-start(bf16[64,1280]{1,0:T(8,128)(2,1)S(1)} %slice.143), channel_id=1, source_target_pairs={{0,2},{1,3},{2,0},{3,1},{4,6},{5,7},{6,4},{7,5},{8,10},{9,11},{10,... | collective-permute-start | bytes 491528 | tf_op jit(solution)/shard_map/ppermute | solution.py:376
  229.5 13.3 %collective-permute-start.33 = (bf16[16,6144]{1,0:T(8,128)(2,1)S(1)}, bf16[16,6144]{1,0:T(8,128)(2,1)S(1)}, u32[]{:S(2)}, u32[]{:S(2)}) collective-permute-start(bf16[16,6144]{1,0:T(8,128)(2,1)S(1)} %slice.167), channel_id=1, source_target_pairs={{0,8},{1,9},{2,10},{3,11},{4,12},{5,13},{6,14},{7,15},{8,0},{9,1},... | collective-permute-start | bytes 589832 | tf_op jit(solution)/shard_map/ppermute | solution.py:376
  231.6 10.7 %collective-permute-start.37 = (bf16[64,2304]{1,0:T(8,128)(2,1)S(1)}, bf16[64,2304]{1,0:T(8,128)(2,1)S(1)}, u32[]{:S(2)}, u32[]{:S(2)}) collective-permute-start(bf16[64,2304]{1,0:T(8,128)(2,1)S(1)} %slice.139), channel_id=1, source_target_pairs={{0,4},{1,5},{2,6},{3,7},{4,0},{5,1},{6,2},{7,3},{8,12},{9,13},{10,... | collective-permute-start | bytes 884744 | tf_op jit(solution)/shard_map/ppermute | solution.py:376
  232.0 10.3 %collective-permute-start.38 = (bf16[64,2560]{1,0:T(8,128)(2,1)S(1)}, bf16[64,2560]{1,0:T(8,128)(2,1)S(1)}, u32[]{:S(2)}, u32[]{:S(2)}) collective-permute-start(bf16[64,2560]{1,0:T(8,128)(2,1)S(1)} %slice.141), channel_id=1, source_target_pairs={{0,1},{1,0},{2,3},{3,2},{4,5},{5,4},{6,7},{7,6},{8,9},{9,8},{10,11... | collective-permute-start | bytes 983048 | tf_op jit(solution)/shard_map/ppermute | solution.py:376
  242.4 4.5 %collective-permute-start.42 = (bf16[32,1280]{1,0:T(8,128)(2,1)S(1)}, bf16[32,1280]{1,0:T(8,128)(2,1)S(1)}, u32[]{:S(2)}, u32[]{:S(2)}) collective-permute-start(bf16[32,1280]{1,0:T(8,128)(2,1)S(1)} %slice.149), channel_id=1, source_target_pairs={{0,1},{1,0},{2,3},{3,2},{4,5},{5,4},{6,7},{7,6},{8,9},{9,8},{10,11... | collective-permute-start | bytes 245768 | tf_op jit(solution)/shard_map/ppermute | solution.py:376
  242.8 7.1 %collective-permute-start.41 = (bf16[32,2560]{1,0:T(8,128)(2,1)S(1)}, bf16[32,2560]{1,0:T(8,128)(2,1)S(1)}, u32[]{:S(2)}, u32[]{:S(2)}) collective-permute-start(bf16[32,2560]{1,0:T(8,128)(2,1)S(1)} %slice.147), channel_id=1, source_target_pairs={{0,4},{1,5},{2,6},{3,7},{4,0},{5,1},{6,2},{7,3},{8,12},{9,13},{10,... | collective-permute-start | bytes 491528 | tf_op jit(solution)/shard_map/ppermute | solution.py:376
  244.6 5.2 %collective-permute-start.40 = (bf16[32,2304]{1,0:T(8,128)(2,1)S(1)}, bf16[32,2304]{1,0:T(8,128)(2,1)S(1)}, u32[]{:S(2)}, u32[]{:S(2)}) collective-permute-start(bf16[32,2304]{1,0:T(8,128)(2,1)S(1)} %slice.145), channel_id=1, source_target_pairs={{0,2},{1,3},{2,0},{3,1},{4,6},{5,7},{6,4},{7,5},{8,10},{9,11},{10,... | collective-permute-start | bytes 442376 | tf_op jit(solution)/shard_map/ppermute | solution.py:376
  250.0 9.2 %collective-permute-start.43 = (bf16[16,6144]{1,0:T(8,128)(2,1)S(1)}, bf16[16,6144]{1,0:T(8,128)(2,1)S(1)}, u32[]{:S(2)}, u32[]{:S(2)}) collective-permute-start(bf16[16,6144]{1,0:T(8,128)(2,1)S(1)} %slice.169), channel_id=1, source_target_pairs={{0,8},{1,9},{2,10},{3,11},{4,12},{5,13},{6,14},{7,15},{8,0},{9,1},... | collective-permute-start | bytes 589832 | tf_op jit(solution)/shard_map/ppermute | solution.py:376
  (2 other events, 5.6 us)

commit v5 on v4

--- a/solution.py
+++ b/solution.py
@@ -336,7 +336,7 @@
                 ),
                 out_shape=jax.ShapeDtypeStruct((tall, broad), jnp.bfloat16),
                 input_output_aliases=aliases,
-                compiler_params=pltpu.CompilerParams(vmem_limit_bytes=32 * 1024 * 1024),
+                compiler_params=pltpu.CompilerParams(vmem_limit_bytes=48 * 1024 * 1024),
                 cost_estimate=pl.CostEstimate(
                     flops=tall * broad // shares,
                     bytes_accessed=tokens * broad // shares,

time: 260 us -> 259 us (level)
  local copies, waits for them, and re-layouts: 7.25 us -> 1.67 us
  Pallas kernels: 96.5 us -> 100 us
    unnamed x13 -> x5, local copies, waits for them, and re-layouts: 5.68 us -> 0.1 us
    pallas_call x4, Pallas kernels: 33.3 us -> 37.7 us  [call(): pl.pallas_call(functools.partial(grad_kernel, block, factor, (off[0] * ti...]
  transfers between devices with their start and end apart: 44 -> 44, of which waited for: 22 -> 22; matrix products, arithmetic and copies ran while one was open for 2% -> 2% of each run, Pallas kernels for 37% -> 39%
where the time goes in v5:
time: 259 us; the launch traced here: 258 us
  Pallas kernels  100 us (39%)
  waiting for transfers between devices  97.1 us (37%)
  starting transfers between devices  49.7 us (19%)
  other arithmetic  8.34 us (3%)
    ppermute x40, waiting for transfers between devices, swap(): return lax.ppermute(value, 'col', [(i, i ^ 1 << bit) for i in range(n)])  95.9 us
    ppermute x40, starting transfers between devices, swap(): return lax.ppermute(value, 'col', [(i, i ^ 1 << bit) for i in range(n)])  48.6 us
    pallas_call x2, Pallas kernels, forward(): pl.pallas_call(functools.partial(forward_kernel, moves, block), in_specs=...  39.3 us
    pallas_call x4, Pallas kernels, call(): pl.pallas_call(functools.partial(grad_kernel, block, factor, (off[0] * ti...  37.7 us
    pallas_call x2, Pallas kernels, backward(): pl.pallas_call(functools.partial(backward_kernel, parts, block), in_specs...  23.4 us
  transfers between devices with their start and end apart: 44, of which 22 were waited for; matrix products, arithmetic and copies ran while one was open for 2% of the time, Pallas kernels for 39%

profile of v5, /device:TPU:0, one launch (start us, length us, event | category | flops | bytes accessed | tf_op | source)
XLA Modules:
  0.0 258.3 jit_solution(3340010175465407819)
XLA Ops:
  0.6 1.3 slice_bitcast_fusion.2
  2.0 4.1 %collective-permute-start = (bf16[2,16,6144]{2,1,0:T(8,128)(2,1)S(1)}, bf16[2,16,6144]{2,1,0:T(8,128)(2,1)S(1)}, u32[]{:S(2)}, u32[]{:S(2)}) collective-permute-start(bf16[2,16,6144]{2,1,0:T(8,128)(2,1)S(1)} %pad_maximum_fusion.12), channel_id=1, source_target_pairs={{0,8},{1,9},{2,10},{3,11},{4,12},{5,13},{6,14},{7,15},{8,0},{9,1},... | collective-permute-start | bytes 1179656 | tf_op jit(solution)/shard_map/ppermute | solution.py:376
  6.1 17.5 %collective-permute-done = bf16[2,16,6144]{2,1,0:T(8,128)(2,1)S(1)} collective-permute-done((bf16[2,16,6144]{2,1,0:T(8,128)(2,1)S(1)}, bf16[2,16,6144]{2,1,0:T(8,128)(2,1)S(1)}, u32[]{:S(2)}, u32[]{:S(2)}) %collective-permute-start) | collective-permute-done | bytes 393248 | tf_op jit(solution)/shard_map/ppermute | solution.py:376
  23.7 1.6 collective-permute-start.1
  25.3 1.6 collective-permute-start.4
  27.7 3.0 %collective-permute-done.4 = bf16[2,32,1280]{2,1,0:T(8,128)(2,1)S(1)} collective-permute-done((bf16[2,32,1280]{2,1,0:T(8,128)(2,1)S(1)}, bf16[2,32,1280]{2,1,0:T(8,128)(2,1)S(1)}, u32[]{:S(2)}, u32[]{:S(2)}) %collective-permute-start.4) | collective-permute-done | bytes 163872 | tf_op jit(solution)/shard_map/ppermute | solution.py:376
  31.3 1.3 collective-permute-done.1
  32.6 2.5 collective-permute-done.3
  35.1 3.4 %collective-permute-start.5 = (bf16[2,16,6144]{2,1,0:T(8,128)(2,1)S(1)}, bf16[2,16,6144]{2,1,0:T(8,128)(2,1)S(1)}, u32[]{:S(2)}, u32[]{:S(2)}) collective-permute-start(bf16[2,16,6144]{2,1,0:T(8,128)(2,1)S(1)} %pad_maximum_fusion.13), channel_id=1, source_target_pairs={{0,8},{1,9},{2,10},{3,11},{4,12},{5,13},{6,14},{7,15},{8,0},{9,1},... | collective-permute-start | bytes 1179656 | tf_op jit(solution)/shard_map/ppermute | solution.py:376
  38.5 1.7 collective-permute-start.2
  40.9 14.3 %collective-permute-done.5 = bf16[2,16,6144]{2,1,0:T(8,128)(2,1)S(1)} collective-permute-done((bf16[2,16,6144]{2,1,0:T(8,128)(2,1)S(1)}, bf16[2,16,6144]{2,1,0:T(8,128)(2,1)S(1)}, u32[]{:S(2)}, u32[]{:S(2)}) %collective-permute-start.5) | collective-permute-done | bytes 393248 | tf_op jit(solution)/shard_map/ppermute | solution.py:376
  55.2 4.5 %collective-permute-done.2 = bf16[2,64,2304]{2,1,0:T(8,128)(2,1)S(1)} collective-permute-done((bf16[2,64,2304]{2,1,0:T(8,128)(2,1)S(1)}, bf16[2,64,2304]{2,1,0:T(8,128)(2,1)S(1)}, u32[]{:S(2)}, u32[]{:S(2)}) %collective-permute-start.2) | collective-permute-done | bytes 589856 | tf_op jit(solution)/shard_map/ppermute | solution.py:376
  59.9 1.1 pad_maximum_fusion.refs_2_
  62.3 1.4 collective-permute-start.10
  63.6 2.8 %collective-permute-done.12 = bf16[2,32,1280]{2,1,0:T(8,128)(2,1)S(1)} collective-permute-done((bf16[2,32,1280]{2,1,0:T(8,128)(2,1)S(1)}, bf16[2,32,1280]{2,1,0:T(8,128)(2,1)S(1)}, u32[]{:S(2)}, u32[]{:S(2)}) %collective-permute-start.12) | collective-permute-done | bytes 163872 | tf_op jit(solution)/shard_map/ppermute | solution.py:376
  67.0 4.3 %collective-permute-done.8 = bf16[2,32,2304]{2,1,0:T(8,128)(2,1)S(1)} collective-permute-done((bf16[2,32,2304]{2,1,0:T(8,128)(2,1)S(1)}, bf16[2,32,2304]{2,1,0:T(8,128)(2,1)S(1)}, u32[]{:S(2)}, u32[]{:S(2)}) %collective-permute-start.8) | collective-permute-done | bytes 294944 | tf_op jit(solution)/shard_map/ppermute | solution.py:376
  72.5 2.2 collective-permute-start.11
  75.5 6.5 %collective-permute-done.9 = bf16[2,64,2304]{2,1,0:T(8,128)(2,1)S(1)} collective-permute-done((bf16[2,64,2304]{2,1,0:T(8,128)(2,1)S(1)}, bf16[2,64,2304]{2,1,0:T(8,128)(2,1)S(1)}, u32[]{:S(2)}, u32[]{:S(2)}) %collective-permute-start.9) | collective-permute-done | bytes 589856 | tf_op jit(solution)/shard_map/ppermute | solution.py:376
  83.2 1.1 pad_maximum_fusion.1.refs_9_.refs_2_
  84.4 1.6 collective-permute-start.15
  86.0 1.7 collective-permute-start.14
  89.7 8.9 %collective-permute-done.16.refs_5_ = bf16[2,128,1280]{2,1,0:T(8,128)(2,1)S(1)} collective-permute-done((bf16[2,128,1280]{2,1,0:T(8,128)(2,1)S(1)}, bf16[2,128,1280]{2,1,0:T(8,128)(2,1)S(1)}, u32[]{:S(2)}, u32[]{:S(2)}) %collective-permute-start.16) | collective-permute-done | bytes 655392 | tf_op jit(solution)/shard_map/ppermute | solution.py:376
  98.7 16.3 %collective-permute-done.14.refs_1_ = bf16[2,128,2304]{2,1,0:T(8,128)(2,1)} collective-permute-done((bf16[2,128,2304]{2,1,0:T(8,128)(2,1)S(1)}, bf16[2,128,2304]{2,1,0:T(8,128)(2,1)}, u32[]{:S(2)}, u32[]{:S(2)}) %collective-permute-start.14) | collective-permute-done | bytes 1179680 | tf_op jit(solution)/shard_map/ppermute | solution.py:376
  115.0 1.5 collective-permute-done.15.refs_3_
  116.4 19.7 %forward.2 = (bf16[2,256,6144]{2,1,0:T(8,128)(2,1)}, bf16[256,1536]{1,0:T(8,128)(2,1)S(1)}, bf16[256,1536]{1,0:T(8,128)(2,1)S(1)}) custom-call(s32[48,12]{1,0:T(8,128)S(1)} %copy.12.up_on.pattern, s32[12,48]{1,0:T(8,128)S(1)} %copy-done, bf16[2,128,2304]{2,1,0:T(8,128)(2,1)S(1)} %pad_maximum_fusion.2.refs_0_, ...), custom_call_target="tpu_custom_call" | custom-call | flops 1572864 | bytes 1572864 | tf_op jit(solution)/shard_map/forward/pallas_call | solution.py:174
  136.8 1.2 collective-permute-start.22
  140.7 11.7 %backward.2 = (bf16[128,2304]{1,0:T(8,128)(2,1)S(1)}, bf16[128,2304]{1,0:T(8,128)(2,1)S(1)}, bf16[128,2560]{1,0:T(8,128)(2,1)S(1)}, bf16[128,2560]{1,0:T(8,128)(...) custom-call(s32[48,12]{1,0:T(8,128)S(1)} %copy.12.up_on.pattern, ...), custom_call_target="tpu_custom_call" | custom-call | flops 1572864 | bytes 1572864 | tf_op jit(solution)/shard_map/backward/pallas_call | solution.py:250
  152.4 1.3 collective-permute-start.29
  153.7 1.5 collective-permute-start.21
  155.2 1.7 collective-permute-start.27
  156.9 19.5 %forward.3 = (bf16[2,256,6144]{2,1,0:T(8,128)(2,1)}, bf16[256,1536]{1,0:T(8,128)(2,1)S(1)}, bf16[256,1536]{1,0:T(8,128)(2,1)S(1)}) custom-call(s32[48,12]{1,0:T(8,128)S(1)} %copy.12.up_on.pattern, s32[12,48]{1,0:T(8,128)S(1)} %copy-done, bf16[2,128,2304]{2,1,0:T(8,128)(2,1)} %pad_maximum_fusion.3.refs_8_.refs_0_, ...), custom_call_target="tpu_custom_call" | custom-call | flops 1572864 | bytes 1572864 | tf_op jit(solution)/shard_map/forward/pallas_call | solution.py:174
  177.7 1.7 collective-permute-start.23
  180.9 2.4 collective-permute-done.30
  183.8 2.6 %collective-permute-done.23 = bf16[64,2304]{1,0:T(8,128)(2,1)S(1)} collective-permute-done((bf16[64,2304]{1,0:T(8,128)(2,1)S(1)}, bf16[64,2304]{1,0:T(8,128)(2,1)S(1)}, u32[]{:S(2)}, u32[]{:S(2)}) %collective-permute-start.23) | collective-permute-done | bytes 294944 | tf_op jit(solution)/shard_map/ppermute | solution.py:376
  186.5 1.8 collective-permute-start.26
  188.3 1.4 collective-permute-done.28
  189.8 11.7 %backward.3 = (bf16[128,2304]{1,0:T(8,128)(2,1)S(1)}, bf16[128,2304]{1,0:T(8,128)(2,1)S(1)}, bf16[128,2560]{1,0:T(8,128)(2,1)S(1)}, bf16[128,2560]{1,0:T(8,128)(...) custom-call(s32[48,12]{1,0:T(8,128)S(1)} %copy.12.up_on.pattern, ...), custom_call_target="tpu_custom_call" | custom-call | flops 1572864 | bytes 1572864 | tf_op jit(solution)/shard_map/backward/pallas_call | solution.py:250
  202.8 1.2 collective-permute-start.36
  204.0 9.5 %grad.4.refs_7_ = bf16[1536,6144]{1,0:T(8,128)(2,1)} custom-call(s32[12,48]{1,0:T(8,128)S(1)} %copy-done, bf16[256,1536]{1,0:T(8,128)(2,1)S(1)} %get-tuple-element.95.refs_0_, bf16[256,1536]{1,0:T(8,128)(2,1)S(1)} %get-tuple-element.93.refs_1_, bf16[2,256,6144]{2,1,0:T(8,128)(2,1)} %get-tuple-element.67.refs_2_.refs_0_, ...), custom_call_target="tpu_custom_call" | custom-call | flops 4718592 | bytes 1572864 | tf_op jit(solution)/shard_map/grad/pallas_call | solution.py:323
  214.4 9.5 %grad.5.refs_7_ = bf16[6144,1536]{1,0:T(8,128)(2,1)} custom-call(s32[48,12]{1,0:T(8,128)S(1)} %copy.12.up_on.pattern, bf16[2,256,6144]{2,1,0:T(8,128)(2,1)} %get-tuple-element.67.refs_2_.refs_0_, bf16[2,256,6144]{2,1,0:T(8,128)(2,1)} %get-tuple-element.68.refs_3_.refs_1_, bf16[256,1536]{1,0:T(8,128)(2,1)S(1)} %get-tuple-element.96.dhid_ref.refs_2_, ...), custom_call_target="tpu_custom_call" | custom-call | flops 4718592 | bytes 393216 | tf_op jit(solution)/shard_map/grad/pallas_call | solution.py:323
  224.5 1.1 collective-permute-start.39
  225.7 2.1 collective-permute-start.33
  228.1 1.8 collective-permute-start.38
  230.0 9.5 %grad.6 = bf16[6144,1536]{1,0:T(8,128)(2,1)} custom-call(s32[48,12]{1,0:T(8,128)S(1)} %copy.12.up_on.pattern, bf16[2,256,6144]{2,1,0:T(8,128)(2,1)} %get-tuple-element.67.refs_2_.refs_0_, bf16[2,256,6144]{2,1,0:T(8,128)(2,1)} %get-tuple-element.68.refs_3_.refs_1_, ...), custom_call_target="tpu_custom_call", output_to_operand_aliasing={{}: (8, {})} | custom-call | flops 4718592 | bytes 393216 | tf_op jit(solution)/shard_map/grad/pallas_call | solution.py:323
  240.1 1.8 collective-permute-start.41
  242.6 1.6 collective-permute-done.42
  244.2 2.8 %collective-permute-done.40 = bf16[32,2304]{1,0:T(8,128)(2,1)S(1)} collective-permute-done((bf16[32,2304]{1,0:T(8,128)(2,1)S(1)}, bf16[32,2304]{1,0:T(8,128)(2,1)S(1)}, u32[]{:S(2)}, u32[]{:S(2)}) %collective-permute-start.40) | collective-permute-done | bytes 147488 | tf_op jit(solution)/shard_map/ppermute | solution.py:376
  248.3 9.2 %grad.7 = bf16[1536,6144]{1,0:T(8,128)(2,1)} custom-call(s32[12,48]{1,0:T(8,128)S(1)} %copy-done, bf16[256,1536]{1,0:T(8,128)(2,1)S(1)} %get-tuple-element.95.refs_0_, bf16[256,1536]{1,0:T(8,128)(2,1)S(1)} %get-tuple-element.93.refs_1_, bf16[2,256,6144]{2,1,0:T(8,128)(2,1)} %get-tuple-element.67.refs_2_.refs_0_, ...), custom_call_target="tpu_custom_call", output_to_operand_aliasing={{}: (8, {})} | custom-call | flops 4718592 | bytes 1572864 | tf_op jit(solution)/shard_map/grad/pallas_call | solution.py:323
  (115 shorter events, 22.6 us)
Async XLA Ops:
  2.0 21.6 %collective-permute-start = (bf16[2,16,6144]{2,1,0:T(8,128)(2,1)S(1)}, bf16[2,16,6144]{2,1,0:T(8,128)(2,1)S(1)}, u32[]{:S(2)}, u32[]{:S(2)}) collective-permute-start(bf16[2,16,6144]{2,1,0:T(8,128)(2,1)S(1)} %pad_maximum_fusion.12), channel_id=1, source_target_pairs={{0,8},{1,9},{2,10},{3,11},{4,12},{5,13},{6,14},{7,15},{8,0},{9,1},... | collective-permute-start | bytes 1179656 | tf_op jit(solution)/shard_map/ppermute | solution.py:376
  23.7 8.9 %collective-permute-start.1 = (bf16[2,32,2304]{2,1,0:T(8,128)(2,1)S(1)}, bf16[2,32,2304]{2,1,0:T(8,128)(2,1)S(1)}, u32[]{:S(2)}, u32[]{:S(2)}) collective-permute-start(bf16[2,32,2304]{2,1,0:T(8,128)(2,1)S(1)} %slice.152), channel_id=1, source_target_pairs={{0,2},{1,3},{2,0},{3,1},{4,6},{5,7},{6,4},{7,5},{8,10},{9,11},{10,... | collective-permute-start | bytes 884744 | tf_op jit(solution)/shard_map/ppermute | solution.py:376
  25.3 5.4 %collective-permute-start.4 = (bf16[2,32,1280]{2,1,0:T(8,128)(2,1)S(1)}, bf16[2,32,1280]{2,1,0:T(8,128)(2,1)S(1)}, u32[]{:S(2)}, u32[]{:S(2)}) collective-permute-start(bf16[2,32,1280]{2,1,0:T(8,128)(2,1)S(1)} %pad_maximum_fusion.19), channel_id=1, source_target_pairs={{0,1},{1,0},{2,3},{3,2},{4,5},{5,4},{6,7},{7,6},{8,9},{9,8},{10,11... | collective-permute-start | bytes 491528 | tf_op jit(solution)/shard_map/ppermute | solution.py:376
  27.0 8.1 %collective-permute-start.3 = (bf16[2,32,2560]{2,1,0:T(8,128)(2,1)S(1)}, bf16[2,32,2560]{2,1,0:T(8,128)(2,1)S(1)}, u32[]{:S(2)}, u32[]{:S(2)}) collective-permute-start(bf16[2,32,2560]{2,1,0:T(8,128)(2,1)S(1)} %slice.153), channel_id=1, source_target_pairs={{0,4},{1,5},{2,6},{3,7},{4,0},{5,1},{6,2},{7,3},{8,12},{9,13},{10,... | collective-permute-start | bytes 983048 | tf_op jit(solution)/shard_map/ppermute | solution.py:376
  30.7 10.1 %collective-permute-start.7 = (bf16[2,64,1280]{2,1,0:T(8,128)(2,1)S(1)}, bf16[2,64,1280]{2,1,0:T(8,128)(2,1)S(1)}, u32[]{:S(2)}, u32[]{:S(2)}) collective-permute-start(bf16[2,64,1280]{2,1,0:T(8,128)(2,1)S(1)} %pad_maximum_fusion.17), channel_id=1, source_target_pairs={{0,2},{1,3},{2,0},{3,1},{4,6},{5,7},{6,4},{7,5},{8,10},{9,11},{10,... | collective-permute-start | bytes 983048 | tf_op jit(solution)/shard_map/ppermute | solution.py:376
  35.1 20.1 %collective-permute-start.5 = (bf16[2,16,6144]{2,1,0:T(8,128)(2,1)S(1)}, bf16[2,16,6144]{2,1,0:T(8,128)(2,1)S(1)}, u32[]{:S(2)}, u32[]{:S(2)}) collective-permute-start(bf16[2,16,6144]{2,1,0:T(8,128)(2,1)S(1)} %pad_maximum_fusion.13), channel_id=1, source_target_pairs={{0,8},{1,9},{2,10},{3,11},{4,12},{5,13},{6,14},{7,15},{8,0},{9,1},... | collective-permute-start | bytes 1179656 | tf_op jit(solution)/shard_map/ppermute | solution.py:376
  38.5 21.3 %collective-permute-start.2 = (bf16[2,64,2304]{2,1,0:T(8,128)(2,1)S(1)}, bf16[2,64,2304]{2,1,0:T(8,128)(2,1)S(1)}, u32[]{:S(2)}, u32[]{:S(2)}) collective-permute-start(bf16[2,64,2304]{2,1,0:T(8,128)(2,1)S(1)} %pad_maximum_fusion.10), channel_id=1, source_target_pairs={{0,4},{1,5},{2,6},{3,7},{4,0},{5,1},{6,2},{7,3},{8,12},{9,13},{10,... | collective-permute-start | bytes 1769480 | tf_op jit(solution)/shard_map/ppermute | solution.py:376
  40.3 19.6 %collective-permute-start.6 = (bf16[2,64,2560]{2,1,0:T(8,128)(2,1)S(1)}, bf16[2,64,2560]{2,1,0:T(8,128)(2,1)S(1)}, u32[]{:S(2)}, u32[]{:S(2)}) collective-permute-start(bf16[2,64,2560]{2,1,0:T(8,128)(2,1)S(1)} %pad_maximum_fusion.6), channel_id=1, source_target_pairs={{0,1},{1,0},{2,3},{3,2},{4,5},{5,4},{6,7},{7,6},{8,9},{9,8},{10,11... | collective-permute-start | bytes 1966088 | tf_op jit(solution)/shard_map/ppermute | solution.py:376
  61.0 5.4 %collective-permute-start.12 = (bf16[2,32,1280]{2,1,0:T(8,128)(2,1)S(1)}, bf16[2,32,1280]{2,1,0:T(8,128)(2,1)S(1)}, u32[]{:S(2)}, u32[]{:S(2)}) collective-permute-start(bf16[2,32,1280]{2,1,0:T(8,128)(2,1)S(1)} %slice.123), channel_id=1, source_target_pairs={{0,1},{1,0},{2,3},{3,2},{4,5},{5,4},{6,7},{7,6},{8,9},{9,8},{10,11... | collective-permute-start | bytes 491528 | tf_op jit(solution)/shard_map/ppermute | solution.py:376
  61.7 9.6 %collective-permute-start.8 = (bf16[2,32,2304]{2,1,0:T(8,128)(2,1)S(1)}, bf16[2,32,2304]{2,1,0:T(8,128)(2,1)S(1)}, u32[]{:S(2)}, u32[]{:S(2)}) collective-permute-start(bf16[2,32,2304]{2,1,0:T(8,128)(2,1)S(1)} %slice.121), channel_id=1, source_target_pairs={{0,2},{1,3},{2,0},{3,1},{4,6},{5,7},{6,4},{7,5},{8,10},{9,11},{10,... | collective-permute-start | bytes 884744 | tf_op jit(solution)/shard_map/ppermute | solution.py:376
  62.3 10.2 %collective-permute-start.10 = (bf16[2,32,2560]{2,1,0:T(8,128)(2,1)S(1)}, bf16[2,32,2560]{2,1,0:T(8,128)(2,1)S(1)}, u32[]{:S(2)}, u32[]{:S(2)}) collective-permute-start(bf16[2,32,2560]{2,1,0:T(8,128)(2,1)S(1)} %slice.122), channel_id=1, source_target_pairs={{0,4},{1,5},{2,6},{3,7},{4,0},{5,1},{6,2},{7,3},{8,12},{9,13},{10,... | collective-permute-start | bytes 983048 | tf_op jit(solution)/shard_map/ppermute | solution.py:376
  66.5 9.0 %collective-permute-start.13 = (bf16[2,64,1280]{2,1,0:T(8,128)(2,1)S(1)}, bf16[2,64,1280]{2,1,0:T(8,128)(2,1)S(1)}, u32[]{:S(2)}, u32[]{:S(2)}) collective-permute-start(bf16[2,64,1280]{2,1,0:T(8,128)(2,1)S(1)} %pad_maximum_fusion.18), channel_id=1, source_target_pairs={{0,2},{1,3},{2,0},{3,1},{4,6},{5,7},{6,4},{7,5},{8,10},{9,11},{10,... | collective-permute-start | bytes 983048 | tf_op jit(solution)/shard_map/ppermute | solution.py:376
  71.3 10.7 %collective-permute-start.9 = (bf16[2,64,2304]{2,1,0:T(8,128)(2,1)S(1)}, bf16[2,64,2304]{2,1,0:T(8,128)(2,1)S(1)}, u32[]{:S(2)}, u32[]{:S(2)}) collective-permute-start(bf16[2,64,2304]{2,1,0:T(8,128)(2,1)S(1)} %pad_maximum_fusion.11), channel_id=1, source_target_pairs={{0,4},{1,5},{2,6},{3,7},{4,0},{5,1},{6,2},{7,3},{8,12},{9,13},{10,... | collective-permute-start | bytes 1769480 | tf_op jit(solution)/shard_map/ppermute | solution.py:376
  72.5 10.8 %collective-permute-start.11 = (bf16[2,64,2560]{2,1,0:T(8,128)(2,1)S(1)}, bf16[2,64,2560]{2,1,0:T(8,128)(2,1)S(1)}, u32[]{:S(2)}, u32[]{:S(2)}) collective-permute-start(bf16[2,64,2560]{2,1,0:T(8,128)(2,1)S(1)} %pad_maximum_fusion.8), channel_id=1, source_target_pairs={{0,1},{1,0},{2,3},{3,2},{4,5},{5,4},{6,7},{7,6},{8,9},{9,8},{10,11... | collective-permute-start | bytes 1966088 | tf_op jit(solution)/shard_map/ppermute | solution.py:376
  83.2 6.5 %copy-start.1 = (s32[48,12]{0,1:T(8,128)S(1)}, s32[48,12]{0,1:T(8,128)}, u32[]{:S(2)}) copy-start(s32[48,12]{0,1:T(8,128)} %param.10) | copy-start | bytes 6916
  83.2 33.3 %copy-start = (s32[12,48]{1,0:T(8,128)S(1)}, s32[12,48]{1,0:T(8,128)}, u32[]{:S(2)}) copy-start(s32[12,48]{1,0:T(8,128)} %pattern.5) | copy-start | bytes 6916
  84.4 32.0 %collective-permute-start.15 = (bf16[2,128,2560]{2,1,0:T(8,128)(2,1)}, bf16[2,128,2560]{2,1,0:T(8,128)(2,1)}, u32[]{:S(2)}, u32[]{:S(2)}) collective-permute-start(bf16[2,128,2560]{2,1,0:T(8,128)(2,1)} %pad_maximum_fusion.refs_2_), channel_id=1, source_target_pairs={{0,2},{1,3},{2,0},{3,1},{4,6},{5,7},{6,4},{7,5},{8,10},{9,11},{10,... | collective-permute-start | bytes 3932168 | tf_op jit(solution)/shard_map/ppermute | solution.py:376
  86.0 29.0 %collective-permute-start.14 = (bf16[2,128,2304]{2,1,0:T(8,128)(2,1)S(1)}, bf16[2,128,2304]{2,1,0:T(8,128)(2,1)}, u32[]{:S(2)}, u32[]{:S(2)}) collective-permute-start(bf16[2,128,2304]{2,1,0:T(8,128)(2,1)S(1)} %pad_maximum_fusion.2.refs_0_), channel_id=1, source_target_pairs={{0,1},{1,0},{2,3},{3,2},{4,5},{5,4},{6,7},{7,6},{8,9},{9,8},{10,11... | collective-permute-start | bytes 3538952 | tf_op jit(solution)/shard_map/ppermute | solution.py:376
  87.7 11.0 %collective-permute-start.16 = (bf16[2,128,1280]{2,1,0:T(8,128)(2,1)S(1)}, bf16[2,128,1280]{2,1,0:T(8,128)(2,1)S(1)}, u32[]{:S(2)}, u32[]{:S(2)}) collective-permute-start(bf16[2,128,1280]{2,1,0:T(8,128)(2,1)S(1)} %pad_maximum_fusion.7.refs_4_), channel_id=1, source_target_pairs={{0,4},{1,5},{2,6},{3,7},{4,0},{5,1},{6,2},{7,3},{8,12},{9,13},{10,... | collective-permute-start | bytes 1966088 | tf_op jit(solution)/shard_map/ppermute | solution.py:376
  88.8 49.9 %collective-permute-start.19 = (bf16[2,128,2560]{2,1,0:T(8,128)(2,1)}, bf16[2,128,2560]{2,1,0:T(8,128)(2,1)}, u32[]{:S(2)}, u32[]{:S(2)}) collective-permute-start(bf16[2,128,2560]{2,1,0:T(8,128)(2,1)} %pad_maximum_fusion.1.refs_9_.refs_2_), channel_id=1, source_target_pairs={{0,2},{1,3},{2,0},{3,1},{4,6},{5,7},{6,4},{7,5},{8,10},{9,11},{10,... | collective-permute-start | bytes 3932168 | tf_op jit(solution)/shard_map/ppermute | solution.py:376
  89.1 48.8 %collective-permute-start.18 = (bf16[2,128,2304]{2,1,0:T(8,128)(2,1)}, bf16[2,128,2304]{2,1,0:T(8,128)(2,1)}, u32[]{:S(2)}, u32[]{:S(2)}) collective-permute-start(bf16[2,128,2304]{2,1,0:T(8,128)(2,1)} %pad_maximum_fusion.3.refs_8_.refs_0_), channel_id=1, source_target_pairs={{0,1},{1,0},{2,3},{3,2},{4,5},{5,4},{6,7},{7,6},{8,9},{9,8},{10,11... | collective-permute-start | bytes 3538952 | tf_op jit(solution)/shard_map/ppermute | solution.py:376
  136.2 2.5 collective-permute-start.20
  136.3 3.4 %collective-permute-start.17 = (bf16[256,1536]{1,0:T(8,128)(2,1)S(1)}, bf16[256,1536]{1,0:T(8,128)(2,1)S(1)}, u32[]{:S(2)}, u32[]{:S(2)}) collective-permute-start(bf16[256,1536]{1,0:T(8,128)(2,1)S(1)} %get-tuple-element.53), channel_id=1, source_target_pairs={{0,16},{16,0},{1,17},{17,1},{2,18},{18,2},{3,19},{19,3},{4,20},{20... | collective-permute-start | bytes 2359304 | tf_op jit(solution)/shard_map/ppermute | solution.py:384
  136.8 20.1 %collective-permute-start.22 = (bf16[2,128,1280]{2,1,0:T(8,128)(2,1)S(1)}, bf16[2,128,1280]{2,1,0:T(8,128)(2,1)S(1)}, u32[]{:S(2)}, u32[]{:S(2)}) collective-permute-start(bf16[2,128,1280]{2,1,0:T(8,128)(2,1)S(1)} %pad_maximum_fusion.9.refs_10_.refs_4_), channel_id=1, source_target_pairs={{0,4},{1,5},{2,6},{3,7},{4,0},{5,1},{6,2},{7,3},{8,12},{9,13},{10,... | collective-permute-start | bytes 1966088 | tf_op jit(solution)/shard_map/ppermute | solution.py:376
  152.4 24.6 %collective-permute-start.29 = (bf16[128,1280]{1,0:T(8,128)(2,1)S(1)}, bf16[128,1280]{1,0:T(8,128)(2,1)S(1)}, u32[]{:S(2)}, u32[]{:S(2)}) collective-permute-start(bf16[128,1280]{1,0:T(8,128)(2,1)S(1)} %get-tuple-element.62.refs_13_), channel_id=1, source_target_pairs={{0,4},{1,5},{2,6},{3,7},{4,0},{5,1},{6,2},{7,3},{8,12},{9,13},{10,... | collective-permute-start | bytes 983048 | tf_op jit(solution)/shard_map/ppermute | solution.py:376
  153.7 23.8 %collective-permute-start.21 = (bf16[128,2304]{1,0:T(8,128)(2,1)S(1)}, bf16[128,2304]{1,0:T(8,128)(2,1)S(1)}, u32[]{:S(2)}, u32[]{:S(2)}) collective-permute-start(bf16[128,2304]{1,0:T(8,128)(2,1)S(1)} %get-tuple-element.58.refs_9_), channel_id=1, source_target_pairs={{0,1},{1,0},{2,3},{3,2},{4,5},{5,4},{6,7},{7,6},{8,9},{9,8},{10,11... | collective-permute-start | bytes 1769480 | tf_op jit(solution)/shard_map/ppermute | solution.py:376
  155.2 24.2 %collective-permute-start.27 = (bf16[128,2560]{1,0:T(8,128)(2,1)S(1)}, bf16[128,2560]{1,0:T(8,128)(2,1)S(1)}, u32[]{:S(2)}, u32[]{:S(2)}) collective-permute-start(bf16[128,2560]{1,0:T(8,128)(2,1)S(1)} %get-tuple-element.60.refs_11_), channel_id=1, source_target_pairs={{0,2},{1,3},{2,0},{3,1},{4,6},{5,7},{6,4},{7,5},{8,10},{9,11},{10,... | collective-permute-start | bytes 1966088 | tf_op jit(solution)/shard_map/ppermute | solution.py:376
  176.4 3.3 %collective-permute-start.25 = (bf16[256,1536]{1,0:T(8,128)(2,1)S(1)}, bf16[256,1536]{1,0:T(8,128)(2,1)S(1)}, u32[]{:S(2)}, u32[]{:S(2)}) collective-permute-start(bf16[256,1536]{1,0:T(8,128)(2,1)S(1)} %get-tuple-element.65), channel_id=1, source_target_pairs={{0,16},{16,0},{1,17},{17,1},{2,18},{18,2},{3,19},{19,3},{4,20},{20... | collective-permute-start | bytes 2359304 | tf_op jit(solution)/shard_map/ppermute | solution.py:384
  176.5 3.4 %collective-permute-start.24 = (bf16[256,1536]{1,0:T(8,128)(2,1)S(1)}, bf16[256,1536]{1,0:T(8,128)(2,1)S(1)}, u32[]{:S(2)}, u32[]{:S(2)}) collective-permute-start(bf16[256,1536]{1,0:T(8,128)(2,1)S(1)} %get-tuple-element.63), channel_id=1, source_target_pairs={{0,16},{16,0},{1,17},{17,1},{2,18},{18,2},{3,19},{19,3},{4,20},{20... | collective-permute-start | bytes 2359304 | tf_op jit(solution)/shard_map/ppermute | solution.py:384
  177.1 6.2 %collective-permute-start.30 = (bf16[64,1280]{1,0:T(8,128)(2,1)S(1)}, bf16[64,1280]{1,0:T(8,128)(2,1)S(1)}, u32[]{:S(2)}, u32[]{:S(2)}) collective-permute-start(bf16[64,1280]{1,0:T(8,128)(2,1)S(1)} %slice.161), channel_id=1, source_target_pairs={{0,2},{1,3},{2,0},{3,1},{4,6},{5,7},{6,4},{7,5},{8,10},{9,11},{10,... | collective-permute-start | bytes 491528 | tf_op jit(solution)/shard_map/ppermute | solution.py:376
  177.7 8.8 %collective-permute-start.23 = (bf16[64,2304]{1,0:T(8,128)(2,1)S(1)}, bf16[64,2304]{1,0:T(8,128)(2,1)S(1)}, u32[]{:S(2)}, u32[]{:S(2)}) collective-permute-start(bf16[64,2304]{1,0:T(8,128)(2,1)S(1)} %slice.155), channel_id=1, source_target_pairs={{0,4},{1,5},{2,6},{3,7},{4,0},{5,1},{6,2},{7,3},{8,12},{9,13},{10,... | collective-permute-start | bytes 884744 | tf_op jit(solution)/shard_map/ppermute | solution.py:376
  179.6 10.1 %collective-permute-start.28 = (bf16[64,2560]{1,0:T(8,128)(2,1)S(1)}, bf16[64,2560]{1,0:T(8,128)(2,1)S(1)}, u32[]{:S(2)}, u32[]{:S(2)}) collective-permute-start(bf16[64,2560]{1,0:T(8,128)(2,1)S(1)} %slice.159), channel_id=1, source_target_pairs={{0,1},{1,0},{2,3},{3,2},{4,5},{5,4},{6,7},{7,6},{8,9},{9,8},{10,11... | collective-permute-start | bytes 983048 | tf_op jit(solution)/shard_map/ppermute | solution.py:376
  183.4 30.0 %collective-permute-start.32 = (bf16[32,1280]{1,0:T(8,128)(2,1)S(1)}, bf16[32,1280]{1,0:T(8,128)(2,1)S(1)}, u32[]{:S(2)}, u32[]{:S(2)}) collective-permute-start(bf16[32,1280]{1,0:T(8,128)(2,1)S(1)} %slice.165), channel_id=1, source_target_pairs={{0,1},{1,0},{2,3},{3,2},{4,5},{5,4},{6,7},{7,6},{8,9},{9,8},{10,11... | collective-permute-start | bytes 245768 | tf_op jit(solution)/shard_map/ppermute | solution.py:376
  186.5 37.3 %collective-permute-start.26 = (bf16[32,2304]{1,0:T(8,128)(2,1)S(1)}, bf16[32,2304]{1,0:T(8,128)(2,1)S(1)}, u32[]{:S(2)}, u32[]{:S(2)}) collective-permute-start(bf16[32,2304]{1,0:T(8,128)(2,1)S(1)} %slice.157), channel_id=1, source_target_pairs={{0,2},{1,3},{2,0},{3,1},{4,6},{5,7},{6,4},{7,5},{8,10},{9,11},{10,... | collective-permute-start | bytes 442376 | tf_op jit(solution)/shard_map/ppermute | solution.py:376
  201.5 22.6 %collective-permute-start.34 = (bf16[128,2304]{1,0:T(8,128)(2,1)S(1)}, bf16[128,2304]{1,0:T(8,128)(2,1)S(1)}, u32[]{:S(2)}, u32[]{:S(2)}) collective-permute-start(bf16[128,2304]{1,0:T(8,128)(2,1)S(1)} %get-tuple-element.74.refs_5_), channel_id=1, source_target_pairs={{0,1},{1,0},{2,3},{3,2},{4,5},{5,4},{6,7},{7,6},{8,9},{9,8},{10,11... | collective-permute-start | bytes 1769480 | tf_op jit(solution)/shard_map/ppermute | solution.py:376
  201.8 22.4 %collective-permute-start.35 = (bf16[128,2560]{1,0:T(8,128)(2,1)S(1)}, bf16[128,2560]{1,0:T(8,128)(2,1)S(1)}, u32[]{:S(2)}, u32[]{:S(2)}) collective-permute-start(bf16[128,2560]{1,0:T(8,128)(2,1)S(1)} %get-tuple-element.76.refs_7_), channel_id=1, source_target_pairs={{0,2},{1,3},{2,0},{3,1},{4,6},{5,7},{6,4},{7,5},{8,10},{9,11},{10,... | collective-permute-start | bytes 1966088 | tf_op jit(solution)/shard_map/ppermute | solution.py:376
  202.8 21.2 %collective-permute-start.36 = (bf16[128,1280]{1,0:T(8,128)(2,1)S(1)}, bf16[128,1280]{1,0:T(8,128)(2,1)S(1)}, u32[]{:S(2)}, u32[]{:S(2)}) collective-permute-start(bf16[128,1280]{1,0:T(8,128)(2,1)S(1)} %get-tuple-element.78.refs_9_), channel_id=1, source_target_pairs={{0,4},{1,5},{2,6},{3,7},{4,0},{5,1},{6,2},{7,3},{8,12},{9,13},{10,... | collective-permute-start | bytes 983048 | tf_op jit(solution)/shard_map/ppermute | solution.py:376
  213.5 10.4 %collective-permute-start.31 = (bf16[32,2560]{1,0:T(8,128)(2,1)S(1)}, bf16[32,2560]{1,0:T(8,128)(2,1)S(1)}, u32[]{:S(2)}, u32[]{:S(2)}) collective-permute-start(bf16[32,2560]{1,0:T(8,128)(2,1)S(1)} %slice.163), channel_id=1, source_target_pairs={{0,4},{1,5},{2,6},{3,7},{4,0},{5,1},{6,2},{7,3},{8,12},{9,13},{10,... | collective-permute-start | bytes 491528 | tf_op jit(solution)/shard_map/ppermute | solution.py:376
  224.5 15.0 %collective-permute-start.39 = (bf16[64,1280]{1,0:T(8,128)(2,1)S(1)}, bf16[64,1280]{1,0:T(8,128)(2,1)S(1)}, u32[]{:S(2)}, u32[]{:S(2)}) collective-permute-start(bf16[64,1280]{1,0:T(8,128)(2,1)S(1)} %slice.143), channel_id=1, source_target_pairs={{0,2},{1,3},{2,0},{3,1},{4,6},{5,7},{6,4},{7,5},{8,10},{9,11},{10,... | collective-permute-start | bytes 491528 | tf_op jit(solution)/shard_map/ppermute | solution.py:376
  225.7 14.4 %collective-permute-start.33 = (bf16[16,6144]{1,0:T(8,128)(2,1)S(1)}, bf16[16,6144]{1,0:T(8,128)(2,1)S(1)}, u32[]{:S(2)}, u32[]{:S(2)}) collective-permute-start(bf16[16,6144]{1,0:T(8,128)(2,1)S(1)} %slice.167), channel_id=1, source_target_pairs={{0,8},{1,9},{2,10},{3,11},{4,12},{5,13},{6,14},{7,15},{8,0},{9,1},... | collective-permute-start | bytes 589832 | tf_op jit(solution)/shard_map/ppermute | solution.py:376
  227.7 11.8 %collective-permute-start.37 = (bf16[64,2304]{1,0:T(8,128)(2,1)S(1)}, bf16[64,2304]{1,0:T(8,128)(2,1)S(1)}, u32[]{:S(2)}, u32[]{:S(2)}) collective-permute-start(bf16[64,2304]{1,0:T(8,128)(2,1)S(1)} %slice.139), channel_id=1, source_target_pairs={{0,4},{1,5},{2,6},{3,7},{4,0},{5,1},{6,2},{7,3},{8,12},{9,13},{10,... | collective-permute-start | bytes 884744 | tf_op jit(solution)/shard_map/ppermute | solution.py:376
  228.1 11.4 %collective-permute-start.38 = (bf16[64,2560]{1,0:T(8,128)(2,1)S(1)}, bf16[64,2560]{1,0:T(8,128)(2,1)S(1)}, u32[]{:S(2)}, u32[]{:S(2)}) collective-permute-start(bf16[64,2560]{1,0:T(8,128)(2,1)S(1)} %slice.141), channel_id=1, source_target_pairs={{0,1},{1,0},{2,3},{3,2},{4,5},{5,4},{6,7},{7,6},{8,9},{9,8},{10,11... | collective-permute-start | bytes 983048 | tf_op jit(solution)/shard_map/ppermute | solution.py:376
  239.7 4.5 %collective-permute-start.42 = (bf16[32,1280]{1,0:T(8,128)(2,1)S(1)}, bf16[32,1280]{1,0:T(8,128)(2,1)S(1)}, u32[]{:S(2)}, u32[]{:S(2)}) collective-permute-start(bf16[32,1280]{1,0:T(8,128)(2,1)S(1)} %slice.149), channel_id=1, source_target_pairs={{0,1},{1,0},{2,3},{3,2},{4,5},{5,4},{6,7},{7,6},{8,9},{9,8},{10,11... | collective-permute-start | bytes 245768 | tf_op jit(solution)/shard_map/ppermute | solution.py:376
  240.1 7.1 %collective-permute-start.41 = (bf16[32,2560]{1,0:T(8,128)(2,1)S(1)}, bf16[32,2560]{1,0:T(8,128)(2,1)S(1)}, u32[]{:S(2)}, u32[]{:S(2)}) collective-permute-start(bf16[32,2560]{1,0:T(8,128)(2,1)S(1)} %slice.147), channel_id=1, source_target_pairs={{0,4},{1,5},{2,6},{3,7},{4,0},{5,1},{6,2},{7,3},{8,12},{9,13},{10,... | collective-permute-start | bytes 491528 | tf_op jit(solution)/shard_map/ppermute | solution.py:376
  241.9 5.2 %collective-permute-start.40 = (bf16[32,2304]{1,0:T(8,128)(2,1)S(1)}, bf16[32,2304]{1,0:T(8,128)(2,1)S(1)}, u32[]{:S(2)}, u32[]{:S(2)}) collective-permute-start(bf16[32,2304]{1,0:T(8,128)(2,1)S(1)} %slice.145), channel_id=1, source_target_pairs={{0,2},{1,3},{2,0},{3,1},{4,6},{5,7},{6,4},{7,5},{8,10},{9,11},{10,... | collective-permute-start | bytes 442376 | tf_op jit(solution)/shard_map/ppermute | solution.py:376
  247.2 10.3 %collective-permute-start.43 = (bf16[16,6144]{1,0:T(8,128)(2,1)S(1)}, bf16[16,6144]{1,0:T(8,128)(2,1)S(1)}, u32[]{:S(2)}, u32[]{:S(2)}) collective-permute-start(bf16[16,6144]{1,0:T(8,128)(2,1)S(1)} %slice.169), channel_id=1, source_target_pairs={{0,8},{1,9},{2,10},{3,11},{4,12},{5,13},{6,14},{7,15},{8,0},{9,1},... | collective-permute-start | bytes 589832 | tf_op jit(solution)/shard_map/ppermute | solution.py:376
